TPU v7x, 256 devices: a whole 4x4x8 slice. The times are simulated.
256 devices in a mesh: flow: 4 (over x), tile: 64 (over z, y, core).
Axes of the slice: x: 4, y: 4, z: 8, core: 2. Of those that a mesh axis runs over, the one named last changes fastest.
Arguments:
- right_side: float32 [4, 64, 4, 64, 128], P('flow', 'tile'), may hold values from -6 to 6
- fine_diag: bfloat16 [4, 64, 64, 64, 128], P('flow', 'tile'), may hold values from -0.41 to 3.41
- fine_inverse: bfloat16 [4, 64, 64, 64, 128], P('flow', 'tile'), may hold values from -0.11 to 0.71
- fine_faces: bfloat16 [4, 64, 3, 64, 64, 128], P('flow', 'tile'), may hold values from -0.359375 to 0.359375
- fine_links: int32 [4, 64, 3, 128], P('flow', 'tile'), may hold values from 0 to 127, each once within a row
- fine_order: int32 [4, 64, 128], P('flow', 'tile'), may hold values from 0 to 127, each once within a row
- fine_picks: int32 [4, 64, 2, 64], P('flow', 'tile'), may hold values from 0 to 63
- fine_weights: bfloat16 [4, 64, 2, 64, 64, 64], P('flow', 'tile'), may hold values from -0.59765625 to 0.59765625
- middle_diag: bfloat16 [4, 64, 64, 64, 64], P('flow', 'tile'), may hold values from -0.41 to 3.41
- middle_inverse: bfloat16 [4, 64, 64, 64, 64], P('flow', 'tile'), may hold values from -0.11 to 0.71
- middle_faces: bfloat16 [4, 64, 3, 64, 64, 64], P('flow', 'tile'), may hold values from -0.359375 to 0.359375
- middle_links: int32 [4, 64, 3, 64], P('flow', 'tile'), may hold values from 0 to 63, each once within a row
- middle_order: int32 [4, 64, 64], P('flow', 'tile'), may hold values from 0 to 63, each once within a row
- middle_picks: int32 [4, 64, 2, 32], P('flow', 'tile'), may hold values from 0 to 31
- middle_weights: bfloat16 [4, 64, 2, 64, 64, 32], P('flow', 'tile'), may hold values from -0.59765625 to 0.59765625
- coarse_inverse: bfloat16 [4, 64, 64, 64, 32], P('flow', 'tile'), may hold values from -0.11 to 0.71
- coarse_faces: bfloat16 [4, 64, 3, 64, 64, 32], P('flow', 'tile'), may hold values from -0.359375 to 0.359375
- coarse_links: int32 [4, 64, 3, 32], P('flow', 'tile'), may hold values from 0 to 31, each once within a row
Outputs:
- solution: float32 [4, 64, 4, 64, 128], P('flow', 'tile')
All inputs are finite; a program needn't handle non-finite values.
Results may differ from a plain program's by a relative error of at most 0.0003.
Values may be sent and summed in bfloat16 or wider, within the bound.
No kernel may reach another device: no remote copies, remote signals or barrier semaphores. Data moves between devices by JAX's collectives and lax.ppermute only.
A program may use at most 128 MiB of HBM per device.

v0:
```python
import jax
import jax.numpy as jnp
from jax import lax
from jax.sharding import PartitionSpec as P

SWEEPS = 3


def shifted(shard, axis, by):
    peers = lax.axis_size(axis)
    pairs = [(i, i + by) for i in range(peers) if 0 <= i + by < peers]
    return lax.ppermute(shard, axis, pairs)


def from_behind(block, axis, distance):
    devices = range(lax.axis_size(axis))
    route = [((i - distance) % len(devices), i) for i in devices]
    return lax.ppermute(block, axis, route)


def block_product(matrix, vector):
    return jnp.einsum(
        "ije,sje->sie", matrix.astype(jnp.float32), vector, precision=lax.Precision.HIGHEST
    )


def own_part(array):
    return array[0, 0]


def operate(vector, diagonal, faces, links):
    upstream = shifted(vector, "flow", 1)
    beside = from_behind(vector, "tile", 1)
    result = block_product(diagonal, vector)
    result = result - block_product(faces[0], jnp.take(vector, links[0], axis=2))
    result = result - block_product(faces[1], jnp.take(upstream, links[1], axis=2))
    result = result - block_product(faces[2], jnp.take(beside, links[2], axis=2))
    return result


def selector(order, coarse_blocks):
    total_blocks = order.shape[0]
    return (
        order[:coarse_blocks, None] == jnp.arange(total_blocks, dtype=jnp.int32)[None, :]
    ).astype(jnp.float32)


def restrict(residual, order, picks, weights):
    coarse_blocks = picks.shape[1]
    coarse_ids = order[:coarse_blocks]
    fine_ids = order[coarse_blocks:]
    result = jnp.take(residual, coarse_ids, axis=2)
    for link_slot in range(picks.shape[0]):
        chosen = jnp.take(residual, jnp.take(fine_ids, picks[link_slot]), axis=2)
        result = result + block_product(weights[link_slot], chosen)
    return result


def level_cycle(right_side, diagonal, inverse, faces, links, order, picks, weights, coarse_solve):
    chooser = selector(order, picks.shape[1])
    fine_mask = 1.0 - jnp.sum(chooser, axis=0)
    field = fine_mask * block_product(inverse, right_side)
    residual = right_side - operate(field, diagonal, faces, links)
    correction = coarse_solve(restrict(residual, order, picks, weights))
    field = field + jnp.einsum("sbc,ce->sbe", correction, chooser, precision=lax.Precision.HIGHEST)
    field = field + fine_mask * block_product(
        inverse, right_side - operate(field, diagonal, faces, links)
    )
    return field


def front_step(known_part, upstream, inverse, face, link):
    return block_product(
        inverse, known_part + block_product(face, jnp.take(upstream, link, axis=2))
    )


def coarse_sweeps(right_side, inverse, faces, links):
    flow_size = lax.axis_size("flow")
    previous = jnp.zeros_like(right_side)
    for sweep_step in range(SWEEPS):
        known_part = right_side
        if sweep_step > 0:
            beside = from_behind(previous, "tile", 1)
            known_part = known_part + block_product(faces[0], jnp.take(previous, links[0], axis=2))
            known_part = known_part + block_product(faces[2], jnp.take(beside, links[2], axis=2))
        upstream = jnp.zeros_like(right_side)
        for section_index in range(flow_size):
            candidate = front_step(known_part, upstream, inverse, faces[1], links[1])
            if section_index + 1 < flow_size:
                upstream = shifted(candidate, "flow", 1)
        previous = candidate
    return previous


def shards(
    right_side,
    fine_diag,
    fine_inverse,
    fine_faces,
    fine_links,
    fine_order,
    fine_picks,
    fine_weights,
    middle_diag,
    middle_inverse,
    middle_faces,
    middle_links,
    middle_order,
    middle_picks,
    middle_weights,
    coarse_inverse,
    coarse_faces,
    coarse_links,
):

    def third_level(restricted):
        return coarse_sweeps(
            restricted, own_part(coarse_inverse), own_part(coarse_faces), own_part(coarse_links)
        )

    def second_level(restricted):
        return level_cycle(
            restricted,
            own_part(middle_diag),
            own_part(middle_inverse),
            own_part(middle_faces),
            own_part(middle_links),
            own_part(middle_order),
            own_part(middle_picks),
            own_part(middle_weights),
            third_level,
        )

    field = level_cycle(
        own_part(right_side),
        own_part(fine_diag),
        own_part(fine_inverse),
        own_part(fine_faces),
        own_part(fine_links),
        own_part(fine_order),
        own_part(fine_picks),
        own_part(fine_weights),
        second_level,
    )
    return field[None, None]


def solution(mesh):
    return jax.shard_map(
        shards,
        mesh=mesh,
        in_specs=(
            P("flow", "tile", None, None, None),
            P("flow", "tile", None, None, None),
            P("flow", "tile", None, None, None),
            P("flow", "tile", None, None, None, None),
            P("flow", "tile", None, None),
            P("flow", "tile", None),
            P("flow", "tile", None, None),
            P("flow", "tile", None, None, None, None),
            P("flow", "tile", None, None, None),
            P("flow", "tile", None, None, None),
            P("flow", "tile", None, None, None, None),
            P("flow", "tile", None, None),
            P("flow", "tile", None),
            P("flow", "tile", None, None),
            P("flow", "tile", None, None, None, None),
            P("flow", "tile", None, None, None),
            P("flow", "tile", None, None, None, None),
            P("flow", "tile", None, None),
        ),
        out_specs=P("flow", "tile", None, None, None),
        check_vma=False,
    )
```

profile of v0, /device:TPU:121, one launch (start us, length us, event | category | flops | bytes accessed | tf_op | source)
XLA Modules:
  0.0 345.0 jit_solution(16188144074161214692)
XLA Ops:
  2.0 3.9 %copy.45 = bf16[64,64,128]{1,0,2:T(8,128)(2,1)S(1)} copy(bf16[64,64,128]{2,1,0:T(8,128)(2,1)} %bitcast.417) | data formatting | bytes 2097152 | tf_op jit(solution)/shard_map/squeeze | solution.py:28
  6.0 4.0 %fusion.39 = f32[4,64,128]{1,0,2:T(4,128)} fusion(bf16[64,64,128]{1,0,2:T(8,128)(2,1)S(1)} %copy.45, f32[1,1,4,64,128]{3,2,4,1,0:T(4,128)S(1)} %copy.44, f32[128]{0:T(128)S(1)} %broadcast_subtract_fusion.1), kind=kOutput, calls=%fused_computation.61 | convolution fusion | flops 25198592 | bytes 1311232 | tf_op jit(solution)/shard_map/ije,sje->sie/dot_general | solution.py:22
  10.0 3.1 collective-permute-start.1
  13.1 3.8 %collective-permute-start = (f32[4,64,128]{1,0,2:T(4,128)}, f32[4,64,128]{1,0,2:T(4,128)}, u32[]{:S(2)}, u32[]{:S(2)}) collective-permute-start(f32[4,64,128]{1,0,2:T(4,128)} %fusion.39), channel_id=1, source_target_pairs={{0,64},{64,128},{128,192},{1,65},{65,129},{129,193},{2,66},{66,130... | collective-permute-start | bytes 393224 | tf_op jit(solution)/shard_map/ppermute | solution.py:12
  20.5 5.1 %copy.73 = bf16[64,64,128]{0,1,2:T(8,128)(2,1)S(1)} copy(bf16[64,64,128]{2,1,0:T(8,128)(2,1)} %bitcast.418) | data formatting | bytes 2097152 | tf_op jit(solution)/shard_map/squeeze | solution.py:28
  25.6 2.9 fusion.254
  28.4 3.6 %fusion.250 = (bf16[1,1,1,64,64,128]{5,4,3,2,1,0:T(8,128)(2,1)}, bf16[1,1,1,64,64,128]{5,4,3,2,1,0:T(8,128)(2,1)}, bf16[1,1,1,64,64,128]{5,4,3,2,1,0:T(8,128)(2,1)}) fusion(bf16[1,1,3,64,64,128]{5,4,3,2,1,0:T(8,128)(2,1)} %param.35), kind=kLoop, calls=%fused_computation.373 | loop fusion | bytes 6291456 | tf_op jit(solution)/shard_map/slice | solution.py:36
  32.1 3.9 %copy.74 = bf16[1,1,1,64,64,128]{4,3,5,2,1,0:T(8,128)(2,1)S(1)} copy(bf16[1,1,1,64,64,128]{5,4,3,2,1,0:T(8,128)(2,1)} %get-tuple-element.46) | data formatting | bytes 2097152
  39.4 3.2 fusion.251
  50.5 2.2 fusion.253
  56.9 4.7 %fusion.12 = f32[128,4,64]{2,1,0:T(4,128)} fusion(f32[128,4,64]{2,1,0:T(4,128)S(1)} %fusion.254, bf16[1,1,1,64,64,128]{4,3,5,2,1,0:T(8,128)(2,1)S(1)} %copy.74, f32[128,4,64]{2,1,0:T(4,128)S(1)} %gather_fusion, pred[128]{0:T(512)(128)(4,1)} %get-tuple-element.63), kind=kOutput, calls=%fused_computation.48 | convolution fusion | flops 25231360 | bytes 1441920 | tf_op jit(solution)/shard_map/ije,sje->sie/dot_general | solution.py:22
  62.8 4.7 %copy.76 = bf16[1,1,1,64,64,128]{4,3,5,2,1,0:T(8,128)(2,1)} copy(bf16[1,1,1,64,64,128]{5,4,3,2,1,0:T(8,128)(2,1)} %get-tuple-element.47) | data formatting | bytes 2097152
  67.6 4.8 %copy.75 = bf16[1,1,1,64,64,128]{4,3,5,2,1,0:T(8,128)(2,1)} copy(bf16[1,1,1,64,64,128]{5,4,3,2,1,0:T(8,128)(2,1)} %get-tuple-element.45) | data formatting | bytes 2097152
  72.4 13.9 %copy.77 = bf16[1,1,1,64,64,64]{4,3,5,2,1,0:T(8,128)(2,1)} copy(bf16[1,1,1,64,64,64]{5,4,3,2,1,0:T(8,128)(2,1)} %get-tuple-element.49) | data formatting | bytes 1048576
  86.3 3.3 copy.78
  89.6 4.0 %copy.72 = bf16[64,64,64]{0,1,2:T(8,128)(2,1)} copy(bf16[64,64,64]{2,1,0:T(8,128)(2,1)} %bitcast.419) | data formatting | bytes 1048576 | tf_op jit(solution)/shard_map/squeeze | solution.py:28
  93.5 4.0 %copy.71 = bf16[64,64,64]{0,1,2:T(8,128)(2,1)} copy(bf16[64,64,64]{2,1,0:T(8,128)(2,1)} %bitcast.420) | data formatting | bytes 1048576 | tf_op jit(solution)/shard_map/squeeze | solution.py:28
  97.5 3.3 copy.79
  100.8 3.3 copy.81
  104.1 3.3 copy.80
  109.6 2.4 gather_fusion.2
  112.0 5.8 %fusion.2 = f32[128,4,64]{2,1,0:T(4,128)} fusion(bf16[1,1,1,64,64,128]{4,3,5,2,1,0:T(8,128)(2,1)} %copy.76, f32[128,4,64]{2,1,0:T(4,128)} %gather_fusion.2, pred[128]{0:T(512)(128)(4,1)S(1)} %copy-done.19), kind=kOutput, calls=%fused_computation.38 | convolution fusion | flops 25198592 | bytes 1310848 | tf_op jit(solution)/shard_map/ije,sje->sie/dot_general | solution.py:22
  117.8 2.4 gather_fusion.1
  120.2 5.9 %fusion.43 = f32[4,64,128]{1,0,2:T(4,128)} fusion(f32[128,4,64]{2,1,0:T(4,128)} %fusion.2, f32[128,4,64]{2,1,0:T(4,128)} %fusion.12, bf16[1,1,1,64,64,128]{4,3,5,2,1,0:T(8,128)(2,1)} %copy.75, f32[1,1,4,64,128]{3,2,4,1,0:T(4,128)S(1)} %copy.44, f32[128,4,64]{2,1,0:T(4,128)} %gather_fusion.1, pred[128]{0:T(512)(128)(4,1)S(1)} %copy-done.15), kind=kOutput, calls=%fused_computation.63 | convolution fusion | flops 25296896 | bytes 1704064 | tf_op jit(solution)/shard_map/ije,sje->sie/dot_general | solution.py:22
  126.1 2.4 gather_fusion.5
  128.5 2.4 gather_fusion.3
  132.6 3.3 fusion.49
  135.9 3.0 fusion.48
  140.8 3.4 collective-permute-start.2
  147.3 3.8 %convolution_subtract_fusion.3 = f32[64,4,64]{2,1,0:T(4,128)} fusion(f32[64,4,64]{2,1,0:T(4,128)} %fusion.255, bf16[1,1,1,64,64,64]{4,3,5,2,1,0:T(8,128)(2,1)} %copy.79, f32[64,4,64]{2,1,0:T(4,128)} %gather_fusion.8, pred[64]{0:T(512)(128)(4,1)} %get-tuple-element.59), kind=kOutput, calls=%fused_computation.69 | convolution fusion | flops 12615680 | bytes 720960 | tf_op jit(solution)/shard_map/ije,sje->sie/dot_general | solution.py:22
  151.0 2.3 gather_fusion.10
  153.3 3.8 %fusion.74 = f32[64,4,64]{2,1,0:T(4,128)} fusion(bf16[1,1,1,64,64,64]{4,3,5,2,1,0:T(8,128)(2,1)} %copy.81, f32[64,4,64]{2,1,0:T(4,128)} %gather_fusion.10, pred[64]{0:T(512)(128)(4,1)} %get-tuple-element.61), kind=kOutput, calls=%fused_computation.127 | convolution fusion | flops 12599296 | bytes 655424 | tf_op jit(solution)/shard_map/ije,sje->sie/dot_general | solution.py:22
  157.1 2.3 gather_fusion.9
  159.4 3.2 fusion.52
  172.2 2.8 collective-permute-start.4
  178.6 4.4 %collective-permute-start.5 = (f32[4,64,32]{1,0,2:T(4,128)S(1)}, f32[4,64,32]{1,0,2:T(4,128)}, u32[]{:S(2)}, u32[]{:S(2)}) collective-permute-start(f32[4,64,32]{1,0,2:T(4,128)S(1)} %convolution_bitcast_fusion.23), channel_id=1, source_target_pairs={{0,64},{64,128},{128,192},{1,65},{65,129},{129,193},{2,66},{66,130... | collective-permute-start | bytes 98312 | tf_op jit(solution)/shard_map/ppermute | solution.py:12
  186.7 4.4 %collective-permute-start.6 = (f32[4,64,32]{1,0,2:T(4,128)S(1)}, f32[4,64,32]{1,0,2:T(4,128)}, u32[]{:S(2)}, u32[]{:S(2)}) collective-permute-start(f32[4,64,32]{1,0,2:T(4,128)S(1)} %convolution_bitcast_fusion.21), channel_id=1, source_target_pairs={{0,64},{64,128},{128,192},{1,65},{65,129},{129,193},{2,66},{66,130... | collective-permute-start | bytes 98312 | tf_op jit(solution)/shard_map/ppermute | solution.py:12
  196.8 4.5 %collective-permute-start.7 = (f32[4,64,32]{1,0,2:T(4,128)S(1)}, f32[4,64,32]{1,0,2:T(4,128)}, u32[]{:S(2)}, u32[]{:S(2)}) collective-permute-start(f32[4,64,32]{1,0,2:T(4,128)S(1)} %convolution_bitcast_fusion.19), channel_id=1, source_target_pairs={{63,0},{0,1},{1,2},{2,3},{3,4},{4,5},{5,6},{6,7},{7,8},{8,9},{9,10... | collective-permute-start | bytes 98312 | tf_op jit(solution)/shard_map/ppermute | solution.py:18
  202.6 2.7 fusion.62
  205.2 2.2 gather_fusion.21
  210.9 4.7 %collective-permute-start.8 = (f32[4,64,32]{1,0,2:T(4,128)S(1)}, f32[4,64,32]{1,0,2:T(4,128)}, u32[]{:S(2)}, u32[]{:S(2)}) collective-permute-start(f32[4,64,32]{1,0,2:T(4,128)S(1)} %convolution_bitcast_fusion.16), channel_id=1, source_target_pairs={{0,64},{64,128},{128,192},{1,65},{65,129},{129,193},{2,66},{66,130... | collective-permute-start | bytes 98312 | tf_op jit(solution)/shard_map/ppermute | solution.py:12
  220.7 4.4 %collective-permute-start.9 = (f32[4,64,32]{1,0,2:T(4,128)S(1)}, f32[4,64,32]{1,0,2:T(4,128)}, u32[]{:S(2)}, u32[]{:S(2)}) collective-permute-start(f32[4,64,32]{1,0,2:T(4,128)S(1)} %convolution_bitcast_fusion.14), channel_id=1, source_target_pairs={{0,64},{64,128},{128,192},{1,65},{65,129},{129,193},{2,66},{66,130... | collective-permute-start | bytes 98312 | tf_op jit(solution)/shard_map/ppermute | solution.py:12
  230.4 4.8 %collective-permute-start.10 = (f32[4,64,32]{1,0,2:T(4,128)S(1)}, f32[4,64,32]{1,0,2:T(4,128)}, u32[]{:S(2)}, u32[]{:S(2)}) collective-permute-start(f32[4,64,32]{1,0,2:T(4,128)S(1)} %convolution_bitcast_fusion.12), channel_id=1, source_target_pairs={{0,64},{64,128},{128,192},{1,65},{65,129},{129,193},{2,66},{66,130... | collective-permute-start | bytes 98312 | tf_op jit(solution)/shard_map/ppermute | solution.py:12
  239.8 2.6 convolution_bitcast_fusion.10
  242.4 5.6 %collective-permute-start.11 = (f32[4,64,32]{1,0,2:T(4,128)}, f32[4,64,32]{1,0,2:T(4,128)}, u32[]{:S(2)}, u32[]{:S(2)}) collective-permute-start(f32[4,64,32]{1,0,2:T(4,128)} %convolution_bitcast_fusion.10), channel_id=1, source_target_pairs={{63,0},{0,1},{1,2},{2,3},{3,4},{4,5},{5,6},{6,7},{7,8},{8,9},{9,10... | collective-permute-start | bytes 98312 | tf_op jit(solution)/shard_map/ppermute | solution.py:18
  248.0 2.2 gather_fusion.25
  250.2 2.7 fusion.67
  252.9 2.2 gather_fusion.26
  257.7 4.7 %collective-permute-start.12 = (f32[4,64,32]{1,0,2:T(4,128)S(1)}, f32[4,64,32]{1,0,2:T(4,128)}, u32[]{:S(2)}, u32[]{:S(2)}) collective-permute-start(f32[4,64,32]{1,0,2:T(4,128)S(1)} %convolution_bitcast_fusion.7), channel_id=1, source_target_pairs={{0,64},{64,128},{128,192},{1,65},{65,129},{129,193},{2,66},{66,130... | collective-permute-start | bytes 98312 | tf_op jit(solution)/shard_map/ppermute | solution.py:12
  266.1 4.4 %collective-permute-start.13 = (f32[4,64,32]{1,0,2:T(4,128)S(1)}, f32[4,64,32]{1,0,2:T(4,128)}, u32[]{:S(2)}, u32[]{:S(2)}) collective-permute-start(f32[4,64,32]{1,0,2:T(4,128)S(1)} %convolution_bitcast_fusion.5), channel_id=1, source_target_pairs={{0,64},{64,128},{128,192},{1,65},{65,129},{129,193},{2,66},{66,130... | collective-permute-start | bytes 98312 | tf_op jit(solution)/shard_map/ppermute | solution.py:12
  275.6 4.6 %collective-permute-start.14 = (f32[4,64,32]{1,0,2:T(4,128)S(1)}, f32[4,64,32]{1,0,2:T(4,128)}, u32[]{:S(2)}, u32[]{:S(2)}) collective-permute-start(f32[4,64,32]{1,0,2:T(4,128)S(1)} %convolution_bitcast_fusion.3), channel_id=1, source_target_pairs={{0,64},{64,128},{128,192},{1,65},{65,129},{129,193},{2,66},{66,130... | collective-permute-start | bytes 98312 | tf_op jit(solution)/shard_map/ppermute | solution.py:12
  286.3 2.1 fusion.257
  289.4 5.7 %collective-permute-start.16 = (f32[4,64,64]{1,0,2:T(4,128)S(1)}, f32[4,64,64]{1,0,2:T(4,128)S(1)}, u32[]{:S(2)}, u32[]{:S(2)}) collective-permute-start(f32[4,64,64]{1,0,2:T(4,128)S(1)} %add.134), channel_id=1, source_target_pairs={{63,0},{0,1},{1,2},{2,3},{3,4},{4,5},{5,6},{6,7},{7,8},{8,9},{9,10... | collective-permute-start | bytes 196616 | tf_op jit(solution)/shard_map/ppermute | solution.py:18
  295.1 4.1 %collective-permute-start.15 = (f32[4,64,64]{1,0,2:T(4,128)S(1)}, f32[4,64,64]{1,0,2:T(4,128)S(1)}, u32[]{:S(2)}, u32[]{:S(2)}) collective-permute-start(f32[4,64,64]{1,0,2:T(4,128)S(1)} %add.134), channel_id=1, source_target_pairs={{0,64},{64,128},{128,192},{1,65},{65,129},{129,193},{2,66},{66,130... | collective-permute-start | bytes 196616 | tf_op jit(solution)/shard_map/ppermute | solution.py:12
  299.2 3.0 convolution_subtract_fusion.1
  303.0 3.0 fusion.72
  306.8 3.0 fusion.55
  309.8 2.1 fusion.56
  313.5 3.3 fusion.258
  318.5 5.0 %collective-permute-start.17 = (f32[4,64,128]{1,0,2:T(4,128)S(1)}, f32[4,64,128]{1,0,2:T(4,128)}, u32[]{:S(2)}, u32[]{:S(2)}) collective-permute-start(f32[4,64,128]{1,0,2:T(4,128)S(1)} %add.136), channel_id=1, source_target_pairs={{0,64},{64,128},{128,192},{1,65},{65,129},{129,193},{2,66},{66,130... | collective-permute-start | bytes 393224 | tf_op jit(solution)/shard_map/ppermute | solution.py:12
  323.5 3.4 fusion.15
  328.7 5.0 %fusion = f32[128,4,64]{2,1,0:T(4,128)S(1)} fusion(bf16[1,1,1,64,64,128]{4,3,5,2,1,0:T(8,128)(2,1)} %copy.76, f32[128,4,64]{2,1,0:T(4,128)S(1)} %gather_fusion.35, pred[128]{0:T(512)(128)(4,1)S(1)} %copy-done.20), kind=kOutput, calls=%fused_computation.36 | convolution fusion | flops 25198592 | bytes 1310848 | tf_op jit(solution)/shard_map/ije,sje->sie/dot_general | solution.py:22
  335.6 5.0 %fusion.40 = f32[4,64,128]{1,0,2:T(4,128)S(1)} fusion(f32[128,4,64]{2,1,0:T(4,128)S(1)} %fusion, f32[128,4,64]{2,1,0:T(4,128)S(1)} %fusion.15, bf16[1,1,1,64,64,128]{4,3,5,2,1,0:T(8,128)(2,1)} %copy.75, f32[1,1,4,64,128]{3,2,4,1,0:T(4,128)S(1)} %copy.44, f32[128,4,64]{2,1,0:T(4,128)S(1)} %gather_fusion.34, pred[128]{0:T(512)(128)(4,1)S(1)} %copy-done.16), kind=kOutput, calls=%fused_computation.62 | convolution fusion | flops 25296896 | bytes 1704064 | tf_op jit(solution)/shard_map/ije,sje->sie/dot_general | solution.py:22
  340.6 3.4 fusion.38
  (188 shorter events, 100.7 us)
Async XLA Ops:
  0.8 9.2 %copy-start.24 = (s32[64]{0:T(128)}, s32[64]{0:T(128)S(1)}, u32[]{:S(2)}) copy-start(s32[64]{0:T(128)S(1)} %get-tuple-element.78) | copy-start | bytes 772
  0.9 9.1 %copy-start.29 = (f32[128]{0:T(128)}, f32[128]{0:T(128)S(1)}, u32[]{:S(2)}) copy-start(f32[128]{0:T(128)S(1)} %broadcast_subtract_fusion.1) | copy-start | bytes 1540
  5.9 14.5 %copy-start.1 = (bf16[64,64,128]{1,0,2:T(8,128)(2,1)}, bf16[64,64,128]{1,0,2:T(8,128)(2,1)S(1)}, u32[]{:S(2)}) copy-start(bf16[64,64,128]{1,0,2:T(8,128)(2,1)S(1)} %copy.45) | copy-start | bytes 3145732
  5.9 11.0 %copy-start.27 = (s32[1,1,128]{2,1,0:T(1,128)S(1)}, s32[1,1,128]{2,1,0:T(1,128)}, u32[]{:S(2)}) copy-start(s32[1,1,128]{2,1,0:T(1,128)} %param.37) | copy-start | bytes 1540
  5.9 11.6 %copy-start.28 = (s32[1,1,64]{2,1,0:T(1,128)S(1)}, s32[1,1,64]{2,1,0:T(1,128)}, u32[]{:S(2)}) copy-start(s32[1,1,64]{2,1,0:T(1,128)} %param.44) | copy-start | bytes 772
  6.0 12.2 %copy-start.31 = (s32[1,1,3,128]{3,1,2,0:T(1,128)S(1)}, s32[1,1,3,128]{3,1,2,0:T(1,128)}, u32[]{:S(2)}) copy-start(s32[1,1,3,128]{3,1,2,0:T(1,128)} %param.36) | copy-start | bytes 4612
  10.0 99.6 %collective-permute-start.1 = (f32[4,64,128]{1,0,2:T(4,128)}, f32[4,64,128]{1,0,2:T(4,128)}, u32[]{:S(2)}, u32[]{:S(2)}) collective-permute-start(f32[4,64,128]{1,0,2:T(4,128)} %fusion.39), channel_id=1, source_target_pairs={{63,0},{0,1},{1,2},{2,3},{3,4},{4,5},{5,6},{6,7},{7,8},{8,9},{9,10... | collective-permute-start | bytes 393224 | tf_op jit(solution)/shard_map/ppermute | solution.py:18
  13.1 104.7 %collective-permute-start = (f32[4,64,128]{1,0,2:T(4,128)}, f32[4,64,128]{1,0,2:T(4,128)}, u32[]{:S(2)}, u32[]{:S(2)}) collective-permute-start(f32[4,64,128]{1,0,2:T(4,128)} %fusion.39), channel_id=1, source_target_pairs={{0,64},{64,128},{128,192},{1,65},{65,129},{129,193},{2,66},{66,130... | collective-permute-start | bytes 393224 | tf_op jit(solution)/shard_map/ppermute | solution.py:12
  17.6 25.6 %copy-start.26 = (s32[32]{0:T(128)}, s32[32]{0:T(128)S(1)}, u32[]{:S(2)}) copy-start(s32[32]{0:T(128)S(1)} %get-tuple-element.76) | copy-start | bytes 388
  18.7 1.7 copy-start.13
  25.6 6.5 %copy-start = (bf16[64,64,128]{0,1,2:T(8,128)(2,1)}, bf16[64,64,128]{0,1,2:T(8,128)(2,1)S(1)}, u32[]{:S(2)}) copy-start(bf16[64,64,128]{0,1,2:T(8,128)(2,1)S(1)} %copy.73) | copy-start | bytes 3145732
  32.1 4.0 %copy-start.21 = (s32[1,1,2,64]{3,2,1,0:T(2,128)S(1)}, s32[1,1,2,64]{3,2,1,0:T(2,128)}, u32[]{:S(2)}) copy-start(s32[1,1,2,64]{3,2,1,0:T(2,128)} %param.38) | copy-start | bytes 1540
  39.4 4.4 %copy-start.32 = (s32[1,1,3,64]{3,1,2,0:T(1,128)S(1)}, s32[1,1,3,64]{3,1,2,0:T(1,128)}, u32[]{:S(2)}) copy-start(s32[1,1,3,64]{3,1,2,0:T(1,128)} %param.43) | copy-start | bytes 2308
  39.4 5.6 %copy-start.5 = (bf16[1,1,3,64,64,64]{5,4,3,2,1,0:T(8,128)(2,1)S(1)}, bf16[1,1,3,64,64,64]{5,4,3,2,1,0:T(8,128)(2,1)}, u32[]{:S(2)}) copy-start(bf16[1,1,3,64,64,64]{5,4,3,2,1,0:T(8,128)(2,1)} %param.42) | copy-start | bytes 4718596
  45.0 3.0 copy-start.22
  46.8 6.0 %copy-start.33 = (s32[1,1,3,32]{3,1,2,0:T(1,128)S(1)}, s32[1,1,3,32]{3,1,2,0:T(1,128)}, u32[]{:S(2)}) copy-start(s32[1,1,3,32]{3,1,2,0:T(1,128)} %param.49) | copy-start | bytes 1156
  49.4 4.0 %copy-start.11 = (bf16[1,1,3,64,64,32]{4,5,3,2,1,0:T(8,128)(2,1)S(1)}, bf16[1,1,3,64,64,32]{4,5,3,2,1,0:T(8,128)(2,1)}, u32[]{:S(2)}) copy-start(bf16[1,1,3,64,64,32]{4,5,3,2,1,0:T(8,128)(2,1)} %param.48) | copy-start | bytes 2359300
  104.1 4.9 %copy-start.34 = (s32[32]{0:T(128)S(1)}, s32[32]{0:T(128)}, u32[]{:S(2)}) copy-start(s32[32]{0:T(128)} %get-tuple-element.19) | copy-start | bytes 388
  104.1 7.9 %copy-start.19 = (pred[128]{0:T(512)(128)(4,1)S(1)}, pred[128]{0:T(512)(128)(4,1)}, u32[]{:S(2)}) copy-start(pred[128]{0:T(512)(128)(4,1)} %get-tuple-element.65) | copy-start | bytes 388
  107.4 12.8 %copy-start.15 = (pred[128]{0:T(512)(128)(4,1)S(1)}, pred[128]{0:T(512)(128)(4,1)}, u32[]{:S(2)}) copy-start(pred[128]{0:T(512)(128)(4,1)} %get-tuple-element.36) | copy-start | bytes 388
  132.6 6.3 %copy-start.4 = (bf16[64,64,64]{0,1,2:T(8,128)(2,1)S(1)}, bf16[64,64,64]{0,1,2:T(8,128)(2,1)}, u32[]{:S(2)}) copy-start(bf16[64,64,64]{0,1,2:T(8,128)(2,1)} %copy.72) | copy-start | bytes 1572868
  132.6 11.7 %copy-start.3 = (bf16[64,64,64]{0,1,2:T(8,128)(2,1)S(1)}, bf16[64,64,64]{0,1,2:T(8,128)(2,1)}, u32[]{:S(2)}) copy-start(bf16[64,64,64]{0,1,2:T(8,128)(2,1)} %copy.71) | copy-start | bytes 1572868
  138.9 1.5 copy-start.8
  140.4 16.7 %copy-start.6 = (f32[4,64,64]{1,0,2:T(4,128)}, f32[4,64,64]{1,0,2:T(4,128)S(1)}, u32[]{:S(2)}) copy-start(f32[4,64,64]{1,0,2:T(4,128)S(1)} %fusion.47) | copy-start | bytes 196612
  140.4 10.6 %collective-permute-start.3 = (f32[4,64,64]{1,0,2:T(4,128)S(1)}, f32[4,64,64]{1,0,2:T(4,128)}, u32[]{:S(2)}, u32[]{:S(2)}) collective-permute-start(f32[4,64,64]{1,0,2:T(4,128)S(1)} %fusion.47), channel_id=1, source_target_pairs={{63,0},{0,1},{1,2},{2,3},{3,4},{4,5},{5,6},{6,7},{7,8},{8,9},{9,10... | collective-permute-start | bytes 196616 | tf_op jit(solution)/shard_map/ppermute | solution.py:18
  140.8 16.3 %collective-permute-start.2 = (f32[4,64,64]{1,0,2:T(4,128)S(1)}, f32[4,64,64]{1,0,2:T(4,128)}, u32[]{:S(2)}, u32[]{:S(2)}) collective-permute-start(f32[4,64,64]{1,0,2:T(4,128)S(1)} %fusion.47), channel_id=1, source_target_pairs={{0,64},{64,128},{128,192},{1,65},{65,129},{129,193},{2,66},{66,130... | collective-permute-start | bytes 196616 | tf_op jit(solution)/shard_map/ppermute | solution.py:12
  172.2 3.5 %collective-permute-start.4 = (f32[4,64,32]{1,0,2:T(4,128)S(1)}, f32[4,64,32]{1,0,2:T(4,128)}, u32[]{:S(2)}, u32[]{:S(2)}) collective-permute-start(f32[4,64,32]{1,0,2:T(4,128)S(1)} %convolution_bitcast_fusion.25), channel_id=1, source_target_pairs={{0,64},{64,128},{128,192},{1,65},{65,129},{129,193},{2,66},{66,130... | collective-permute-start | bytes 98312 | tf_op jit(solution)/shard_map/ppermute | solution.py:12
  178.6 5.1 %collective-permute-start.5 = (f32[4,64,32]{1,0,2:T(4,128)S(1)}, f32[4,64,32]{1,0,2:T(4,128)}, u32[]{:S(2)}, u32[]{:S(2)}) collective-permute-start(f32[4,64,32]{1,0,2:T(4,128)S(1)} %convolution_bitcast_fusion.23), channel_id=1, source_target_pairs={{0,64},{64,128},{128,192},{1,65},{65,129},{129,193},{2,66},{66,130... | collective-permute-start | bytes 98312 | tf_op jit(solution)/shard_map/ppermute | solution.py:12
  186.7 5.7 %collective-permute-start.6 = (f32[4,64,32]{1,0,2:T(4,128)S(1)}, f32[4,64,32]{1,0,2:T(4,128)}, u32[]{:S(2)}, u32[]{:S(2)}) collective-permute-start(f32[4,64,32]{1,0,2:T(4,128)S(1)} %convolution_bitcast_fusion.21), channel_id=1, source_target_pairs={{0,64},{64,128},{128,192},{1,65},{65,129},{129,193},{2,66},{66,130... | collective-permute-start | bytes 98312 | tf_op jit(solution)/shard_map/ppermute | solution.py:12
  196.8 8.5 %collective-permute-start.7 = (f32[4,64,32]{1,0,2:T(4,128)S(1)}, f32[4,64,32]{1,0,2:T(4,128)}, u32[]{:S(2)}, u32[]{:S(2)}) collective-permute-start(f32[4,64,32]{1,0,2:T(4,128)S(1)} %convolution_bitcast_fusion.19), channel_id=1, source_target_pairs={{63,0},{0,1},{1,2},{2,3},{3,4},{4,5},{5,6},{6,7},{7,8},{8,9},{9,10... | collective-permute-start | bytes 98312 | tf_op jit(solution)/shard_map/ppermute | solution.py:18
  210.9 5.4 %collective-permute-start.8 = (f32[4,64,32]{1,0,2:T(4,128)S(1)}, f32[4,64,32]{1,0,2:T(4,128)}, u32[]{:S(2)}, u32[]{:S(2)}) collective-permute-start(f32[4,64,32]{1,0,2:T(4,128)S(1)} %convolution_bitcast_fusion.16), channel_id=1, source_target_pairs={{0,64},{64,128},{128,192},{1,65},{65,129},{129,193},{2,66},{66,130... | collective-permute-start | bytes 98312 | tf_op jit(solution)/shard_map/ppermute | solution.py:12
  220.7 5.3 %collective-permute-start.9 = (f32[4,64,32]{1,0,2:T(4,128)S(1)}, f32[4,64,32]{1,0,2:T(4,128)}, u32[]{:S(2)}, u32[]{:S(2)}) collective-permute-start(f32[4,64,32]{1,0,2:T(4,128)S(1)} %convolution_bitcast_fusion.14), channel_id=1, source_target_pairs={{0,64},{64,128},{128,192},{1,65},{65,129},{129,193},{2,66},{66,130... | collective-permute-start | bytes 98312 | tf_op jit(solution)/shard_map/ppermute | solution.py:12
  230.4 5.5 %collective-permute-start.10 = (f32[4,64,32]{1,0,2:T(4,128)S(1)}, f32[4,64,32]{1,0,2:T(4,128)}, u32[]{:S(2)}, u32[]{:S(2)}) collective-permute-start(f32[4,64,32]{1,0,2:T(4,128)S(1)} %convolution_bitcast_fusion.12), channel_id=1, source_target_pairs={{0,64},{64,128},{128,192},{1,65},{65,129},{129,193},{2,66},{66,130... | collective-permute-start | bytes 98312 | tf_op jit(solution)/shard_map/ppermute | solution.py:12
  239.8 17.4 %copy-start.12 = (f32[4,64,32]{1,0,2:T(4,128)S(1)}, f32[4,64,32]{1,0,2:T(4,128)}, u32[]{:S(2)}) copy-start(f32[4,64,32]{1,0,2:T(4,128)} %convolution_bitcast_fusion.26) | copy-start | bytes 98308
  242.4 10.5 %collective-permute-start.11 = (f32[4,64,32]{1,0,2:T(4,128)}, f32[4,64,32]{1,0,2:T(4,128)}, u32[]{:S(2)}, u32[]{:S(2)}) collective-permute-start(f32[4,64,32]{1,0,2:T(4,128)} %convolution_bitcast_fusion.10), channel_id=1, source_target_pairs={{63,0},{0,1},{1,2},{2,3},{3,4},{4,5},{5,6},{6,7},{7,8},{8,9},{9,10... | collective-permute-start | bytes 98312 | tf_op jit(solution)/shard_map/ppermute | solution.py:18
  257.2 7.4 %copy-start.10 = (f32[4,64,32]{1,0,2:T(4,128)}, f32[4,64,32]{1,0,2:T(4,128)S(1)}, u32[]{:S(2)}) copy-start(f32[4,64,32]{1,0,2:T(4,128)S(1)} %fusion.68) | copy-start | bytes 98308
  257.7 5.4 %collective-permute-start.12 = (f32[4,64,32]{1,0,2:T(4,128)S(1)}, f32[4,64,32]{1,0,2:T(4,128)}, u32[]{:S(2)}, u32[]{:S(2)}) collective-permute-start(f32[4,64,32]{1,0,2:T(4,128)S(1)} %convolution_bitcast_fusion.7), channel_id=1, source_target_pairs={{0,64},{64,128},{128,192},{1,65},{65,129},{129,193},{2,66},{66,130... | collective-permute-start | bytes 98312 | tf_op jit(solution)/shard_map/ppermute | solution.py:12
  265.5 20.7 %copy-start.7 = (f32[4,64,64]{1,0,2:T(4,128)S(1)}, f32[4,64,64]{1,0,2:T(4,128)}, u32[]{:S(2)}) copy-start(f32[4,64,64]{1,0,2:T(4,128)} %copy-done.6) | copy-start | bytes 196612
  266.1 5.1 %collective-permute-start.13 = (f32[4,64,32]{1,0,2:T(4,128)S(1)}, f32[4,64,32]{1,0,2:T(4,128)}, u32[]{:S(2)}, u32[]{:S(2)}) collective-permute-start(f32[4,64,32]{1,0,2:T(4,128)S(1)} %convolution_bitcast_fusion.5), channel_id=1, source_target_pairs={{0,64},{64,128},{128,192},{1,65},{65,129},{129,193},{2,66},{66,130... | collective-permute-start | bytes 98312 | tf_op jit(solution)/shard_map/ppermute | solution.py:12
  275.6 5.1 %collective-permute-start.14 = (f32[4,64,32]{1,0,2:T(4,128)S(1)}, f32[4,64,32]{1,0,2:T(4,128)}, u32[]{:S(2)}, u32[]{:S(2)}) collective-permute-start(f32[4,64,32]{1,0,2:T(4,128)S(1)} %convolution_bitcast_fusion.3), channel_id=1, source_target_pairs={{0,64},{64,128},{128,192},{1,65},{65,129},{129,193},{2,66},{66,130... | collective-permute-start | bytes 98312 | tf_op jit(solution)/shard_map/ppermute | solution.py:12
  285.2 17.8 %copy-start.18 = (pred[64]{0:T(512)(128)(4,1)S(1)}, pred[64]{0:T(512)(128)(4,1)}, u32[]{:S(2)}) copy-start(pred[64]{0:T(512)(128)(4,1)} %get-tuple-element.61) | copy-start | bytes 196
  288.5 18.3 %copy-start.9 = (f32[4,64,64]{1,0,2:T(4,128)S(1)}, f32[4,64,64]{1,0,2:T(4,128)}, u32[]{:S(2)}) copy-start(f32[4,64,64]{1,0,2:T(4,128)} %copy-done.8) | copy-start | bytes 196612
  288.5 18.3 %copy-start.14 = (pred[64]{0:T(512)(128)(4,1)S(1)}, pred[64]{0:T(512)(128)(4,1)}, u32[]{:S(2)}) copy-start(pred[64]{0:T(512)(128)(4,1)} %get-tuple-element.24) | copy-start | bytes 196
  289.4 12.8 %collective-permute-start.16 = (f32[4,64,64]{1,0,2:T(4,128)S(1)}, f32[4,64,64]{1,0,2:T(4,128)S(1)}, u32[]{:S(2)}, u32[]{:S(2)}) collective-permute-start(f32[4,64,64]{1,0,2:T(4,128)S(1)} %add.134), channel_id=1, source_target_pairs={{63,0},{0,1},{1,2},{2,3},{3,4},{4,5},{5,6},{6,7},{7,8},{8,9},{9,10... | collective-permute-start | bytes 196616 | tf_op jit(solution)/shard_map/ppermute | solution.py:18
  295.1 10.9 %collective-permute-start.15 = (f32[4,64,64]{1,0,2:T(4,128)S(1)}, f32[4,64,64]{1,0,2:T(4,128)S(1)}, u32[]{:S(2)}, u32[]{:S(2)}) collective-permute-start(f32[4,64,64]{1,0,2:T(4,128)S(1)} %add.134), channel_id=1, source_target_pairs={{0,64},{64,128},{128,192},{1,65},{65,129},{129,193},{2,66},{66,130... | collective-permute-start | bytes 196616 | tf_op jit(solution)/shard_map/ppermute | solution.py:12
  302.2 7.7 %copy-start.23 = (f32[64]{0:T(128)S(1)}, f32[64]{0:T(128)}, u32[]{:S(2)}) copy-start(f32[64]{0:T(128)} %broadcast_subtract_fusion) | copy-start | bytes 772
  303.0 9.0 %copy-start.25 = (s32[64]{0:T(128)S(1)}, s32[64]{0:T(128)}, u32[]{:S(2)}) copy-start(s32[64]{0:T(128)} %copy-done.24) | copy-start | bytes 772
  312.3 11.2 %copy-start.17 = (pred[128]{0:T(512)(128)(4,1)S(1)}, pred[128]{0:T(512)(128)(4,1)}, u32[]{:S(2)}) copy-start(pred[128]{0:T(512)(128)(4,1)} %get-tuple-element.63) | copy-start | bytes 388
  316.8 11.9 %copy-start.20 = (pred[128]{0:T(512)(128)(4,1)S(1)}, pred[128]{0:T(512)(128)(4,1)}, u32[]{:S(2)}) copy-start(pred[128]{0:T(512)(128)(4,1)} %get-tuple-element.65) | copy-start | bytes 388
  317.8 9.1 %collective-permute-start.18 = (f32[4,64,128]{1,0,2:T(4,128)S(1)}, f32[4,64,128]{1,0,2:T(4,128)}, u32[]{:S(2)}, u32[]{:S(2)}) collective-permute-start(f32[4,64,128]{1,0,2:T(4,128)S(1)} %add.136), channel_id=1, source_target_pairs={{63,0},{0,1},{1,2},{2,3},{3,4},{4,5},{5,6},{6,7},{7,8},{8,9},{9,10... | collective-permute-start | bytes 393224 | tf_op jit(solution)/shard_map/ppermute | solution.py:18
  318.5 15.2 %collective-permute-start.17 = (f32[4,64,128]{1,0,2:T(4,128)S(1)}, f32[4,64,128]{1,0,2:T(4,128)}, u32[]{:S(2)}, u32[]{:S(2)}) collective-permute-start(f32[4,64,128]{1,0,2:T(4,128)S(1)} %add.136), channel_id=1, source_target_pairs={{0,64},{64,128},{128,192},{1,65},{65,129},{129,193},{2,66},{66,130... | collective-permute-start | bytes 393224 | tf_op jit(solution)/shard_map/ppermute | solution.py:12
  326.9 8.6 %copy-start.16 = (pred[128]{0:T(512)(128)(4,1)S(1)}, pred[128]{0:T(512)(128)(4,1)}, u32[]{:S(2)}) copy-start(pred[128]{0:T(512)(128)(4,1)} %get-tuple-element.36) | copy-start | bytes 388
  333.7 6.9 %copy-start.2 = (bf16[64,64,128]{1,0,2:T(8,128)(2,1)S(1)}, bf16[64,64,128]{1,0,2:T(8,128)(2,1)}, u32[]{:S(2)}) copy-start(bf16[64,64,128]{1,0,2:T(8,128)(2,1)} %copy-done.1) | copy-start | bytes 3145732
  333.7 6.9 %copy-start.30 = (f32[128]{0:T(128)S(1)}, f32[128]{0:T(128)}, u32[]{:S(2)}) copy-start(f32[128]{0:T(128)} %copy-done.29) | copy-start | bytes 1540
where the time goes:
time: 351 us; the launch traced here: 345 us
  local copies, waits for them, and re-layouts  132 us (38%)
  matrix products  118 us (34%)
  starting transfers between devices  75.5 us (22%)
  other arithmetic  13.1 us (4%)
  waiting for transfers between devices  5.66 us (2%)
    dot_general x50, matrix products, block_product(): jnp.einsum('ije,sje->sie', matrix.astype(jnp.float32), vector, precision=...  117 us
    ppermute x13, starting transfers between devices, shifted(): return lax.ppermute(shard, axis, pairs)  55.7 us
    unnamed x79, local copies, waits for them, and re-layouts  41.8 us
    ppermute x6, starting transfers between devices, from_behind(): return lax.ppermute(block, axis, route)  19.8 us
    squeeze x5, local copies, waits for them, and re-layouts, own_part(): return array[0, 0]  18.6 us
    gather x10, local copies, waits for them, and re-layouts, front_step(): jnp.take(upstream, link, axis=2)  16.7 us
    gather x8, local copies, waits for them, and re-layouts, restrict(): chosen = jnp.take(residual, jnp.take(fine_ids, picks[link_slot]), axis=2)  9.74 us
    gather x4, local copies, waits for them, and re-layouts, operate(): jnp.take(upstream, links[1], axis=2)  7.36 us
  transfers between devices with their start and end apart: 19, of which 8 were waited for; matrix products, arithmetic and copies ran while one was open for 41% of the time, Pallas kernels for 0%

commit v1 on v0

v1 whole, which is shorter than its diff:
```python
import functools

import jax
import jax.numpy as jnp
from jax import lax
from jax.experimental import pallas as pl
from jax.experimental.pallas import tpu as pltpu
from jax.sharding import PartitionSpec as P

SWEEPS = 3
S = 4
B = 64
LANES = 128


F_LINK, F_PICK, F_COARSE = 0, 3, 5
M_LINK, M_PICK, M_COARSE, M_FINE = 6, 9, 11, 12
C_LINK, M_POS, TABLE = 13, 16, 24


def lane_index():
    return lax.broadcasted_iota(jnp.int32, (1, LANES), 1)


def take_lanes(x, index):
    rows = x.reshape(-1, LANES)
    index = jnp.broadcast_to(index, rows.shape)
    return jnp.take_along_axis(rows, index, axis=1, mode="promise_in_bounds").reshape(x.shape)


def expand(packed, index, out, scale=None):
    rows = packed.shape[1]
    r = B // rows
    for h in range(r):
        values = take_lanes(packed, index + h * (LANES // r))
        if scale is not None:
            values = values * scale
        out[:, h * rows : (h + 1) * rows, :] = values


def pack(wide, r):
    rows = B // r
    group = lane_index() // (LANES // r)
    result = wide[:, :rows, :]
    for h in range(1, r):
        result = jnp.where(group == h, wide[:, h * rows : (h + 1) * rows, :], result)
    return result


def fold(parts):
    row = lax.broadcasted_iota(jnp.int32, (8, LANES), 0)
    high = row >= 4
    mid = (row & 2) > 0
    low = (row & 1) > 0
    level = []
    for i in range(4):
        a, b = parts[i], parts[i + 4]
        level.append(jnp.where(high, b, a) + pltpu.roll(jnp.where(high, a, b), 4, 0))
    pairs = []
    for i in range(2):
        a, b = level[i], level[i + 2]
        pairs.append(jnp.where(mid, b + pltpu.roll(b, 2, 0), a + pltpu.roll(a, 6, 0)))
    a, b = pairs
    return jnp.where(low, b + pltpu.roll(b, 1, 0), a + pltpu.roll(a, 7, 0))


def products(blocks, fields, rows, emit):
    def body(step, carry):
        base = pl.multiple_of(step * 8, 8)
        parts = [[None] * 8 for _ in range(S)]
        for block, field in zip(blocks, fields):
            for i in range(8):
                matrix = block[base + i].astype(jnp.float32)
                for s in range(S):
                    part = jnp.sum((matrix * field[s]).reshape(8, 8, LANES), axis=0)
                    parts[s][i] = part if parts[s][i] is None else parts[s][i] + part
        for s in range(S):
            emit(s, pl.ds(base, 8), fold(parts[s]))
        return carry

    lax.fori_loop(0, rows // 8, body, 0)


def positions(order, n):
    padded = order if n == LANES else jnp.where(lane_index() < n, order, -1)
    hit = padded == lax.broadcasted_iota(jnp.int32, (LANES, LANES), 0)
    place = lax.broadcasted_iota(jnp.int32, (8, LANES), 1).astype(jnp.float32)
    return lax.dot_general(
        place.astype(jnp.bfloat16),
        hit.astype(jnp.float32).astype(jnp.bfloat16),
        (((1,), (1,)), ((), ())),
        preferred_element_type=jnp.float32,
    )


def start_kernel(b, inverse, order, f0, sent):
    place = positions(order[...], LANES)
    mask = (place[0:1] >= 63.5).astype(jnp.float32)

    def emit(s, rows, tile):
        f0[s, rows, :] = tile * mask

    products([inverse], [b], B, emit)
    lane = lane_index()
    index = take_lanes(jnp.broadcast_to(order[...], (8, LANES)), 64 + lane % 64)[0:1]
    wide = take_lanes(f0[...], index)
    sent[0:128, :] = pack(wide, 2).reshape(128, LANES)
    sent[128:136, :] = place


def prepare_kernel(
    f_links, f_order, f_picks, m_links, m_order, m_picks, c_links,
    m_diag, m_inverse, m_faces, f_weights, c_inverse, c_faces, m_weights,
    table, middle, coarse,
):
    lane = lane_index()

    def spread(row, n):
        return jnp.concatenate([row] * (LANES // n), axis=1)

    def pick(source, index):
        source = jnp.broadcast_to(source, (8, LANES))
        return take_lanes(source, jnp.broadcast_to(index, (8, LANES)))[0:1]

    for k in range(3):
        table[F_LINK + k : F_LINK + k + 1, :] = f_links[k : k + 1, :]
        table[M_LINK + k : M_LINK + k + 1, :] = spread(m_links[k : k + 1, :], 64)
        table[C_LINK + k : C_LINK + k + 1, :] = spread(c_links[k : k + 1, :], 32)
    order = f_order[...]
    wide_order = spread(m_order[...], 64)
    for k in range(2):
        table[F_PICK + k : F_PICK + k + 1, :] = pick(order, 64 + spread(f_picks[k : k + 1, :], 64))
        table[M_PICK + k : M_PICK + k + 1, :] = pick(wide_order, 32 + spread(m_picks[k : k + 1, :], 32))
    table[F_COARSE : F_COARSE + 1, :] = pick(order, lane % 64)
    table[M_COARSE : M_COARSE + 1, :] = pick(wide_order, lane % 32)
    table[M_FINE : M_FINE + 1, :] = pick(wide_order, 32 + lane % 32)
    place = positions(wide_order, 64)
    place = pick(place.astype(jnp.int32), lane % 64)
    table[M_POS:TABLE, :] = jnp.broadcast_to(place, (TABLE - M_POS, LANES))

    def halves(i, carry):
        for slot, source in enumerate(
            [m_diag, m_inverse, m_faces.at[0], m_faces.at[1], m_faces.at[2], f_weights.at[0], f_weights.at[1]]
        ):
            middle[slot, i] = jnp.concatenate([source[i], source[32 + i]], axis=1)
        return carry

    def quarters(i, carry):
        for slot, source in enumerate(
            [c_inverse, c_faces.at[0], c_faces.at[1], c_faces.at[2], m_weights.at[0], m_weights.at[1]]
        ):
            coarse[slot, i] = jnp.concatenate([source[16 * q + i] for q in range(4)], axis=1)
        return carry

    lax.fori_loop(0, 32, halves, 0)
    lax.fori_loop(0, 16, quarters, 0)


M_DIAG, M_INVERSE, M_FACE, F_WEIGHT = 0, 1, 2, 5
C_INVERSE, C_FACE, M_WEIGHT = 0, 1, 4


def row(table, k):
    return table[k : k + 1, :]


def fine_local_kernel(b, f0, diag, faces, links, out, own, linked):
    own[...] = -f0[...]
    linked[...] = take_lanes(f0[...], row(links, 0))

    def emit(s, rows, tile):
        out[s, rows, :] = b[s, rows, :] + tile

    products([diag, faces.at[0]], [own, linked], B, emit)


def chosen(place, index, low, high):
    spot = take_lanes(jnp.broadcast_to(place, (8, LANES)), jnp.broadcast_to(index, (8, LANES)))[0:1]
    inside = (spot >= low) & (spot < high)
    return jnp.clip(spot - low, 0, high - low - 1), inside.astype(jnp.float32)


def fine_down_kernel(
    known, up, beside, faces, table, middle, flow,
    r0, right, f0, sent, v1, v2, wide,
):
    gate = (flow[0] > 0).astype(jnp.float32)
    for v, got, k, scale in ((v1, up, 1, gate), (v2, beside, 2, None)):
        index, inside = chosen(got[128:136, :].astype(jnp.int32)[0:1], row(table, F_LINK + k), 64, 128)
        expand(got[0:128, :].reshape(S, 32, LANES), index, v, inside if scale is None else inside * scale)

    def emit_residual(s, rows, tile):
        r0[s, rows, :] = known[s, rows, :] + tile

    products([faces.at[1], faces.at[2]], [v1, v2], B, emit_residual)
    residual = r0[...]
    v1[...] = take_lanes(residual, row(table, F_PICK))
    v2[...] = take_lanes(residual, row(table, F_PICK + 1))
    wide[...] = take_lanes(residual, row(table, F_COARSE))
    right[...] = pack(wide[...], 2)

    def emit_right(s, rows, tile):
        right[s, rows, :] += tile

    products([middle.at[F_WEIGHT], middle.at[F_WEIGHT + 1]], [v1, v2], 32, emit_right)
    expand(right[...], lane_index() % 64, wide)
    mask = (row(table, M_POS) >= 32).astype(jnp.float32)

    def emit_field(s, rows, tile):
        f0[s, rows, :] = tile * mask

    products([middle.at[M_INVERSE]], [wide], 32, emit_field)
    expand(f0[...], row(table, M_FINE), wide)
    sent[0:64, :] = pack(wide[...], 4).reshape(64, LANES)
    sent[64:72, :] = table[M_POS:TABLE, :].astype(jnp.float32)


def middle_local_kernel(b, f0, middle, table, out, own, linked):
    expand(-f0[...], lane_index() % 64, own)
    expand(f0[...], row(table, M_LINK), linked)

    def emit(s, rows, tile):
        out[s, rows, :] = b[s, rows, :] + tile

    products([middle.at[M_DIAG], middle.at[M_FACE]], [own, linked], 32, emit)


def middle_down_kernel(
    known, up, beside, middle, coarse, table, flow,
    r0, right, first, v1, v2, wide,
):
    gate = (flow[0] > 0).astype(jnp.float32)
    for v, got, k, scale in ((v1, up, 1, gate), (v2, beside, 2, None)):
        index, inside = chosen(got[64:72, :].astype(jnp.int32)[0:1], row(table, M_LINK + k), 32, 64)
        expand(got[0:64, :].reshape(S, 16, LANES), index, v, inside if scale is None else inside * scale)

    def emit_residual(s, rows, tile):
        r0[s, rows, :] = known[s, rows, :] + tile

    products([middle.at[M_FACE + 1], middle.at[M_FACE + 2]], [v1, v2], 32, emit_residual)
    residual = r0[...]
    expand(residual, row(table, M_PICK), v1)
    expand(residual, row(table, M_PICK + 1), v2)
    expand(residual, row(table, M_COARSE), wide)
    right[...] = pack(wide[...], 4)

    def emit_right(s, rows, tile):
        right[s, rows, :] += tile

    products([coarse.at[M_WEIGHT], coarse.at[M_WEIGHT + 1]], [v1, v2], 16, emit_right)
    expand(right[...], lane_index() % 32, wide)
    start = (flow[0] == 0).astype(jnp.float32)

    def emit_first(s, rows, tile):
        first[s, rows, :] = tile * start

    products([coarse.at[C_INVERSE]], [wide], 16, emit_first)


def coarse_local_kernel(right, own, coarse, table, out, wide):
    expand(own[...], row(table, C_LINK), wide)

    def emit(s, rows, tile):
        out[s, rows, :] = right[s, rows, :] + tile

    products([coarse.at[C_FACE]], [wide], 16, emit)


def coarse_step_kernel(step, known, own, up, beside, coarse, table, flow, out, v1, v2, total):
    g = flow[0]
    gate = (g > 0).astype(jnp.float32)
    expand(up[...], row(table, C_LINK + 1), v1, gate)
    expand(beside[...], row(table, C_LINK + 2), v2)

    def emit_total(s, rows, tile):
        total[s, rows, :] = known[s, rows, :] + tile

    products([coarse.at[C_FACE + 1], coarse.at[C_FACE + 2]], [v1, v2], 16, emit_total)
    expand(total[...], lane_index() % 32, v1)
    sweep = jnp.broadcast_to(step - g, (8, LANES))

    def emit(s, rows, tile):
        fresh = jnp.where(sweep >= 0, tile, 0.0)
        out[s, rows, :] = jnp.where(sweep < SWEEPS, fresh, own[s, rows, :])

    products([coarse.at[C_INVERSE]], [v1], 16, emit)


def middle_up_local_kernel(r0, fix, middle, table, out, own, linked):
    place = row(table, M_POS)
    index, inside = chosen(place, lane_index() % 64, 0, 32)
    expand(-fix[...], index, own, inside)
    index, inside = chosen(place, row(table, M_LINK), 0, 32)
    expand(fix[...], index, linked, inside)

    def emit(s, rows, tile):
        out[s, rows, :] = r0[s, rows, :] + tile

    products([middle.at[M_DIAG], middle.at[M_FACE]], [own, linked], 32, emit)


def middle_up_kernel(
    known, f0, fix, up, beside, up_place, beside_place, middle, table, flow,
    out, v1, v2, total,
):
    gate = (flow[0] > 0).astype(jnp.float32)
    for v, got, places, k, scale in ((v1, up, up_place, 1, gate), (v2, beside, beside_place, 2, None)):
        place = places[64:72, :].astype(jnp.int32)[0:1]
        index, inside = chosen(place, row(table, M_LINK + k), 0, 32)
        expand(got[...], index, v, inside if scale is None else inside * scale)

    def emit_total(s, rows, tile):
        total[s, rows, :] = known[s, rows, :] + tile

    products([middle.at[M_FACE + 1], middle.at[M_FACE + 2]], [v1, v2], 32, emit_total)
    place = row(table, M_POS)
    index, inside = chosen(place, lane_index() % 64, 0, 32)
    expand(fix[...], index, v1, inside)
    out[...] = f0[...] + pack(v1[...], 2)
    expand(total[...], lane_index() % 64, v2)
    mask = (place >= 32).astype(jnp.float32)

    def emit(s, rows, tile):
        out[s, rows, :] += tile * mask

    products([middle.at[M_INVERSE]], [v2], 32, emit)


def fine_up_local_kernel(r0, fix, diag, faces, links, sent, out, own, linked):
    place = sent[128:136, :].astype(jnp.int32)[0:1]
    index, inside = chosen(place, lane_index(), 0, 64)
    expand(-fix[...], index, own, inside)
    index, inside = chosen(place, row(links, 0), 0, 64)
    expand(fix[...], index, linked, inside)

    def emit(s, rows, tile):
        out[s, rows, :] = r0[s, rows, :] + tile

    products([diag, faces.at[0]], [own, linked], B, emit)


def fine_up_kernel(
    known, f0, fix, up, beside, up_place, beside_place, faces, inverse, links, sent, flow,
    out, v1, v2, total,
):
    gate = (flow[0] > 0).astype(jnp.float32)
    for v, got, places, k, scale in ((v1, up, up_place, 1, gate), (v2, beside, beside_place, 2, None)):
        place = places[128:136, :].astype(jnp.int32)[0:1]
        index, inside = chosen(place, row(links, k), 0, 64)
        expand(got[...], index, v, inside if scale is None else inside * scale)

    def emit_total(s, rows, tile):
        total[s, rows, :] = known[s, rows, :] + tile

    products([faces.at[1], faces.at[2]], [v1, v2], B, emit_total)
    place = sent[128:136, :].astype(jnp.int32)[0:1]
    index, inside = chosen(place, lane_index(), 0, 64)
    expand(fix[...], index, v1, inside)
    mask = (place >= 64).astype(jnp.float32)

    def emit(s, rows, tile):
        out[s, rows, :] = f0[s, rows, :] + v1[s, rows, :] + tile * mask

    products([inverse], [total], B, emit)


WIDE = pltpu.VMEM((S, B, LANES), jnp.float32)


def f32(*shape):
    return jax.ShapeDtypeStruct(shape, jnp.float32)


def call(kernel, operands, outs, scratch=(), work=1.0, flow=None):
    specs = [pl.BlockSpec(memory_space=pltpu.VMEM)] * len(operands)
    if flow is not None:
        specs.append(pl.BlockSpec(memory_space=pltpu.SMEM))
        operands = (*operands, flow)
    return pl.pallas_call(
        kernel,
        out_shape=outs,
        in_specs=specs,
        out_specs=jax.tree.map(lambda _: pl.BlockSpec(memory_space=pltpu.VMEM), outs),
        scratch_shapes=list(scratch),
        compiler_params=pltpu.CompilerParams(vmem_limit_bytes=40 * 1024 * 1024),
        cost_estimate=pl.CostEstimate(
            flops=int(work * 4_000_000), bytes_accessed=int(work * 1_000_000), transcendentals=0
        ),
    )(*operands)


def from_behind(block, axis):
    size = lax.axis_size(axis)
    return lax.ppermute(block, axis, [(i, (i + 1) % size) for i in range(size)])


def own_part(array):
    return array[0, 0]


def shards(*arrays):
    (
        b, f_diag, f_inverse, f_faces, f_links, f_order, f_picks, f_weights,
        m_diag, m_inverse, m_faces, m_links, m_order, m_picks, m_weights,
        c_inverse, c_faces, c_links,
    ) = map(own_part, arrays)
    flow_size = lax.axis_size("flow")
    flow = lax.axis_index("flow").astype(jnp.int32).reshape(1)
    f_order = f_order.reshape(1, LANES)
    m_order = m_order.reshape(1, 64)

    f0, f_sent = call(start_kernel, (b, f_inverse, f_order), (f32(S, B, LANES), f32(136, LANES)))
    f_up, f_beside = from_behind(f_sent, "flow"), from_behind(f_sent, "tile")
    table, middle, coarse = call(
        prepare_kernel,
        (
            f_links, f_order, f_picks, m_links, m_order, m_picks, c_links,
            m_diag, m_inverse, m_faces, f_weights, c_inverse, c_faces, m_weights,
        ),
        (
            jax.ShapeDtypeStruct((TABLE, LANES), jnp.int32),
            jax.ShapeDtypeStruct((7, 32, B, LANES), jnp.bfloat16),
            jax.ShapeDtypeStruct((6, 16, B, LANES), jnp.bfloat16),
        ),
    )
    known = call(
        fine_local_kernel, (b, f0, f_diag, f_faces, f_links), f32(S, B, LANES), (WIDE, WIDE), 2.0
    )
    f_r0, right, m_f0, m_sent = call(
        fine_down_kernel,
        (known, f_up, f_beside, f_faces, table, middle),
        (f32(S, B, LANES), f32(S, 32, LANES), f32(S, 32, LANES), f32(72, LANES)),
        (WIDE, WIDE, WIDE),
        3.5,
        flow,
    )
    m_up, m_beside = from_behind(m_sent, "flow"), from_behind(m_sent, "tile")
    known = call(middle_local_kernel, (right, m_f0, middle, table), f32(S, 32, LANES), (WIDE, WIDE))
    m_r0, right, value = call(
        middle_down_kernel,
        (known, m_up, m_beside, middle, coarse, table),
        (f32(S, 32, LANES), f32(S, 16, LANES), f32(S, 16, LANES)),
        (WIDE, WIDE, WIDE),
        2.0,
        flow,
    )
    packed16 = pltpu.VMEM((S, 16, LANES), jnp.float32)
    for step in range(1, SWEEPS + flow_size - 1):
        up, beside = from_behind(value, "flow"), from_behind(value, "tile")
        known = call(coarse_local_kernel, (right, value, coarse, table), f32(S, 16, LANES), (WIDE,), 0.25)
        value = call(
            functools.partial(coarse_step_kernel, step),
            (known, value, up, beside, coarse, table),
            f32(S, 16, LANES),
            (WIDE, WIDE, packed16),
            0.75,
            flow,
        )
    beside = from_behind(value, "tile")
    known = call(middle_up_local_kernel, (m_r0, value, middle, table), f32(S, 32, LANES), (WIDE, WIDE))
    fix = call(
        middle_up_kernel,
        (known, m_f0, value, up, beside, m_up, m_beside, middle, table),
        f32(S, 32, LANES),
        (WIDE, WIDE, pltpu.VMEM((S, 32, LANES), jnp.float32)),
        1.5,
        flow,
    )
    up, beside = from_behind(fix, "flow"), from_behind(fix, "tile")
    known = call(
        fine_up_local_kernel,
        (f_r0, fix, f_diag, f_faces, f_links, f_sent),
        f32(S, B, LANES),
        (WIDE, WIDE),
        2.0,
    )
    field = call(
        fine_up_kernel,
        (known, f0, fix, up, beside, f_up, f_beside, f_faces, f_inverse, f_links, f_sent),
        f32(S, B, LANES),
        (WIDE, WIDE, WIDE),
        3.0,
        flow,
    )
    return field[None, None]


def solution(mesh):
    ranks = (5, 5, 5, 6, 4, 3, 4, 6, 5, 5, 6, 4, 3, 4, 6, 5, 6, 4)
    return jax.shard_map(
        shards,
        mesh=mesh,
        in_specs=tuple(P("flow", "tile", *[None] * (rank - 2)) for rank in ranks),
        out_specs=P("flow", "tile", None, None, None),
        check_vma=False,
    )
```

time: 351 us -> 110 us (0.31)
  the two profiles are of different devices: /device:TPU:121 before, /device:TPU:2 now
where the time goes in v1:
time: 110 us; the launch traced here: 109 us
  waiting for transfers between devices  49.2 us (45%)
  Pallas kernels  31.7 us (29%)
  local copies, waits for them, and re-layouts  16.6 us (15%)
  starting transfers between devices  11.4 us (10%)
    ppermute x17, waiting for transfers between devices, from_behind(): return lax.ppermute(block, axis, [(i, (i + 1) % size) for i in range(size)])  49.2 us
    pallas_call x20, Pallas kernels, call(): pl.pallas_call(kernel, out_shape=outs, in_specs=specs, out_specs=jax.tree...  31.7 us
    unnamed x44, local copies, waits for them, and re-layouts  16.6 us
    ppermute x17, starting transfers between devices, from_behind(): return lax.ppermute(block, axis, [(i, (i + 1) % size) for i in range(size)])  11.4 us
  transfers between devices with their start and end apart: 17, of which 15 were waited for; matrix products, arithmetic and copies ran while one was open for 7% of the time, Pallas kernels for 15%

profile of v1, /device:TPU:2, one launch (start us, length us, event | category | flops | bytes accessed | tf_op | source)
XLA Modules:
  0.0 109.2 jit_solution(2055179724904985524)
XLA Ops:
  0.0 1.2 %copy-done.3 = bf16[1,1,64,64,128]{4,3,2,1,0:T(8,128)(2,1)S(1)} copy-done((bf16[1,1,64,64,128]{4,3,2,1,0:T(8,128)(2,1)S(1)}, bf16[1,1,64,64,128]{4,3,2,1,0:T(8,128)(2,1)}, u32[]{:S(2)}) %copy-start.3) | copy-done | bytes 1048600
  1.2 0.9 copy-done.9
  2.1 0.7 copy-done.11
  2.8 1.1 %shard_map.172 = (f32[4,64,128]{2,1,0:T(8,128)S(1)}, f32[136,128]{1,0:T(8,128)S(1)}) custom-call(f32[4,64,128]{2,1,0:T(8,128)S(1)} %bitcast.40, bf16[64,64,128]{2,1,0:T(8,128)(2,1)S(1)} %bitcast.34, s32[1,128]{1,0:T(1,128)S(1)} %bitcast.48), custom_call_target="tpu_custom_call" | custom-call | flops 4000000 | bytes 1000000 | tf_op jit(solution)/shard_map/pallas_call | solution.py:379
  3.9 1.6 %collective-permute-start = (f32[136,128]{1,0:T(8,128)S(1)}, f32[136,128]{1,0:T(8,128)S(1)}, u32[]{:S(2)}, u32[]{:S(2)}) collective-permute-start(f32[136,128]{1,0:T(8,128)S(1)} %get-tuple-element.18.sent), channel_id=1, source_target_pairs={{0,64},{64,128},{128,192},{192,0},{1,65},{65,129},{129,193},{193,1... | collective-permute-start | bytes 208904 | tf_op jit(solution)/shard_map/ppermute | solution.py:394
  5.5 0.7 copy.30
  6.2 4.2 %copy.20 = bf16[1,1,3,64,64,32]{5,4,3,2,1,0:T(8,128)(2,1)} copy(bf16[1,1,3,64,64,32]{4,5,3,2,1,0:T(8,128)(2,1)} %param.34) | data formatting | bytes 1572864 | tf_op args[16]
  10.3 0.0 copy-start.12
  10.4 0.0 copy-start.13
  10.4 0.0 copy-start.14
  10.4 0.0 copy-start.15
  10.4 1.0 copy.21
  11.4 1.5 %copy.19 = bf16[1,1,64,64,32]{4,3,2,1,0:T(8,128)(2,1)S(1)} copy(bf16[1,1,64,64,32]{3,4,2,1,0:T(8,128)(2,1)} %param.33) | data formatting | bytes 524288 | tf_op args[15]
  13.0 0.0 copy-start.5
  13.1 1.9 %copy-done.5 = bf16[1,1,3,64,64,64]{5,4,3,2,1,0:T(8,128)(2,1)S(1)} copy-done((bf16[1,1,3,64,64,64]{5,4,3,2,1,0:T(8,128)(2,1)S(1)}, bf16[1,1,3,64,64,64]{5,4,3,2,1,0:T(8,128)(2,1)}, u32[]{:S(2)}) %copy-start.5) | copy-done | bytes 1572888
  14.9 1.6 %copy-done.6 = bf16[1,1,2,64,64,64]{5,4,3,2,1,0:T(8,128)(2,1)S(1)} copy-done((bf16[1,1,2,64,64,64]{5,4,3,2,1,0:T(8,128)(2,1)S(1)}, bf16[1,1,2,64,64,64]{5,4,3,2,1,0:T(8,128)(2,1)}, u32[]{:S(2)}) %copy-start.6) | copy-done | bytes 1048600
  16.5 1.2 %copy-done.7 = bf16[1,1,64,64,64]{4,3,2,1,0:T(8,128)(2,1)S(1)} copy-done((bf16[1,1,64,64,64]{4,3,2,1,0:T(8,128)(2,1)S(1)}, bf16[1,1,64,64,64]{4,3,2,1,0:T(8,128)(2,1)}, u32[]{:S(2)}) %copy-start.7) | copy-done | bytes 524312
  17.8 1.2 %copy-done.8 = bf16[1,1,64,64,64]{4,3,2,1,0:T(8,128)(2,1)S(1)} copy-done((bf16[1,1,64,64,64]{4,3,2,1,0:T(8,128)(2,1)S(1)}, bf16[1,1,64,64,64]{4,3,2,1,0:T(8,128)(2,1)}, u32[]{:S(2)}) %copy-start.8) | copy-done | bytes 524312
  19.0 9.4 %shard_map.174 = (s32[24,128]{1,0:T(8,128)S(1)}, bf16[7,32,64,128]{3,2,1,0:T(8,128)(2,1)}, bf16[6,16,64,128]{3,2,1,0:T(8,128)(2,1)S(1)}) custom-call(s32[3,128]{1,0:T(4,128)S(1)} %bitcast.42, s32[1,128]{1,0:T(1,128)S(1)} %bitcast.49, s32[2,64]{1,0:T(2,128)S(1)} %bitcast.50, s32[3,64]{1,0:T(4,128)S(1)} %bitcast.47, s32[1,64]{1,0:T(1,128)S(1)} %bitcast.52, ...), custom_call_target="tpu_custom_call" | custom-call | flops 4000000 | bytes 1000000 | tf_op jit(solution)/shard_map/pallas_call | solution.py:379
  28.4 1.6 %shard_map.173.known = f32[4,64,128]{2,1,0:T(8,128)S(1)} custom-call(f32[4,64,128]{2,1,0:T(8,128)S(1)} %bitcast.41, f32[4,64,128]{2,1,0:T(8,128)S(1)} %get-tuple-element.17.f0, bf16[64,64,128]{2,1,0:T(8,128)(2,1)S(1)} %bitcast.32, bf16[3,64,64,128]{3,2,1,0:T(8,128)(2,1)S(1)} %bitcast.26, s32[3,128]{1,0:T(4,128)S(1)} %bitcast.43), custom_call_target="tpu_custom_call" | custom-call | flops 8000000 | bytes 2000000 | tf_op jit(solution)/shard_map/pallas_call | solution.py:379
  30.0 0.4 copy-done
  30.5 3.2 %shard_map.175 = (f32[4,64,128]{2,1,0:T(8,128)S(1)}, f32[4,32,128]{2,1,0:T(8,128)S(1)}, f32[4,32,128]{2,1,0:T(8,128)S(1)}, f32[72,128]{1,0:T(8,128)S(1)}) custom-call(f32[4,64,128]{2,1,0:T(8,128)S(1)} %shard_map.173.known, f32[136,128]{1,0:T(8,128)S(1)} %collective-permute-done.up.up_place, f32[136,128]{1,0:T(8,128)S(1)} %collective-permute-done.1.beside.beside_place, ...), custom_call_target="tpu_custom_call" | custom-call | flops 14000000 | bytes 3500000 | tf_op jit(solution)/shard_map/pallas_call | solution.py:379
  33.7 1.3 %collective-permute-start.2 = (f32[72,128]{1,0:T(8,128)S(1)}, f32[72,128]{1,0:T(8,128)S(1)}, u32[]{:S(2)}, u32[]{:S(2)}) collective-permute-start(f32[72,128]{1,0:T(8,128)S(1)} %get-tuple-element.24), channel_id=1, source_target_pairs={{0,64},{64,128},{128,192},{192,0},{1,65},{65,129},{129,193},{193,1... | collective-permute-start | bytes 110600 | tf_op jit(solution)/shard_map/ppermute | solution.py:394
  35.0 1.4 %collective-permute-start.3 = (f32[72,128]{1,0:T(8,128)S(1)}, f32[72,128]{1,0:T(8,128)S(1)}, u32[]{:S(2)}, u32[]{:S(2)}) collective-permute-start(f32[72,128]{1,0:T(8,128)S(1)} %get-tuple-element.24), channel_id=1, source_target_pairs={{0,1},{1,2},{2,3},{3,4},{4,5},{5,6},{6,7},{7,8},{8,9},{9,10},{10,1... | collective-permute-start | bytes 110600 | tf_op jit(solution)/shard_map/ppermute | solution.py:394
  36.4 0.9 shard_map.176.known
  37.3 0.5 collective-permute-done.2.up.up_place
  37.7 6.1 %collective-permute-done.3.beside.beside_place = f32[72,128]{1,0:T(8,128)S(1)} collective-permute-done((f32[72,128]{1,0:T(8,128)S(1)}, f32[72,128]{1,0:T(8,128)S(1)}, u32[]{:S(2)}, u32[]{:S(2)}) %collective-permute-start.3) | collective-permute-done | bytes 36896 | tf_op jit(solution)/shard_map/ppermute | solution.py:394
  43.8 1.9 %shard_map.177 = (f32[4,32,128]{2,1,0:T(8,128)S(1)}, f32[4,16,128]{2,1,0:T(8,128)S(1)}, f32[4,16,128]{2,1,0:T(8,128)S(1)}) custom-call(f32[4,32,128]{2,1,0:T(8,128)S(1)} %shard_map.176.known, f32[72,128]{1,0:T(8,128)S(1)} %collective-permute-done.2.up.up_place, f32[72,128]{1,0:T(8,128)S(1)} %collective-permute-done.3.beside.beside_place, ...), custom_call_target="tpu_custom_call" | custom-call | flops 8000000 | bytes 2000000 | tf_op jit(solution)/shard_map/pallas_call | solution.py:379
  45.6 0.6 collective-permute-start.4
  46.2 0.3 shard_map.178.known
  46.5 3.1 %collective-permute-done.4.up = f32[4,16,128]{2,1,0:T(8,128)S(1)} collective-permute-done((f32[4,16,128]{2,1,0:T(8,128)S(1)}, f32[4,16,128]{2,1,0:T(8,128)S(1)}, u32[]{:S(2)}, u32[]{:S(2)}) %collective-permute-start.4) | collective-permute-done | bytes 32800 | tf_op jit(solution)/shard_map/ppermute | solution.py:394
  49.6 3.2 %collective-permute-done.5.beside = f32[4,16,128]{2,1,0:T(8,128)S(1)} collective-permute-done((f32[4,16,128]{2,1,0:T(8,128)S(1)}, f32[4,16,128]{2,1,0:T(8,128)S(1)}, u32[]{:S(2)}, u32[]{:S(2)}) %collective-permute-start.5) | collective-permute-done | bytes 32800 | tf_op jit(solution)/shard_map/ppermute | solution.py:394
  52.9 0.9 shard_map.179.own
  53.7 1.6 %collective-permute-start.6 = (f32[4,16,128]{2,1,0:T(8,128)S(1)}, f32[4,16,128]{2,1,0:T(8,128)S(1)}, u32[]{:S(2)}, u32[]{:S(2)}) collective-permute-start(f32[4,16,128]{2,1,0:T(8,128)S(1)} %shard_map.179.own), channel_id=1, source_target_pairs={{0,64},{64,128},{128,192},{192,0},{1,65},{65,129},{129,193},{193,1... | collective-permute-start | bytes 98312 | tf_op jit(solution)/shard_map/ppermute | solution.py:394
  55.3 0.3 shard_map.180.known
  55.6 2.1 %collective-permute-done.6.up = f32[4,16,128]{2,1,0:T(8,128)S(1)} collective-permute-done((f32[4,16,128]{2,1,0:T(8,128)S(1)}, f32[4,16,128]{2,1,0:T(8,128)S(1)}, u32[]{:S(2)}, u32[]{:S(2)}) %collective-permute-start.6) | collective-permute-done | bytes 32800 | tf_op jit(solution)/shard_map/ppermute | solution.py:394
  57.7 4.2 %collective-permute-done.7.beside = f32[4,16,128]{2,1,0:T(8,128)S(1)} collective-permute-done((f32[4,16,128]{2,1,0:T(8,128)S(1)}, f32[4,16,128]{2,1,0:T(8,128)S(1)}, u32[]{:S(2)}, u32[]{:S(2)}) %collective-permute-start.7) | collective-permute-done | bytes 32800 | tf_op jit(solution)/shard_map/ppermute | solution.py:394
  62.0 0.9 shard_map.181.own
  62.8 1.6 %collective-permute-start.8 = (f32[4,16,128]{2,1,0:T(8,128)S(1)}, f32[4,16,128]{2,1,0:T(8,128)S(1)}, u32[]{:S(2)}, u32[]{:S(2)}) collective-permute-start(f32[4,16,128]{2,1,0:T(8,128)S(1)} %shard_map.181.own), channel_id=1, source_target_pairs={{0,64},{64,128},{128,192},{192,0},{1,65},{65,129},{129,193},{193,1... | collective-permute-start | bytes 98312 | tf_op jit(solution)/shard_map/ppermute | solution.py:394
  64.4 0.0 collective-permute-start.9
  64.4 0.3 shard_map.182.known
  64.7 2.1 %collective-permute-done.8.up = f32[4,16,128]{2,1,0:T(8,128)S(1)} collective-permute-done((f32[4,16,128]{2,1,0:T(8,128)S(1)}, f32[4,16,128]{2,1,0:T(8,128)S(1)}, u32[]{:S(2)}, u32[]{:S(2)}) %collective-permute-start.8) | collective-permute-done | bytes 32800 | tf_op jit(solution)/shard_map/ppermute | solution.py:394
  66.8 4.2 %collective-permute-done.9.beside = f32[4,16,128]{2,1,0:T(8,128)S(1)} collective-permute-done((f32[4,16,128]{2,1,0:T(8,128)S(1)}, f32[4,16,128]{2,1,0:T(8,128)S(1)}, u32[]{:S(2)}, u32[]{:S(2)}) %collective-permute-start.9) | collective-permute-done | bytes 32800 | tf_op jit(solution)/shard_map/ppermute | solution.py:394
  71.1 0.9 shard_map.183.own
  71.9 1.3 %collective-permute-start.10 = (f32[4,16,128]{2,1,0:T(8,128)S(1)}, f32[4,16,128]{2,1,0:T(8,128)S(1)}, u32[]{:S(2)}, u32[]{:S(2)}) collective-permute-start(f32[4,16,128]{2,1,0:T(8,128)S(1)} %shard_map.183.own), channel_id=1, source_target_pairs={{0,64},{64,128},{128,192},{192,0},{1,65},{65,129},{129,193},{193,1... | collective-permute-start | bytes 98312 | tf_op jit(solution)/shard_map/ppermute | solution.py:394
  73.2 0.3 shard_map.184.known
  73.5 2.4 %collective-permute-done.10.up = f32[4,16,128]{2,1,0:T(8,128)S(1)} collective-permute-done((f32[4,16,128]{2,1,0:T(8,128)S(1)}, f32[4,16,128]{2,1,0:T(8,128)S(1)}, u32[]{:S(2)}, u32[]{:S(2)}) %collective-permute-start.10) | collective-permute-done | bytes 32800 | tf_op jit(solution)/shard_map/ppermute | solution.py:394
  75.9 3.9 %collective-permute-done.11.beside = f32[4,16,128]{2,1,0:T(8,128)S(1)} collective-permute-done((f32[4,16,128]{2,1,0:T(8,128)S(1)}, f32[4,16,128]{2,1,0:T(8,128)S(1)}, u32[]{:S(2)}, u32[]{:S(2)}) %collective-permute-start.11) | collective-permute-done | bytes 32800 | tf_op jit(solution)/shard_map/ppermute | solution.py:394
  79.9 0.9 shard_map.185.own
  80.7 0.6 collective-permute-start.12
  81.3 0.3 shard_map.186.known
  81.6 3.1 %collective-permute-done.12.up = f32[4,16,128]{2,1,0:T(8,128)S(1)} collective-permute-done((f32[4,16,128]{2,1,0:T(8,128)S(1)}, f32[4,16,128]{2,1,0:T(8,128)S(1)}, u32[]{:S(2)}, u32[]{:S(2)}) %collective-permute-start.12) | collective-permute-done | bytes 32800 | tf_op jit(solution)/shard_map/ppermute | solution.py:394
  84.7 3.2 %collective-permute-done.13.beside = f32[4,16,128]{2,1,0:T(8,128)S(1)} collective-permute-done((f32[4,16,128]{2,1,0:T(8,128)S(1)}, f32[4,16,128]{2,1,0:T(8,128)S(1)}, u32[]{:S(2)}, u32[]{:S(2)}) %collective-permute-start.13) | collective-permute-done | bytes 32800 | tf_op jit(solution)/shard_map/ppermute | solution.py:394
  88.0 0.9 shard_map.187.fix
  88.8 0.1 collective-permute-start.14
  88.9 1.0 shard_map.188.known
  89.9 5.7 %collective-permute-done.14.beside = f32[4,16,128]{2,1,0:T(8,128)S(1)} collective-permute-done((f32[4,16,128]{2,1,0:T(8,128)S(1)}, f32[4,16,128]{2,1,0:T(8,128)S(1)}, u32[]{:S(2)}, u32[]{:S(2)}) %collective-permute-start.14) | collective-permute-done | bytes 32800 | tf_op jit(solution)/shard_map/ppermute | solution.py:394
  95.6 1.6 %shard_map.189.fix = f32[4,32,128]{2,1,0:T(8,128)S(1)} custom-call(f32[4,32,128]{2,1,0:T(8,128)S(1)} %shard_map.188.known, f32[4,32,128]{2,1,0:T(8,128)S(1)} %get-tuple-element.23.f0, f32[4,16,128]{2,1,0:T(8,128)S(1)} %shard_map.187.fix, f32[4,16,128]{2,1,0:T(8,128)S(1)} %collective-permute-done.12.up, f32[4,16,128]{2,1,0:T(8,128)S(1)} %collective-permute-done.14.beside, ...), custom_call_target="tpu_custom_call" | custom-call | flops 6000000 | bytes 1500000 | tf_op jit(solution)/shard_map/pallas_call | solution.py:379
  97.2 0.0 copy-start.4
  97.2 1.6 %collective-permute-start.15 = (f32[4,32,128]{2,1,0:T(8,128)S(1)}, f32[4,32,128]{2,1,0:T(8,128)S(1)}, u32[]{:S(2)}, u32[]{:S(2)}) collective-permute-start(f32[4,32,128]{2,1,0:T(8,128)S(1)} %shard_map.189.fix), channel_id=1, source_target_pairs={{0,64},{64,128},{128,192},{192,0},{1,65},{65,129},{129,193},{193,1... | collective-permute-start | bytes 196616 | tf_op jit(solution)/shard_map/ppermute | solution.py:394
  98.8 1.7 %shard_map.190.known = f32[4,64,128]{2,1,0:T(8,128)S(1)} custom-call(f32[4,64,128]{2,1,0:T(8,128)S(1)} %get-tuple-element.21.r0, f32[4,32,128]{2,1,0:T(8,128)S(1)} %shard_map.189.fix, bf16[64,64,128]{2,1,0:T(8,128)(2,1)S(1)} %bitcast.33, bf16[3,64,64,128]{3,2,1,0:T(8,128)(2,1)S(1)} %bitcast.28, s32[3,128]{1,0:T(4,128)S(1)} %bitcast.44, ...), custom_call_target="tpu_custom_call" | custom-call | flops 8000000 | bytes 2000000 | tf_op jit(solution)/shard_map/pallas_call | solution.py:379
  100.5 1.1 collective-permute-done.15.up
  101.5 4.2 %collective-permute-done.16.beside = f32[4,32,128]{2,1,0:T(8,128)S(1)} collective-permute-done((f32[4,32,128]{2,1,0:T(8,128)S(1)}, f32[4,32,128]{2,1,0:T(8,128)S(1)}, u32[]{:S(2)}, u32[]{:S(2)}) %collective-permute-start.16) | collective-permute-done | bytes 65568 | tf_op jit(solution)/shard_map/ppermute | solution.py:394
  105.8 3.4 %shard_map.191 = f32[4,64,128]{2,1,0:T(8,128)} custom-call(f32[4,64,128]{2,1,0:T(8,128)S(1)} %shard_map.190.known, f32[4,64,128]{2,1,0:T(8,128)S(1)} %get-tuple-element.17.f0, f32[4,32,128]{2,1,0:T(8,128)S(1)} %shard_map.189.fix, f32[4,32,128]{2,1,0:T(8,128)S(1)} %collective-permute-done.15.up, f32[4,32,128]{2,1,0:T(8,128)S(1)} %collective-permute-done.16.beside, ...), custom_call_target="tpu_custom_call" | custom-call | flops 12000000 | bytes 3000000 | tf_op jit(solution)/shard_map/pallas_call | solution.py:379
  (34 shorter events, 0.1 us)
Async XLA Ops:
  0.0 1.2 %copy-start.3 = (bf16[1,1,64,64,128]{4,3,2,1,0:T(8,128)(2,1)S(1)}, bf16[1,1,64,64,128]{4,3,2,1,0:T(8,128)(2,1)}, u32[]{:S(2)}) copy-start(bf16[1,1,64,64,128]{4,3,2,1,0:T(8,128)(2,1)} %param.20) | copy-start | bytes 3145732
  1.2 0.9 copy-start.9
  2.1 0.7 copy-start.11
  2.8 7.5 %copy-start.16 = (bf16[1,1,2,64,64,32]{4,5,3,2,1,0:T(8,128)(2,1)S(1)}, bf16[1,1,2,64,64,32]{4,5,3,2,1,0:T(8,128)(2,1)}, u32[]{:S(2)}) copy-start(bf16[1,1,2,64,64,32]{4,5,3,2,1,0:T(8,128)(2,1)} %param.32) | copy-start | bytes 1572868
  3.9 26.1 %collective-permute-start = (f32[136,128]{1,0:T(8,128)S(1)}, f32[136,128]{1,0:T(8,128)S(1)}, u32[]{:S(2)}, u32[]{:S(2)}) collective-permute-start(f32[136,128]{1,0:T(8,128)S(1)} %get-tuple-element.18.sent), channel_id=1, source_target_pairs={{0,64},{64,128},{128,192},{192,0},{1,65},{65,129},{129,193},{193,1... | collective-permute-start | bytes 208904 | tf_op jit(solution)/shard_map/ppermute | solution.py:394
  5.5 24.6 %collective-permute-start.1 = (f32[136,128]{1,0:T(8,128)S(1)}, f32[136,128]{1,0:T(8,128)S(1)}, u32[]{:S(2)}, u32[]{:S(2)}) collective-permute-start(f32[136,128]{1,0:T(8,128)S(1)} %get-tuple-element.18.sent), channel_id=1, source_target_pairs={{0,1},{1,2},{2,3},{3,4},{4,5},{5,6},{6,7},{7,8},{8,9},{9,10},{10,1... | collective-permute-start | bytes 208904 | tf_op jit(solution)/shard_map/ppermute | solution.py:394
  10.3 2.6 %copy-start.17 = (s32[1,1,3,32]{3,1,2,0:T(1,128)S(1)}, s32[1,1,3,32]{3,1,2,0:T(1,128)}, u32[]{:S(2)}) copy-start(s32[1,1,3,32]{3,1,2,0:T(1,128)} %param.35) | copy-start | bytes 1156
  10.3 2.6 %copy-start.18 = (s32[1,1,3,64]{3,1,2,0:T(1,128)S(1)}, s32[1,1,3,64]{3,1,2,0:T(1,128)}, u32[]{:S(2)}) copy-start(s32[1,1,3,64]{3,1,2,0:T(1,128)} %param.29) | copy-start | bytes 2308
  10.3 2.7 %copy-start.12 = (s32[1,1,128]{2,1,0:T(1,128)S(1)}, s32[1,1,128]{2,1,0:T(1,128)}, u32[]{:S(2)}) copy-start(s32[1,1,128]{2,1,0:T(1,128)} %param.23) | copy-start | bytes 1540
  10.4 2.7 %copy-start.13 = (s32[1,1,2,64]{3,2,1,0:T(2,128)S(1)}, s32[1,1,2,64]{3,2,1,0:T(2,128)}, u32[]{:S(2)}) copy-start(s32[1,1,2,64]{3,2,1,0:T(2,128)} %param.24) | copy-start | bytes 1540
  10.4 2.7 %copy-start.14 = (s32[1,1,2,32]{3,2,1,0:T(2,128)S(1)}, s32[1,1,2,32]{3,2,1,0:T(2,128)}, u32[]{:S(2)}) copy-start(s32[1,1,2,32]{3,2,1,0:T(2,128)} %param.31) | copy-start | bytes 772
  10.4 2.7 %copy-start.15 = (s32[1,1,64]{2,1,0:T(1,128)S(1)}, s32[1,1,64]{2,1,0:T(1,128)}, u32[]{:S(2)}) copy-start(s32[1,1,64]{2,1,0:T(1,128)} %param.30) | copy-start | bytes 772
  13.0 1.9 %copy-start.5 = (bf16[1,1,3,64,64,64]{5,4,3,2,1,0:T(8,128)(2,1)S(1)}, bf16[1,1,3,64,64,64]{5,4,3,2,1,0:T(8,128)(2,1)}, u32[]{:S(2)}) copy-start(bf16[1,1,3,64,64,64]{5,4,3,2,1,0:T(8,128)(2,1)} %param.28) | copy-start | bytes 4718596
  14.9 1.6 %copy-start.6 = (bf16[1,1,2,64,64,64]{5,4,3,2,1,0:T(8,128)(2,1)S(1)}, bf16[1,1,2,64,64,64]{5,4,3,2,1,0:T(8,128)(2,1)}, u32[]{:S(2)}) copy-start(bf16[1,1,2,64,64,64]{5,4,3,2,1,0:T(8,128)(2,1)} %param.25) | copy-start | bytes 3145732
  16.5 1.2 %copy-start.7 = (bf16[1,1,64,64,64]{4,3,2,1,0:T(8,128)(2,1)S(1)}, bf16[1,1,64,64,64]{4,3,2,1,0:T(8,128)(2,1)}, u32[]{:S(2)}) copy-start(bf16[1,1,64,64,64]{4,3,2,1,0:T(8,128)(2,1)} %param.26) | copy-start | bytes 1572868
  17.8 1.2 %copy-start.8 = (bf16[1,1,64,64,64]{4,3,2,1,0:T(8,128)(2,1)S(1)}, bf16[1,1,64,64,64]{4,3,2,1,0:T(8,128)(2,1)}, u32[]{:S(2)}) copy-start(bf16[1,1,64,64,64]{4,3,2,1,0:T(8,128)(2,1)} %param.27) | copy-start | bytes 1572868
  19.0 9.5 %copy-start.1 = (bf16[1,1,3,64,64,128]{5,4,3,2,1,0:T(8,128)(2,1)S(1)}, bf16[1,1,3,64,64,128]{5,4,3,2,1,0:T(8,128)(2,1)}, u32[]{:S(2)}) copy-start(bf16[1,1,3,64,64,128]{5,4,3,2,1,0:T(8,128)(2,1)} %param.21) | copy-start | bytes 9437188
  19.0 9.5 %copy-start.2 = (bf16[1,1,64,64,128]{4,3,2,1,0:T(8,128)(2,1)S(1)}, bf16[1,1,64,64,128]{4,3,2,1,0:T(8,128)(2,1)}, u32[]{:S(2)}) copy-start(bf16[1,1,64,64,128]{4,3,2,1,0:T(8,128)(2,1)} %param.19) | copy-start | bytes 3145732
  19.0 9.5 %copy-start.10 = (f32[1,1,4,64,128]{4,3,2,1,0:T(8,128)S(1)}, f32[1,1,4,64,128]{4,3,2,1,0:T(8,128)}, u32[]{:S(2)}) copy-start(f32[1,1,4,64,128]{4,3,2,1,0:T(8,128)} %param.18) | copy-start | bytes 393220
  28.4 2.0 %copy-start = (bf16[7,32,64,128]{3,2,1,0:T(8,128)(2,1)S(1)}, bf16[7,32,64,128]{3,2,1,0:T(8,128)(2,1)}, u32[]{:S(2)}) copy-start(bf16[7,32,64,128]{3,2,1,0:T(8,128)(2,1)} %get-tuple-element.20.middle) | copy-start | bytes 11010052
  33.7 4.0 %collective-permute-start.2 = (f32[72,128]{1,0:T(8,128)S(1)}, f32[72,128]{1,0:T(8,128)S(1)}, u32[]{:S(2)}, u32[]{:S(2)}) collective-permute-start(f32[72,128]{1,0:T(8,128)S(1)} %get-tuple-element.24), channel_id=1, source_target_pairs={{0,64},{64,128},{128,192},{192,0},{1,65},{65,129},{129,193},{193,1... | collective-permute-start | bytes 110600 | tf_op jit(solution)/shard_map/ppermute | solution.py:394
  35.0 8.8 %collective-permute-start.3 = (f32[72,128]{1,0:T(8,128)S(1)}, f32[72,128]{1,0:T(8,128)S(1)}, u32[]{:S(2)}, u32[]{:S(2)}) collective-permute-start(f32[72,128]{1,0:T(8,128)S(1)} %get-tuple-element.24), channel_id=1, source_target_pairs={{0,1},{1,2},{2,3},{3,4},{4,5},{5,6},{6,7},{7,8},{8,9},{9,10},{10,1... | collective-permute-start | bytes 110600 | tf_op jit(solution)/shard_map/ppermute | solution.py:394
  45.6 4.0 %collective-permute-start.4 = (f32[4,16,128]{2,1,0:T(8,128)S(1)}, f32[4,16,128]{2,1,0:T(8,128)S(1)}, u32[]{:S(2)}, u32[]{:S(2)}) collective-permute-start(f32[4,16,128]{2,1,0:T(8,128)S(1)} %get-tuple-element.28.own), channel_id=1, source_target_pairs={{0,64},{64,128},{128,192},{192,0},{1,65},{65,129},{129,193},{193,1... | collective-permute-start | bytes 98312 | tf_op jit(solution)/shard_map/ppermute | solution.py:394
  46.2 6.7 %collective-permute-start.5 = (f32[4,16,128]{2,1,0:T(8,128)S(1)}, f32[4,16,128]{2,1,0:T(8,128)S(1)}, u32[]{:S(2)}, u32[]{:S(2)}) collective-permute-start(f32[4,16,128]{2,1,0:T(8,128)S(1)} %get-tuple-element.28.own), channel_id=1, source_target_pairs={{0,1},{1,2},{2,3},{3,4},{4,5},{5,6},{6,7},{7,8},{8,9},{9,10},{10,1... | collective-permute-start | bytes 98312 | tf_op jit(solution)/shard_map/ppermute | solution.py:394
  53.7 4.0 %collective-permute-start.6 = (f32[4,16,128]{2,1,0:T(8,128)S(1)}, f32[4,16,128]{2,1,0:T(8,128)S(1)}, u32[]{:S(2)}, u32[]{:S(2)}) collective-permute-start(f32[4,16,128]{2,1,0:T(8,128)S(1)} %shard_map.179.own), channel_id=1, source_target_pairs={{0,64},{64,128},{128,192},{192,0},{1,65},{65,129},{129,193},{193,1... | collective-permute-start | bytes 98312 | tf_op jit(solution)/shard_map/ppermute | solution.py:394
  55.3 6.7 %collective-permute-start.7 = (f32[4,16,128]{2,1,0:T(8,128)S(1)}, f32[4,16,128]{2,1,0:T(8,128)S(1)}, u32[]{:S(2)}, u32[]{:S(2)}) collective-permute-start(f32[4,16,128]{2,1,0:T(8,128)S(1)} %shard_map.179.own), channel_id=1, source_target_pairs={{0,1},{1,2},{2,3},{3,4},{4,5},{5,6},{6,7},{7,8},{8,9},{9,10},{10,1... | collective-permute-start | bytes 98312 | tf_op jit(solution)/shard_map/ppermute | solution.py:394
  62.8 4.0 %collective-permute-start.8 = (f32[4,16,128]{2,1,0:T(8,128)S(1)}, f32[4,16,128]{2,1,0:T(8,128)S(1)}, u32[]{:S(2)}, u32[]{:S(2)}) collective-permute-start(f32[4,16,128]{2,1,0:T(8,128)S(1)} %shard_map.181.own), channel_id=1, source_target_pairs={{0,64},{64,128},{128,192},{192,0},{1,65},{65,129},{129,193},{193,1... | collective-permute-start | bytes 98312 | tf_op jit(solution)/shard_map/ppermute | solution.py:394
  64.4 6.7 %collective-permute-start.9 = (f32[4,16,128]{2,1,0:T(8,128)S(1)}, f32[4,16,128]{2,1,0:T(8,128)S(1)}, u32[]{:S(2)}, u32[]{:S(2)}) collective-permute-start(f32[4,16,128]{2,1,0:T(8,128)S(1)} %shard_map.181.own), channel_id=1, source_target_pairs={{0,1},{1,2},{2,3},{3,4},{4,5},{5,6},{6,7},{7,8},{8,9},{9,10},{10,1... | collective-permute-start | bytes 98312 | tf_op jit(solution)/shard_map/ppermute | solution.py:394
  71.9 4.0 %collective-permute-start.10 = (f32[4,16,128]{2,1,0:T(8,128)S(1)}, f32[4,16,128]{2,1,0:T(8,128)S(1)}, u32[]{:S(2)}, u32[]{:S(2)}) collective-permute-start(f32[4,16,128]{2,1,0:T(8,128)S(1)} %shard_map.183.own), channel_id=1, source_target_pairs={{0,64},{64,128},{128,192},{192,0},{1,65},{65,129},{129,193},{193,1... | collective-permute-start | bytes 98312 | tf_op jit(solution)/shard_map/ppermute | solution.py:394
  73.2 6.7 %collective-permute-start.11 = (f32[4,16,128]{2,1,0:T(8,128)S(1)}, f32[4,16,128]{2,1,0:T(8,128)S(1)}, u32[]{:S(2)}, u32[]{:S(2)}) collective-permute-start(f32[4,16,128]{2,1,0:T(8,128)S(1)} %shard_map.183.own), channel_id=1, source_target_pairs={{0,1},{1,2},{2,3},{3,4},{4,5},{5,6},{6,7},{7,8},{8,9},{9,10},{10,1... | collective-permute-start | bytes 98312 | tf_op jit(solution)/shard_map/ppermute | solution.py:394
  80.7 4.0 %collective-permute-start.12 = (f32[4,16,128]{2,1,0:T(8,128)S(1)}, f32[4,16,128]{2,1,0:T(8,128)S(1)}, u32[]{:S(2)}, u32[]{:S(2)}) collective-permute-start(f32[4,16,128]{2,1,0:T(8,128)S(1)} %shard_map.185.own), channel_id=1, source_target_pairs={{0,64},{64,128},{128,192},{192,0},{1,65},{65,129},{129,193},{193,1... | collective-permute-start | bytes 98312 | tf_op jit(solution)/shard_map/ppermute | solution.py:394
  81.3 6.7 %collective-permute-start.13 = (f32[4,16,128]{2,1,0:T(8,128)S(1)}, f32[4,16,128]{2,1,0:T(8,128)S(1)}, u32[]{:S(2)}, u32[]{:S(2)}) collective-permute-start(f32[4,16,128]{2,1,0:T(8,128)S(1)} %shard_map.185.own), channel_id=1, source_target_pairs={{0,1},{1,2},{2,3},{3,4},{4,5},{5,6},{6,7},{7,8},{8,9},{9,10},{10,1... | collective-permute-start | bytes 98312 | tf_op jit(solution)/shard_map/ppermute | solution.py:394
  88.8 6.7 %collective-permute-start.14 = (f32[4,16,128]{2,1,0:T(8,128)S(1)}, f32[4,16,128]{2,1,0:T(8,128)S(1)}, u32[]{:S(2)}, u32[]{:S(2)}) collective-permute-start(f32[4,16,128]{2,1,0:T(8,128)S(1)} %shard_map.187.fix), channel_id=1, source_target_pairs={{0,1},{1,2},{2,3},{3,4},{4,5},{5,6},{6,7},{7,8},{8,9},{9,10},{10,1... | collective-permute-start | bytes 98312 | tf_op jit(solution)/shard_map/ppermute | solution.py:394
  97.2 8.6 %copy-start.4 = (bf16[1,1,64,64,128]{4,3,2,1,0:T(8,128)(2,1)S(1)}, bf16[1,1,64,64,128]{4,3,2,1,0:T(8,128)(2,1)}, u32[]{:S(2)}) copy-start(bf16[1,1,64,64,128]{4,3,2,1,0:T(8,128)(2,1)} %param.20) | copy-start | bytes 3145732
  97.2 4.3 %collective-permute-start.15 = (f32[4,32,128]{2,1,0:T(8,128)S(1)}, f32[4,32,128]{2,1,0:T(8,128)S(1)}, u32[]{:S(2)}, u32[]{:S(2)}) collective-permute-start(f32[4,32,128]{2,1,0:T(8,128)S(1)} %shard_map.189.fix), channel_id=1, source_target_pairs={{0,64},{64,128},{128,192},{192,0},{1,65},{65,129},{129,193},{193,1... | collective-permute-start | bytes 196616 | tf_op jit(solution)/shard_map/ppermute | solution.py:394
  98.8 7.0 %collective-permute-start.16 = (f32[4,32,128]{2,1,0:T(8,128)S(1)}, f32[4,32,128]{2,1,0:T(8,128)S(1)}, u32[]{:S(2)}, u32[]{:S(2)}) collective-permute-start(f32[4,32,128]{2,1,0:T(8,128)S(1)} %shard_map.189.fix), channel_id=1, source_target_pairs={{0,1},{1,2},{2,3},{3,4},{4,5},{5,6},{6,7},{7,8},{8,9},{9,10},{10,1... | collective-permute-start | bytes 196616 | tf_op jit(solution)/shard_map/ppermute | solution.py:394

commit v2 on v1

v2 whole, which is shorter than its diff:
```python
import functools

import jax
import jax.numpy as jnp
from jax import lax
from jax.experimental import pallas as pl
from jax.experimental.pallas import tpu as pltpu
from jax.sharding import PartitionSpec as P

SWEEPS = 3
S = 4
B = 64
LANES = 128


F_LINK, F_PICK, F_COARSE, F_FINE = 0, 3, 5, 6
M_LINK, M_PICK, M_COARSE, M_FINE = 7, 10, 12, 13
C_LINK, M_POS, F_POS, TABLE = 14, 24, 32, 40


def lane_index():
    return lax.broadcasted_iota(jnp.int32, (1, LANES), 1)


def take_lanes(x, index):
    rows = x.reshape(-1, LANES)
    index = jnp.broadcast_to(index, rows.shape)
    return jnp.take_along_axis(rows, index, axis=1, mode="promise_in_bounds").reshape(x.shape)


def expand(packed, index, out, scale=None):
    rows = packed.shape[1]
    r = B // rows
    for h in range(r):
        values = take_lanes(packed, index + h * (LANES // r))
        if scale is not None:
            values = values * scale
        out[:, h * rows : (h + 1) * rows, :] = values


def pack(wide, r):
    rows = B // r
    group = lane_index() // (LANES // r)
    result = wide[:, :rows, :]
    for h in range(1, r):
        result = jnp.where(group == h, wide[:, h * rows : (h + 1) * rows, :], result)
    return result


def fold(parts):
    row = lax.broadcasted_iota(jnp.int32, (8, LANES), 0)
    high = row >= 4
    mid = (row & 2) > 0
    low = (row & 1) > 0
    level = []
    for i in range(4):
        a, b = parts[i], parts[i + 4]
        level.append(jnp.where(high, b, a) + pltpu.roll(jnp.where(high, a, b), 4, 0))
    pairs = []
    for i in range(2):
        a, b = level[i], level[i + 2]
        pairs.append(jnp.where(mid, b + pltpu.roll(b, 2, 0), a + pltpu.roll(a, 6, 0)))
    a, b = pairs
    return jnp.where(low, b + pltpu.roll(b, 1, 0), a + pltpu.roll(a, 7, 0))


def products(blocks, fields, rows, emit):
    def body(step, carry):
        base = pl.multiple_of(step * 8, 8)
        parts = [[None] * 8 for _ in range(S)]
        for block, field in zip(blocks, fields):
            for i in range(8):
                matrix = block[base + i].astype(jnp.float32)
                for s in range(S):
                    part = jnp.sum((matrix * field[s]).reshape(8, 8, LANES), axis=0)
                    parts[s][i] = part if parts[s][i] is None else parts[s][i] + part
        for s in range(S):
            emit(s, pl.ds(base, 8), fold(parts[s]))
        return carry

    lax.fori_loop(0, rows // 8, body, 0)


def positions(order, n):
    padded = order if n == LANES else jnp.where(lane_index() < n, order, -1)
    hit = padded == lax.broadcasted_iota(jnp.int32, (LANES, LANES), 0)
    place = lax.broadcasted_iota(jnp.int32, (8, LANES), 1).astype(jnp.float32)
    return lax.dot_general(
        place.astype(jnp.bfloat16),
        hit.astype(jnp.float32).astype(jnp.bfloat16),
        (((1,), (1,)), ((), ())),
        preferred_element_type=jnp.float32,
    )


CHUNKS = 4
SPARE = 8


def copy_out(sent, longer):
    rows = sent.shape[0]
    longer[0:rows, :] = sent[...]
    longer[rows : rows + SPARE, :] = jnp.zeros((SPARE, LANES), jnp.float32)


def copy_field(field, longer):
    rows = S * field.shape[1]
    longer[0:rows, :] = field[...].reshape(rows, LANES)
    longer[rows : rows + SPARE, :] = jnp.zeros((SPARE, LANES), jnp.float32)


def spread(values, n):
    return jnp.concatenate([values] * (LANES // n), axis=1)


def pick(source, index):
    source = jnp.broadcast_to(source, (8, LANES))
    return take_lanes(source, jnp.broadcast_to(index, (8, LANES)))[0:1]


def fill_table(f_links, f_order, f_picks, m_links, m_order, m_picks, c_links, table):
    lane = lane_index()

    def put(place, values):
        table[place : place + 1, :] = values

    for k in range(3):
        put(F_LINK + k, f_links[k])
        put(M_LINK + k, spread(m_links[k], 64))
        put(C_LINK + k, spread(c_links[k], 32))
    order = f_order[...]
    wide_order = spread(m_order[...], 64)
    for k in range(2):
        put(F_PICK + k, pick(order, 64 + spread(f_picks[k : k + 1, :], 64)))
        put(M_PICK + k, pick(wide_order, 32 + spread(m_picks[k : k + 1, :], 32)))
    put(F_COARSE, pick(order, lane % 64))
    put(F_FINE, pick(order, 64 + lane % 64))
    put(M_COARSE, pick(wide_order, lane % 32))
    put(M_FINE, pick(wide_order, 32 + lane % 32))
    place = positions(wide_order, 64).astype(jnp.int32)
    table[M_POS:F_POS, :] = take_lanes(place, lane % 64)
    table[F_POS:TABLE, :] = positions(order, LANES).astype(jnp.int32)


def start_kernel(*refs):
    sources, (f0, sent, longer, table) = refs[:9], refs[9:13]
    held, semaphores = refs[13:22], refs[22]
    b, inverse = held[:2]
    rows = B // CHUNKS
    copies = [pltpu.make_async_copy(sources[k], held[k], semaphores.at[k]) for k in (2, 3, 4, 5, 6, 7, 8, 0)]
    parts = []
    for c in range(CHUNKS):
        part = pl.ds(c * rows, rows)
        parts.append(pltpu.make_async_copy(sources[1].at[part], inverse.at[part], semaphores.at[9 + c]))
    for copy in copies + parts:
        copy.start()
    for copy in copies[:7]:
        copy.wait()
    fill_table(*held[2:], table)
    mask = (row(table, F_POS) >= 64).astype(jnp.float32)
    copies[7].wait()
    for c in range(CHUNKS):
        parts[c].wait()

        def emit(s, at, tile):
            f0[s, pl.ds(pl.multiple_of(c * rows + at.start, 8), 8), :] = tile * mask

        products([inverse.at[pl.ds(c * rows, rows)]], [b], rows, emit)
    wide = take_lanes(f0[...], row(table, F_FINE))
    sent[0:128, :] = pack(wide, 2).reshape(128, LANES)
    sent[128:136, :] = table[F_POS:TABLE, :].astype(jnp.float32)
    copy_out(sent, longer)


def place_lanes(n, offset):
    shape = (n, LANES)
    source = lax.broadcasted_iota(jnp.int32, shape, 0)
    hit = lax.broadcasted_iota(jnp.int32, shape, 1) == source + offset
    return hit.astype(jnp.float32).astype(jnp.bfloat16)


def dot(a, b, contract):
    return lax.dot_general(a, b, (contract, ((), ())), preferred_element_type=jnp.float32)


def pack_halves(sources, out):
    low, high = place_lanes(64, 0), place_lanes(64, 64)

    def body(step, carry):
        base = pl.multiple_of(step * 8, 8)
        for slot, source in enumerate(sources):
            first = source[pl.ds(base, 8)].reshape(8 * B, 64)
            second = source[pl.ds(base + 32, 8)].reshape(8 * B, 64)
            both = dot(first, low, ((1,), (0,))) + dot(second, high, ((1,), (0,)))
            out[slot, pl.ds(base, 8)] = both.astype(jnp.bfloat16).reshape(8, B, LANES)
        return carry

    lax.fori_loop(0, 4, body, 0)


def pack_quarters(sources, out):
    unit = place_lanes(64, 0)[:, :64]

    def body(step, carry):
        for slot, source in enumerate(sources):
            for k in range(4):
                i = step * 4 + k
                points = jnp.concatenate([source[16 * q + i] for q in range(4)], axis=0)
                out[slot, i] = dot(unit, points, ((1,), (1,))).astype(jnp.bfloat16)
        return carry

    lax.fori_loop(0, 4, body, 0)


def select_fine(sources, table, out):
    source = lax.broadcasted_iota(jnp.int32, (LANES, LANES), 0)
    hit = source == jnp.broadcast_to(row(table, F_FINE), (LANES, LANES))
    first = lax.broadcasted_iota(jnp.int32, (LANES, LANES), 1) < 64
    low = jnp.where(hit & first, 1.0, 0.0).astype(jnp.bfloat16)
    high = jnp.where(hit & ~first, 1.0, 0.0).astype(jnp.bfloat16)

    def body(step, carry):
        base = pl.multiple_of(step * 8, 8)
        for slot, source in enumerate(sources):
            a = source[pl.ds(base, 8)].reshape(8 * B, LANES)
            b = source[pl.ds(base + 32, 8)].reshape(8 * B, LANES)
            both = dot(a, low, ((1,), (0,))) + dot(b, high, ((1,), (0,)))
            out[slot, pl.ds(base, 8)] = both.astype(jnp.bfloat16).reshape(8, B, LANES)
        return carry

    lax.fori_loop(0, 4, body, 0)


def select_middle(sources, table, out):
    source = lax.broadcasted_iota(jnp.int32, (LANES, LANES), 0)
    group = lax.broadcasted_iota(jnp.int32, (LANES, LANES), 1) // 32
    hit = source == jnp.broadcast_to(row(table, M_FINE), (LANES, LANES)) + 64 * (group // 2)
    low = jnp.where(hit & (group % 2 == 0), 1.0, 0.0).astype(jnp.bfloat16)
    high = jnp.where(hit & (group % 2 == 1), 1.0, 0.0).astype(jnp.bfloat16)

    def body(step, carry):
        base = pl.multiple_of(step * 8, 8)
        for slot, source in enumerate(sources):
            a = source[pl.ds(base, 8)].reshape(8 * B, LANES)
            b = source[pl.ds(base + 16, 8)].reshape(8 * B, LANES)
            both = dot(a, low, ((1,), (0,))) + dot(b, high, ((1,), (0,)))
            out[slot, pl.ds(base, 8)] = both.astype(jnp.bfloat16).reshape(8, B, LANES)
        return carry

    lax.fori_loop(0, 2, body, 0)


M_INVERSE, F_WEIGHT = 0, 1
M_DIAG, M_FACE = 0, 1
C_INVERSE, M_WEIGHT = 0, 1


def row(table, k):
    return table[k : k + 1, :]


def fine_local_kernel(
    b_hbm, f0_hbm, diag_hbm, faces_hbm, table_hbm, m_inverse_hbm, f_weights_hbm, out, first,
    b, f0, diag, face, table, m_inverse, f_weights, semaphores, own, linked,
):
    sources = [f0_hbm, table_hbm, diag_hbm, faces_hbm.at[0], b_hbm, m_inverse_hbm, f_weights_hbm]
    targets = [f0, table, diag, face, b, m_inverse, f_weights]
    copies = [pltpu.make_async_copy(x, y, semaphores.at[k]) for k, (x, y) in enumerate(zip(sources, targets))]
    for copy in copies:
        copy.start()
    for copy in copies[:5]:
        copy.wait()
    own[...] = -f0[...]
    linked[...] = take_lanes(f0[...], row(table, F_LINK))

    def emit(s, rows, tile):
        out[s, rows, :] = b[s, rows, :] + tile

    products([diag, face], [own, linked], B, emit)
    for copy in copies[5:]:
        copy.wait()
    pack_halves([m_inverse, f_weights.at[0], f_weights.at[1]], first)


def chosen(place, index, low, high):
    spot = take_lanes(jnp.broadcast_to(place, (8, LANES)), jnp.broadcast_to(index, (8, LANES)))[0:1]
    inside = (spot >= low) & (spot < high)
    return jnp.clip(spot - low, 0, high - low - 1), inside.astype(jnp.float32)


def gate_of(flow):
    return (flow[0] > 0).astype(jnp.float32)


def fine_flow_kernel(known, up, faces, table, flow, out, v):
    index, inside = chosen(up[128:136, :].astype(jnp.int32)[0:1], row(table, F_LINK + 1), 64, 128)
    expand(up[0:128, :].reshape(S, 32, LANES), index, v, inside * gate_of(flow))

    def emit(s, rows, tile):
        out[s, rows, :] = known[s, rows, :] + tile

    products([faces.at[1]], [v], B, emit)


def fine_down_kernel(
    known, beside, faces, table, first,
    r0, right, f0, sent, longer, v1, v2, wide,
):
    index, inside = chosen(beside[128:136, :].astype(jnp.int32)[0:1], row(table, F_LINK + 2), 64, 128)
    expand(beside[0:128, :].reshape(S, 32, LANES), index, v2, inside)

    def emit_residual(s, rows, tile):
        r0[s, rows, :] = known[s, rows, :] + tile

    products([faces.at[2]], [v2], B, emit_residual)
    residual = r0[...]
    v1[...] = take_lanes(residual, row(table, F_PICK))
    v2[...] = take_lanes(residual, row(table, F_PICK + 1))
    wide[...] = take_lanes(residual, row(table, F_COARSE))
    right[...] = pack(wide[...], 2)

    def emit_right(s, rows, tile):
        right[s, rows, :] += tile

    products([first.at[F_WEIGHT], first.at[F_WEIGHT + 1]], [v1, v2], 32, emit_right)
    expand(right[...], lane_index() % 64, wide)
    mask = (row(table, M_POS) >= 32).astype(jnp.float32)

    def emit_field(s, rows, tile):
        f0[s, rows, :] = tile * mask

    products([first.at[M_INVERSE]], [wide], 32, emit_field)
    expand(f0[...], row(table, M_FINE), wide)
    sent[0:64, :] = pack(wide[...], 4).reshape(64, LANES)
    sent[64:72, :] = table[M_POS:F_POS, :].astype(jnp.float32)
    copy_out(sent, longer)


def middle_local_kernel(
    b, f0, table, m_diag, m_faces, c_inverse, m_weights, out, middle, coarse, own, linked
):
    pack_halves([m_diag, m_faces.at[0], m_faces.at[1], m_faces.at[2]], middle)
    pack_quarters([c_inverse, m_weights.at[0], m_weights.at[1]], coarse)
    expand(-f0[...], lane_index() % 64, own)
    expand(f0[...], row(table, M_LINK), linked)

    def emit(s, rows, tile):
        out[s, rows, :] = b[s, rows, :] + tile

    products([middle.at[M_DIAG], middle.at[M_FACE]], [own, linked], 32, emit)


def middle_flow_kernel(known, up, middle, table, flow, out, v):
    index, inside = chosen(up[64:72, :].astype(jnp.int32)[0:1], row(table, M_LINK + 1), 32, 64)
    expand(up[0:64, :].reshape(S, 16, LANES), index, v, inside * gate_of(flow))

    def emit(s, rows, tile):
        out[s, rows, :] = known[s, rows, :] + tile

    products([middle.at[M_FACE + 1]], [v], 32, emit)


def middle_down_kernel(
    known, beside, middle, coarse, table, flow,
    r0, right, first, longer, v1, v2, wide,
):
    index, inside = chosen(beside[64:72, :].astype(jnp.int32)[0:1], row(table, M_LINK + 2), 32, 64)
    expand(beside[0:64, :].reshape(S, 16, LANES), index, v2, inside)

    def emit_residual(s, rows, tile):
        r0[s, rows, :] = known[s, rows, :] + tile

    products([middle.at[M_FACE + 2]], [v2], 32, emit_residual)
    residual = r0[...]
    expand(residual, row(table, M_PICK), v1)
    expand(residual, row(table, M_PICK + 1), v2)
    expand(residual, row(table, M_COARSE), wide)
    right[...] = pack(wide[...], 4)

    def emit_right(s, rows, tile):
        right[s, rows, :] += tile

    products([coarse.at[M_WEIGHT], coarse.at[M_WEIGHT + 1]], [v1, v2], 16, emit_right)
    expand(right[...], lane_index() % 32, wide)
    start = (flow[0] == 0).astype(jnp.float32)

    def emit_first(s, rows, tile):
        first[s, rows, :] = tile * start

    products([coarse.at[C_INVERSE]], [wide], 16, emit_first)
    copy_field(first, longer)


def coarse_first_kernel(right, own, c_faces, table, out, faces, wide):
    pack_quarters([c_faces.at[0], c_faces.at[1], c_faces.at[2]], faces)
    coarse_local_kernel(right, own, faces, table, out, wide)


def coarse_fine_kernel(right, own, faces, table, f_inverse, f_faces, out, chosen_fine, wide):
    select_fine([f_inverse, f_faces.at[1], f_faces.at[2]], table, chosen_fine)
    coarse_local_kernel(right, own, faces, table, out, wide)


def coarse_middle_kernel(right, own, faces, table, first, middle, out, chosen_middle, wide):
    sources = [first.at[M_INVERSE], middle.at[M_FACE + 1], middle.at[M_FACE + 2]]
    select_middle(sources, table, chosen_middle)
    coarse_local_kernel(right, own, faces, table, out, wide)


def coarse_local_kernel(right, own, faces, table, out, wide):
    expand(own[...], row(table, C_LINK), wide)

    def emit(s, rows, tile):
        out[s, rows, :] = right[s, rows, :] + tile

    products([faces.at[0]], [wide], 16, emit)


def coarse_flow_kernel(known, up, faces, table, flow, out, v):
    expand(up[...], row(table, C_LINK + 1), v, gate_of(flow))

    def emit(s, rows, tile):
        out[s, rows, :] = known[s, rows, :] + tile

    products([faces.at[1]], [v], 16, emit)


def coarse_step_kernel(step, known, own, beside, coarse, faces, table, flow, out, longer, v1, v2, total):
    expand(beside[0:64, :].reshape(S, 16, LANES), row(table, C_LINK + 2), v2)

    def emit_total(s, rows, tile):
        total[s, rows, :] = known[s, rows, :] + tile

    products([faces.at[2]], [v2], 16, emit_total)
    expand(total[...], lane_index() % 32, v1)
    sweep = jnp.broadcast_to(step - flow[0], (8, LANES))

    def emit(s, rows, tile):
        fresh = jnp.where(sweep >= 0, tile, 0.0)
        out[s, rows, :] = jnp.where(sweep < SWEEPS, fresh, own[s, rows, :])

    products([coarse.at[C_INVERSE]], [v1], 16, emit)
    copy_field(out, longer)


def middle_up_local_kernel(r0, f0, fix, up, up_place, middle, chosen_middle, table, flow, out, base, own, linked, known):
    place = row(table, M_POS)
    index, inside = chosen(place, lane_index() % 64, 0, 32)
    expand(fix[...], index, own, inside)
    base[...] = f0[...] + pack(own[...], 2)
    own[...] = -own[...]
    index, inside = chosen(place, row(table, M_LINK), 0, 32)
    expand(fix[...], index, linked, inside)

    def emit(s, rows, tile):
        known[s, rows, :] = r0[s, rows, :] + tile

    products([middle.at[M_DIAG], middle.at[M_FACE]], [own, linked], 32, emit)
    expand(known[...], row(table, M_FINE), own)
    link = pick(row(table, M_LINK + 1), row(table, M_FINE))
    index, inside = chosen(up_place[64:72, :].astype(jnp.int32)[0:1], link, 0, 32)
    expand(up[...], index, linked, inside * gate_of(flow))
    out[...] = pack(own[...], 4)

    def emit_flow(s, rows, tile):
        out[s, rows, :] += tile

    products([chosen_middle.at[1]], [linked], 16, emit_flow)


def middle_up_kernel(known, base, beside, beside_place, chosen_middle, table, out, longer, v1, v2, total, result):
    link = pick(row(table, M_LINK + 2), row(table, M_FINE))
    index, inside = chosen(beside_place[64:72, :].astype(jnp.int32)[0:1], link, 0, 32)
    expand(beside[...], index, v1, inside)

    def emit_total(s, rows, tile):
        total[s, rows, :] = known[s, rows, :] + tile

    products([chosen_middle.at[2]], [v1], 16, emit_total)
    expand(total[...], lane_index() % 32, v2)

    def emit(s, rows, tile):
        result[s, rows, :] = tile

    products([chosen_middle.at[0]], [v2], 16, emit)
    index, inside = chosen(row(table, M_POS), lane_index() % 64, 32, 64)
    expand(result[...], index, v1, inside)
    out[...] = base[...] + pack(v1[...], 2)
    copy_field(out, longer)


def fine_up_local_kernel(r0, f0, fix, diag, faces, table, out, base, own, linked, known):
    place = row(table, F_POS)
    index, inside = chosen(place, lane_index(), 0, 64)
    expand(fix[...], index, own, inside)
    base[...] = f0[...] + own[...]
    own[...] = -own[...]
    index, inside = chosen(place, row(table, F_LINK), 0, 64)
    expand(fix[...], index, linked, inside)

    def emit(s, rows, tile):
        known[s, rows, :] = r0[s, rows, :] + tile

    products([diag, faces.at[0]], [own, linked], B, emit)
    own[...] = take_lanes(known[...], row(table, F_FINE))
    out[...] = pack(own[...], 2)


def fine_up_flow_kernel(known, up, up_place, chosen_fine, table, flow, out, v):
    link = pick(row(table, F_LINK + 1), row(table, F_FINE))
    index, inside = chosen(up_place[128:136, :].astype(jnp.int32)[0:1], link, 0, 64)
    expand(up[...], index, v, inside * gate_of(flow))

    def emit(s, rows, tile):
        out[s, rows, :] = known[s, rows, :] + tile

    products([chosen_fine.at[1]], [v], 32, emit)


def fine_up_kernel(known, base, beside, beside_place, chosen_fine, table, out, v1, v2, total, result):
    link = pick(row(table, F_LINK + 2), row(table, F_FINE))
    index, inside = chosen(beside_place[128:136, :].astype(jnp.int32)[0:1], link, 0, 64)
    expand(beside[0:128, :].reshape(S, 32, LANES), index, v1, inside)

    def emit_total(s, rows, tile):
        total[s, rows, :] = known[s, rows, :] + tile

    products([chosen_fine.at[2]], [v1], 32, emit_total)
    expand(total[...], lane_index() % 64, v2)

    def emit(s, rows, tile):
        result[s, rows, :] = tile

    products([chosen_fine.at[0]], [v2], 32, emit)
    index, inside = chosen(row(table, F_POS), lane_index(), 64, 128)
    expand(result[...], index, v1, inside)
    out[...] = base[...] + v1[...]


WIDE = pltpu.VMEM((S, B, LANES), jnp.float32)


def f32(*shape):
    return jax.ShapeDtypeStruct(shape, jnp.float32)


def bf16(*shape):
    return jax.ShapeDtypeStruct(shape, jnp.bfloat16)


def call(kernel, operands, outs, scratch=(), work=1.0, flow=None, space=pltpu.VMEM, limit=40 * 1024):
    specs = [pl.BlockSpec(memory_space=space)] * len(operands)
    if flow is not None:
        specs.append(pl.BlockSpec(memory_space=pltpu.SMEM))
        operands = (*operands, flow)
    return pl.pallas_call(
        kernel,
        out_shape=outs,
        in_specs=specs,
        out_specs=jax.tree.map(lambda _: pl.BlockSpec(memory_space=pltpu.VMEM), outs),
        scratch_shapes=list(scratch),
        compiler_params=pltpu.CompilerParams(vmem_limit_bytes=limit * 1024),
        cost_estimate=pl.CostEstimate(
            flops=int(work * 4_000_000), bytes_accessed=int(work * 1_000_000), transcendentals=0
        ),
    )(*operands)


def from_behind(block, axis):
    size = lax.axis_size(axis)
    return lax.ppermute(block, axis, [(i, (i + 1) % size) for i in range(size)])


def own_part(array):
    return array[0, 0]


def shards(*arrays):
    (
        b, f_diag, f_inverse, f_faces, f_links, f_order, f_picks, f_weights,
        m_diag, m_inverse, m_faces, m_links, m_order, m_picks, m_weights,
        c_inverse, c_faces, c_links,
    ) = map(own_part, arrays)
    flow_size = lax.axis_size("flow")
    flow = lax.axis_index("flow").astype(jnp.int32).reshape(1)
    f_order = f_order.reshape(1, LANES)
    m_order = m_order.reshape(1, 64)
    f_links, m_links, c_links = (x.reshape(3, 1, -1) for x in (f_links, m_links, c_links))
    c_inverse, c_faces, m_weights = (jnp.swapaxes(x, -1, -2) for x in (c_inverse, c_faces, m_weights))

    f0, f_sent, f_longer, table = call(
        start_kernel,
        (b, f_inverse, f_links, f_order, f_picks, m_links, m_order, m_picks, c_links),
        (
            f32(S, B, LANES), f32(136, LANES), f32(136 + SPARE, LANES),
            jax.ShapeDtypeStruct((TABLE, LANES), jnp.int32),
        ),
        (
            WIDE,
            pltpu.VMEM((B, B, LANES), jnp.bfloat16),
            *[pltpu.VMEM(x.shape, jnp.int32) for x in (f_links, f_order, f_picks, m_links, m_order, m_picks, c_links)],
            pltpu.SemaphoreType.DMA((9 + CHUNKS,)),
        ),
        space=pltpu.HBM,
        limit=65000,
    )
    f_beside, f_up = from_behind(f_longer, "tile"), from_behind(f_sent, "flow")
    known, first = call(
        fine_local_kernel,
        (b, f0, f_diag, f_faces, table, m_inverse, f_weights),
        (f32(S, B, LANES), bf16(3, 32, B, LANES)),
        (
            WIDE,
            WIDE,
            pltpu.VMEM((B, B, LANES), jnp.bfloat16),
            pltpu.VMEM((B, B, LANES), jnp.bfloat16),
            pltpu.VMEM((TABLE, LANES), jnp.int32),
            pltpu.VMEM(m_inverse.shape, jnp.bfloat16),
            pltpu.VMEM(f_weights.shape, jnp.bfloat16),
            pltpu.SemaphoreType.DMA((7,)),
            WIDE,
            WIDE,
        ),
        3.0,
        space=pltpu.HBM,
        limit=56000,
    )
    known = call(fine_flow_kernel, (known, f_up, f_faces, table), f32(S, B, LANES), (WIDE,), 0.0, flow)
    f_r0, right, m_f0, m_sent, m_longer = call(
        fine_down_kernel,
        (known, f_beside, f_faces, table, first),
        (f32(S, B, LANES), f32(S, 32, LANES), f32(S, 32, LANES), f32(72, LANES), f32(72 + SPARE, LANES)),
        (WIDE, WIDE, WIDE),
        2.5,
    )
    m_beside, m_up = from_behind(m_longer, "tile"), from_behind(m_sent, "flow")
    known, middle, coarse = call(
        middle_local_kernel,
        (right, m_f0, table, m_diag, m_faces, c_inverse, m_weights),
        (f32(S, 32, LANES), bf16(4, 32, B, LANES), bf16(3, 16, B, LANES)),
        (WIDE, WIDE),
        2.0,
    )
    known = call(middle_flow_kernel, (known, m_up, middle, table), f32(S, 32, LANES), (WIDE,), 0.0, flow)
    m_r0, right, value, longer = call(
        middle_down_kernel,
        (known, m_beside, middle, coarse, table),
        (f32(S, 32, LANES), f32(S, 16, LANES), f32(S, 16, LANES), f32(64 + SPARE, LANES)),
        (WIDE, WIDE, WIDE),
        1.5,
        flow,
    )
    packed16 = pltpu.VMEM((S, 16, LANES), jnp.float32)
    packed32 = pltpu.VMEM((S, 32, LANES), jnp.float32)
    for step in range(1, SWEEPS + flow_size - 1):
        beside, up = from_behind(longer, "tile"), from_behind(value, "flow")
        if step == 1:
            known, faces = call(
                coarse_first_kernel,
                (right, value, c_faces, table),
                (f32(S, 16, LANES), bf16(3, 16, B, LANES)),
                (WIDE,),
            )
        elif step == 2:
            known, chosen_fine = call(
                coarse_fine_kernel,
                (right, value, faces, table, f_inverse, f_faces),
                (f32(S, 16, LANES), bf16(3, 32, B, LANES)),
                (WIDE,),
            )
        elif step == 3:
            known, chosen_middle = call(
                coarse_middle_kernel,
                (right, value, faces, table, first, middle),
                (f32(S, 16, LANES), bf16(3, 16, B, LANES)),
                (WIDE,),
            )
        else:
            known = call(coarse_local_kernel, (right, value, faces, table), f32(S, 16, LANES), (WIDE,), 0.25)
        known = call(coarse_flow_kernel, (known, up, faces, table), f32(S, 16, LANES), (WIDE,), 0.0, flow)
        value, longer = call(
            functools.partial(coarse_step_kernel, step),
            (known, value, beside, coarse, faces, table),
            (f32(S, 16, LANES), f32(64 + SPARE, LANES)),
            (WIDE, WIDE, packed16),
            0.5,
            flow,
        )
    beside = from_behind(value, "tile")
    known, base = call(
        middle_up_local_kernel,
        (m_r0, m_f0, value, up, m_up, middle, chosen_middle, table),
        (f32(S, 16, LANES), f32(S, 32, LANES)),
        (WIDE, WIDE, packed32),
        1.25,
        flow,
    )
    fix, longer = call(
        middle_up_kernel,
        (known, base, beside, m_beside, chosen_middle, table),
        (f32(S, 32, LANES), f32(128 + SPARE, LANES)),
        (WIDE, WIDE, packed16, packed16),
        0.5,
    )
    beside, up = from_behind(longer, "tile"), from_behind(fix, "flow")
    known, base = call(
        fine_up_local_kernel,
        (f_r0, f0, fix, f_diag, f_faces, table),
        (f32(S, 32, LANES), f32(S, B, LANES)),
        (WIDE, WIDE, WIDE),
        2.0,
    )
    known = call(fine_up_flow_kernel, (known, up, f_up, chosen_fine, table), f32(S, 32, LANES), (WIDE,), 0.0, flow)
    field = call(
        fine_up_kernel,
        (known, base, beside, f_beside, chosen_fine, table),
        f32(S, B, LANES),
        (WIDE, WIDE, packed32, packed32),
        1.0,
    )
    return field[None, None]


def solution(mesh):
    ranks = (5, 5, 5, 6, 4, 3, 4, 6, 5, 5, 6, 4, 3, 4, 6, 5, 6, 4)
    return jax.shard_map(
        shards,
        mesh=mesh,
        in_specs=tuple(P("flow", "tile", *[None] * (rank - 2)) for rank in ranks),
        out_specs=P("flow", "tile", None, None, None),
        check_vma=False,
    )
```

time: 110 us -> 80.8 us (0.73)
  the two profiles are of different devices: /device:TPU:2 before, /device:TPU:121 now
where the time goes in v2:
time: 80.8 us; the launch traced here: 80 us
  Pallas kernels  36.2 us (45%)
  starting transfers between devices  30.7 us (38%)
  waiting for transfers between devices  11.8 us (15%)
  local copies, waits for them, and re-layouts  1.06 us (1%)
    pallas_call x27, Pallas kernels, call(): pl.pallas_call(kernel, out_shape=outs, in_specs=specs, out_specs=jax.tree...  36.2 us
    ppermute x17, starting transfers between devices, from_behind(): return lax.ppermute(block, axis, [(i, (i + 1) % size) for i in range(size)])  30.7 us
    ppermute x17, waiting for transfers between devices, from_behind(): return lax.ppermute(block, axis, [(i, (i + 1) % size) for i in range(size)])  11.8 us
  transfers between devices with their start and end apart: 17, of which 6 were waited for; matrix products, arithmetic and copies ran while one was open for 0% of the time, Pallas kernels for 28%

profile of v2, /device:TPU:121, one launch (start us, length us, event | category | flops | bytes accessed | tf_op | source)
XLA Modules:
  0.0 80.0 jit_solution(14190755742118840462)
XLA Ops:
  0.0 2.8 %shard_map.172 = (f32[4,64,128]{2,1,0:T(8,128)}, f32[136,128]{1,0:T(8,128)}, f32[144,128]{1,0:T(8,128)}, s32[40,128]{1,0:T(8,128)}) custom-call(f32[4,64,128]{2,1,0:T(8,128)} %bitcast.42, bf16[64,64,128]{2,1,0:T(8,128)(2,1)} %bitcast.33, s32[3,1,128]{2,1,0:T(1,128)} %bitcast.44, s32[1,128]{1,0:T(1,128)} %bitcast.49, s32[2,64]{1,0:T(2,128)} %bitcast.47, ...), custom_call_target="tpu_custom_call" | custom-call | flops 4000000 | bytes 1000000 | tf_op jit(solution)/shard_map/pallas_call | solution.py:556
  2.8 3.1 %collective-permute-start.1 = (f32[144,128]{1,0:T(8,128)}, f32[144,128]{1,0:T(8,128)S(1)}, u32[]{:S(2)}, u32[]{:S(2)}) collective-permute-start(f32[144,128]{1,0:T(8,128)} %get-tuple-element.48), channel_id=1, source_target_pairs={{0,1},{1,2},{2,3},{3,4},{4,5},{5,6},{6,7},{7,8},{8,9},{9,10},{10,1... | collective-permute-start | bytes 221192 | tf_op jit(solution)/shard_map/ppermute | solution.py:571
  6.0 1.2 %collective-permute-start = (f32[136,128]{1,0:T(8,128)}, f32[136,128]{1,0:T(8,128)S(1)}, u32[]{:S(2)}, u32[]{:S(2)}) collective-permute-start(f32[136,128]{1,0:T(8,128)} %get-tuple-element.47), channel_id=1, source_target_pairs={{0,64},{64,128},{128,192},{192,0},{1,65},{65,129},{129,193},{193,1... | collective-permute-start | bytes 208904 | tf_op jit(solution)/shard_map/ppermute | solution.py:571
  7.2 6.2 %shard_map.173 = (f32[4,64,128]{2,1,0:T(8,128)}, bf16[3,32,64,128]{3,2,1,0:T(8,128)(2,1)}) custom-call(f32[4,64,128]{2,1,0:T(8,128)} %bitcast.43, f32[4,64,128]{2,1,0:T(8,128)} %get-tuple-element.44.f0_hbm.f0, bf16[64,64,128]{2,1,0:T(8,128)(2,1)} %bitcast.31, bf16[3,64,64,128]{3,2,1,0:T(8,128)(2,1)} %bitcast.26, ...), custom_call_target="tpu_custom_call" | custom-call | flops 12000000 | bytes 3000000 | tf_op jit(solution)/shard_map/pallas_call | solution.py:556
  13.4 0.0 collective-permute-done.up.up_place
  13.5 1.0 %copy-done.11 = f32[4,64,128]{2,1,0:T(8,128)S(1)} copy-done((f32[4,64,128]{2,1,0:T(8,128)S(1)}, f32[4,64,128]{2,1,0:T(8,128)}, u32[]{:S(2)}) %copy-start.11) | copy-done | bytes 131096
  14.5 1.0 %shard_map.174.known = f32[4,64,128]{2,1,0:T(8,128)S(1)} custom-call(f32[4,64,128]{2,1,0:T(8,128)S(1)} %copy-done.11, f32[136,128]{1,0:T(8,128)S(1)} %collective-permute-done.up.up_place, bf16[3,64,64,128]{3,2,1,0:T(8,128)(2,1)S(1)} %bitcast.27, s32[40,128]{1,0:T(8,128)S(1)} %copy-done.1, s32[1]{0:T(128)} %bitcast.13.flow), custom_call_target="tpu_custom_call" | custom-call | tf_op jit(solution)/shard_map/pallas_call | solution.py:556
  15.4 0.0 collective-permute-done.1.beside.beside_place
  15.5 0.0 copy-start.5
  15.5 0.0 copy-start.7
  15.5 0.0 copy-start.9
  15.5 2.5 %shard_map.175 = (f32[4,64,128]{2,1,0:T(8,128)S(1)}, f32[4,32,128]{2,1,0:T(8,128)S(1)}, f32[4,32,128]{2,1,0:T(8,128)S(1)}, f32[72,128]{1,0:T(8,128)S(1)}, f32[80,128]{1,0:T(8,128)S(1)}) custom-call(f32[4,64,128]{2,1,0:T(8,128)S(1)} %shard_map.174.known, f32[144,128]{1,0:T(8,128)S(1)} %collective-permute-done.1.beside.beside_place, ...), custom_call_target="tpu_custom_call" | custom-call | flops 10000000 | bytes 2500000 | tf_op jit(solution)/shard_map/pallas_call | solution.py:556
  18.1 0.4 collective-permute-start.3
  18.5 1.2 %collective-permute-start.2 = (f32[72,128]{1,0:T(8,128)S(1)}, f32[72,128]{1,0:T(8,128)S(1)}, u32[]{:S(2)}, u32[]{:S(2)}) collective-permute-start(f32[72,128]{1,0:T(8,128)S(1)} %get-tuple-element.54), channel_id=1, source_target_pairs={{0,64},{64,128},{128,192},{192,0},{1,65},{65,129},{129,193},{193,1... | collective-permute-start | bytes 110600 | tf_op jit(solution)/shard_map/ppermute | solution.py:571
  19.7 4.0 %shard_map.176 = (f32[4,32,128]{2,1,0:T(8,128)S(1)}, bf16[4,32,64,128]{3,2,1,0:T(8,128)(2,1)S(1)}, bf16[3,16,64,128]{3,2,1,0:T(8,128)(2,1)S(1)}) custom-call(f32[4,32,128]{2,1,0:T(8,128)S(1)} %get-tuple-element.51.b, f32[4,32,128]{2,1,0:T(8,128)S(1)} %get-tuple-element.52.f0, s32[40,128]{1,0:T(8,128)S(1)} %copy-done.1, bf16[64,64,64]{2,1,0:T(8,128)(2,1)S(1)} %bitcast.37, ...), custom_call_target="tpu_custom_call" | custom-call | flops 8000000 | bytes 2000000 | tf_op jit(solution)/shard_map/pallas_call | solution.py:556
  23.7 0.0 collective-permute-done.2.up.up_place
  23.7 0.0 copy-start.6
  23.7 0.6 shard_map.177.known
  24.3 0.0 collective-permute-done.3.beside.beside_place
  24.4 1.5 %shard_map.178 = (f32[4,32,128]{2,1,0:T(8,128)S(1)}, f32[4,16,128]{2,1,0:T(8,128)S(1)}, f32[4,16,128]{2,1,0:T(8,128)S(1)}, f32[72,128]{1,0:T(8,128)S(1)}) custom-call(f32[4,32,128]{2,1,0:T(8,128)S(1)} %shard_map.177.known, f32[80,128]{1,0:T(8,128)S(1)} %collective-permute-done.3.beside.beside_place, bf16[4,32,64,128]{3,2,1,0:T(8,128)(2,1)S(1)} %get-tuple-element.55.middle, ...), custom_call_target="tpu_custom_call" | custom-call | flops 6000000 | bytes 1500000 | tf_op jit(solution)/shard_map/pallas_call | solution.py:556
  25.9 1.7 %collective-permute-start.5 = (f32[72,128]{1,0:T(8,128)S(1)}, f32[72,128]{1,0:T(8,128)S(1)}, u32[]{:S(2)}, u32[]{:S(2)}) collective-permute-start(f32[72,128]{1,0:T(8,128)S(1)} %get-tuple-element.63), channel_id=1, source_target_pairs={{0,1},{1,2},{2,3},{3,4},{4,5},{5,6},{6,7},{7,8},{8,9},{9,10},{10,1... | collective-permute-start | bytes 110600 | tf_op jit(solution)/shard_map/ppermute | solution.py:571
  27.5 0.9 %collective-permute-start.4 = (f32[4,16,128]{2,1,0:T(8,128)S(1)}, f32[4,16,128]{2,1,0:T(8,128)S(1)}, u32[]{:S(2)}, u32[]{:S(2)}) collective-permute-start(f32[4,16,128]{2,1,0:T(8,128)S(1)} %get-tuple-element.60.own), channel_id=1, source_target_pairs={{0,64},{64,128},{128,192},{192,0},{1,65},{65,129},{129,193},{193,1... | collective-permute-start | bytes 98312 | tf_op jit(solution)/shard_map/ppermute | solution.py:571
  28.5 1.7 %shard_map.179 = (f32[4,16,128]{2,1,0:T(8,128)S(1)}, bf16[3,16,64,128]{3,2,1,0:T(8,128)(2,1)S(1)}) custom-call(f32[4,16,128]{2,1,0:T(8,128)S(1)} %get-tuple-element.59.right, f32[4,16,128]{2,1,0:T(8,128)S(1)} %get-tuple-element.60.own, bf16[3,64,32,64]{3,2,1,0:T(8,128)(2,1)S(1)} %bitcast.36, s32[40,128]{1,0:T(8,128)S(1)} %copy-done.1), custom_call_target="tpu_custom_call" | custom-call | flops 4000000 | bytes 1000000 | tf_op jit(solution)/shard_map/pallas_call | solution.py:556
  30.2 1.3 %collective-permute-done.4.up = f32[4,16,128]{2,1,0:T(8,128)S(1)} collective-permute-done((f32[4,16,128]{2,1,0:T(8,128)S(1)}, f32[4,16,128]{2,1,0:T(8,128)S(1)}, u32[]{:S(2)}, u32[]{:S(2)}) %collective-permute-start.4) | collective-permute-done | bytes 32800 | tf_op jit(solution)/shard_map/ppermute | solution.py:571
  31.5 0.3 shard_map.180.known
  31.8 0.0 collective-permute-done.5.beside
  31.9 0.7 shard_map.181
  32.5 2.5 %collective-permute-start.7 = (f32[72,128]{1,0:T(8,128)S(1)}, f32[72,128]{1,0:T(8,128)S(1)}, u32[]{:S(2)}, u32[]{:S(2)}) collective-permute-start(f32[72,128]{1,0:T(8,128)S(1)} %get-tuple-element.66), channel_id=1, source_target_pairs={{0,1},{1,2},{2,3},{3,4},{4,5},{5,6},{6,7},{7,8},{8,9},{9,10},{10,1... | collective-permute-start | bytes 110600 | tf_op jit(solution)/shard_map/ppermute | solution.py:571
  35.0 0.9 %collective-permute-start.6 = (f32[4,16,128]{2,1,0:T(8,128)S(1)}, f32[4,16,128]{2,1,0:T(8,128)S(1)}, u32[]{:S(2)}, u32[]{:S(2)}) collective-permute-start(f32[4,16,128]{2,1,0:T(8,128)S(1)} %get-tuple-element.64.own), channel_id=1, source_target_pairs={{0,64},{64,128},{128,192},{192,0},{1,65},{65,129},{129,193},{193,1... | collective-permute-start | bytes 98312 | tf_op jit(solution)/shard_map/ppermute | solution.py:571
  35.9 1.7 %shard_map.182 = (f32[4,16,128]{2,1,0:T(8,128)S(1)}, bf16[3,32,64,128]{3,2,1,0:T(8,128)(2,1)S(1)}) custom-call(f32[4,16,128]{2,1,0:T(8,128)S(1)} %get-tuple-element.59.right, f32[4,16,128]{2,1,0:T(8,128)S(1)} %get-tuple-element.64.own, bf16[3,16,64,128]{3,2,1,0:T(8,128)(2,1)S(1)} %get-tuple-element.62.faces, s32[40,128]{1,0:T(8,128)S(1)} %copy-done.1, ...), custom_call_target="tpu_custom_call" | custom-call | flops 4000000 | bytes 1000000 | tf_op jit(solution)/shard_map/pallas_call | solution.py:556
  37.6 1.3 %collective-permute-done.6.up = f32[4,16,128]{2,1,0:T(8,128)S(1)} collective-permute-done((f32[4,16,128]{2,1,0:T(8,128)S(1)}, f32[4,16,128]{2,1,0:T(8,128)S(1)}, u32[]{:S(2)}, u32[]{:S(2)}) %collective-permute-start.6) | collective-permute-done | bytes 32800 | tf_op jit(solution)/shard_map/ppermute | solution.py:571
  39.0 0.3 shard_map.183.known
  39.3 0.0 collective-permute-done.7.beside
  39.3 0.7 shard_map.184
  40.0 2.5 %collective-permute-start.9 = (f32[72,128]{1,0:T(8,128)S(1)}, f32[72,128]{1,0:T(8,128)S(1)}, u32[]{:S(2)}, u32[]{:S(2)}) collective-permute-start(f32[72,128]{1,0:T(8,128)S(1)} %get-tuple-element.69), channel_id=1, source_target_pairs={{0,1},{1,2},{2,3},{3,4},{4,5},{5,6},{6,7},{7,8},{8,9},{9,10},{10,1... | collective-permute-start | bytes 110600 | tf_op jit(solution)/shard_map/ppermute | solution.py:571
  42.4 0.9 %collective-permute-start.8 = (f32[4,16,128]{2,1,0:T(8,128)S(1)}, f32[4,16,128]{2,1,0:T(8,128)S(1)}, u32[]{:S(2)}, u32[]{:S(2)}) collective-permute-start(f32[4,16,128]{2,1,0:T(8,128)S(1)} %get-tuple-element.67.own), channel_id=1, source_target_pairs={{0,64},{64,128},{128,192},{192,0},{1,65},{65,129},{129,193},{193,1... | collective-permute-start | bytes 98312 | tf_op jit(solution)/shard_map/ppermute | solution.py:571
  43.3 1.0 %shard_map.185 = (f32[4,16,128]{2,1,0:T(8,128)S(1)}, bf16[3,16,64,128]{3,2,1,0:T(8,128)(2,1)S(1)}) custom-call(f32[4,16,128]{2,1,0:T(8,128)S(1)} %get-tuple-element.59.right, f32[4,16,128]{2,1,0:T(8,128)S(1)} %get-tuple-element.67.own, bf16[3,16,64,128]{3,2,1,0:T(8,128)(2,1)S(1)} %get-tuple-element.62.faces, s32[40,128]{1,0:T(8,128)S(1)} %copy-done.1, ...), custom_call_target="tpu_custom_call" | custom-call | flops 4000000 | bytes 1000000 | tf_op jit(solution)/shard_map/pallas_call | solution.py:556
  44.4 2.0 %collective-permute-done.8.up = f32[4,16,128]{2,1,0:T(8,128)S(1)} collective-permute-done((f32[4,16,128]{2,1,0:T(8,128)S(1)}, f32[4,16,128]{2,1,0:T(8,128)S(1)}, u32[]{:S(2)}, u32[]{:S(2)}) %collective-permute-start.8) | collective-permute-done | bytes 32800 | tf_op jit(solution)/shard_map/ppermute | solution.py:571
  46.4 0.3 shard_map.186.known
  46.7 0.0 collective-permute-done.9.beside
  46.7 0.7 shard_map.187
  47.4 2.5 %collective-permute-start.11 = (f32[72,128]{1,0:T(8,128)S(1)}, f32[72,128]{1,0:T(8,128)S(1)}, u32[]{:S(2)}, u32[]{:S(2)}) collective-permute-start(f32[72,128]{1,0:T(8,128)S(1)} %get-tuple-element.71), channel_id=1, source_target_pairs={{0,1},{1,2},{2,3},{3,4},{4,5},{5,6},{6,7},{7,8},{8,9},{9,10},{10,1... | collective-permute-start | bytes 110600 | tf_op jit(solution)/shard_map/ppermute | solution.py:571
  49.9 0.9 %collective-permute-start.10 = (f32[4,16,128]{2,1,0:T(8,128)S(1)}, f32[4,16,128]{2,1,0:T(8,128)S(1)}, u32[]{:S(2)}, u32[]{:S(2)}) collective-permute-start(f32[4,16,128]{2,1,0:T(8,128)S(1)} %get-tuple-element.70.own), channel_id=1, source_target_pairs={{0,64},{64,128},{128,192},{192,0},{1,65},{65,129},{129,193},{193,1... | collective-permute-start | bytes 98312 | tf_op jit(solution)/shard_map/ppermute | solution.py:571
  50.8 0.3 shard_map.188.known
  51.1 2.7 %collective-permute-done.10.up = f32[4,16,128]{2,1,0:T(8,128)S(1)} collective-permute-done((f32[4,16,128]{2,1,0:T(8,128)S(1)}, f32[4,16,128]{2,1,0:T(8,128)S(1)}, u32[]{:S(2)}, u32[]{:S(2)}) %collective-permute-start.10) | collective-permute-done | bytes 32800 | tf_op jit(solution)/shard_map/ppermute | solution.py:571
  53.8 0.3 shard_map.189.known
  54.2 0.0 collective-permute-done.11.beside
  54.2 0.7 shard_map.190
  54.8 2.5 %collective-permute-start.13 = (f32[72,128]{1,0:T(8,128)S(1)}, f32[72,128]{1,0:T(8,128)S(1)}, u32[]{:S(2)}, u32[]{:S(2)}) collective-permute-start(f32[72,128]{1,0:T(8,128)S(1)} %get-tuple-element.73), channel_id=1, source_target_pairs={{0,1},{1,2},{2,3},{3,4},{4,5},{5,6},{6,7},{7,8},{8,9},{9,10},{10,1... | collective-permute-start | bytes 110600 | tf_op jit(solution)/shard_map/ppermute | solution.py:571
  57.3 0.9 %collective-permute-start.12 = (f32[4,16,128]{2,1,0:T(8,128)S(1)}, f32[4,16,128]{2,1,0:T(8,128)S(1)}, u32[]{:S(2)}, u32[]{:S(2)}) collective-permute-start(f32[4,16,128]{2,1,0:T(8,128)S(1)} %get-tuple-element.72.own), channel_id=1, source_target_pairs={{0,64},{64,128},{128,192},{192,0},{1,65},{65,129},{129,193},{193,1... | collective-permute-start | bytes 98312 | tf_op jit(solution)/shard_map/ppermute | solution.py:571
  58.2 0.3 shard_map.191.known
  58.5 2.7 %collective-permute-done.12.up = f32[4,16,128]{2,1,0:T(8,128)S(1)} collective-permute-done((f32[4,16,128]{2,1,0:T(8,128)S(1)}, f32[4,16,128]{2,1,0:T(8,128)S(1)}, u32[]{:S(2)}, u32[]{:S(2)}) %collective-permute-start.12) | collective-permute-done | bytes 32800 | tf_op jit(solution)/shard_map/ppermute | solution.py:571
  61.3 0.3 shard_map.192.known
  61.6 1.3 %shard_map.193 = (f32[4,16,128]{2,1,0:T(8,128)S(1)}, f32[72,128]{1,0:T(8,128)}) custom-call(f32[4,16,128]{2,1,0:T(8,128)S(1)} %shard_map.192.known, f32[4,16,128]{2,1,0:T(8,128)S(1)} %get-tuple-element.72.own, f32[72,128]{1,0:T(8,128)S(1)} %collective-permute-done.13.beside, bf16[3,16,64,128]{3,2,1,0:T(8,128)(2,1)S(1)} %get-tuple-element.57.coarse, ...), custom_call_target="tpu_custom_call" | custom-call | flops 2000000 | bytes 500000 | tf_op jit(solution)/shard_map/pallas_call | solution.py:556
  62.9 2.4 %collective-permute-start.14 = (f32[4,16,128]{2,1,0:T(8,128)S(1)}, f32[4,16,128]{2,1,0:T(8,128)S(1)}, u32[]{:S(2)}, u32[]{:S(2)}) collective-permute-start(f32[4,16,128]{2,1,0:T(8,128)S(1)} %get-tuple-element.74.fix), channel_id=1, source_target_pairs={{0,1},{1,2},{2,3},{3,4},{4,5},{5,6},{6,7},{7,8},{8,9},{9,10},{10,1... | collective-permute-start | bytes 98312 | tf_op jit(solution)/shard_map/ppermute | solution.py:571
  65.3 1.5 %shard_map.194 = (f32[4,16,128]{2,1,0:T(8,128)S(1)}, f32[4,32,128]{2,1,0:T(8,128)S(1)}) custom-call(f32[4,32,128]{2,1,0:T(8,128)S(1)} %get-tuple-element.58.r0, f32[4,32,128]{2,1,0:T(8,128)S(1)} %get-tuple-element.52.f0, f32[4,16,128]{2,1,0:T(8,128)S(1)} %get-tuple-element.74.fix, f32[4,16,128]{2,1,0:T(8,128)S(1)} %collective-permute-done.12.up, ...), custom_call_target="tpu_custom_call" | custom-call | flops 5000000 | bytes 1250000 | tf_op jit(solution)/shard_map/pallas_call | solution.py:556
  66.8 1.0 %shard_map.195 = (f32[4,32,128]{2,1,0:T(8,128)S(1)}, f32[136,128]{1,0:T(8,128)S(1)}) custom-call(f32[4,16,128]{2,1,0:T(8,128)S(1)} %get-tuple-element.76.known, f32[4,32,128]{2,1,0:T(8,128)S(1)} %get-tuple-element.77.base, f32[4,16,128]{2,1,0:T(8,128)S(1)} %collective-permute-done.14.beside, f32[80,128]{1,0:T(8,128)S(1)} %collective-permute-done.3.beside.beside_place, ...), custom_call_target="tpu_custom_call" | custom-call | flops 2000000 | bytes 500000 | tf_op jit(solution)/shard_map/pallas_call | solution.py:556
  67.8 5.2 %collective-permute-start.16 = (f32[136,128]{1,0:T(8,128)S(1)}, f32[136,128]{1,0:T(8,128)S(1)}, u32[]{:S(2)}, u32[]{:S(2)}) collective-permute-start(f32[136,128]{1,0:T(8,128)S(1)} %get-tuple-element.82), channel_id=1, source_target_pairs={{0,1},{1,2},{2,3},{3,4},{4,5},{5,6},{6,7},{7,8},{8,9},{9,10},{10,1... | collective-permute-start | bytes 208904 | tf_op jit(solution)/shard_map/ppermute | solution.py:571
  73.0 0.9 %collective-permute-start.15 = (f32[4,32,128]{2,1,0:T(8,128)S(1)}, f32[4,32,128]{2,1,0:T(8,128)S(1)}, u32[]{:S(2)}, u32[]{:S(2)}) collective-permute-start(f32[4,32,128]{2,1,0:T(8,128)S(1)} %get-tuple-element.78.fix), channel_id=1, source_target_pairs={{0,64},{64,128},{128,192},{192,0},{1,65},{65,129},{129,193},{193,1... | collective-permute-start | bytes 196616 | tf_op jit(solution)/shard_map/ppermute | solution.py:571
  73.9 1.9 %shard_map.196 = (f32[4,32,128]{2,1,0:T(8,128)S(1)}, f32[4,64,128]{2,1,0:T(8,128)S(1)}) custom-call(f32[4,64,128]{2,1,0:T(8,128)S(1)} %get-tuple-element.50.r0, f32[4,64,128]{2,1,0:T(8,128)S(1)} %copy-done.10, f32[4,32,128]{2,1,0:T(8,128)S(1)} %get-tuple-element.78.fix, bf16[64,64,128]{2,1,0:T(8,128)(2,1)S(1)} %bitcast.32, ...), custom_call_target="tpu_custom_call" | custom-call | flops 8000000 | bytes 2000000 | tf_op jit(solution)/shard_map/pallas_call | solution.py:556
  75.8 1.6 %collective-permute-done.15.up = f32[4,32,128]{2,1,0:T(8,128)S(1)} collective-permute-done((f32[4,32,128]{2,1,0:T(8,128)S(1)}, f32[4,32,128]{2,1,0:T(8,128)S(1)}, u32[]{:S(2)}, u32[]{:S(2)}) %collective-permute-start.15) | collective-permute-done | bytes 65568 | tf_op jit(solution)/shard_map/ppermute | solution.py:571
  77.3 0.7 shard_map.197.known
  78.0 0.0 collective-permute-done.16.beside
  78.0 2.0 %shard_map.198 = f32[4,64,128]{2,1,0:T(8,128)} custom-call(f32[4,32,128]{2,1,0:T(8,128)S(1)} %shard_map.197.known, f32[4,64,128]{2,1,0:T(8,128)S(1)} %get-tuple-element.81.base, f32[136,128]{1,0:T(8,128)S(1)} %collective-permute-done.16.beside, f32[144,128]{1,0:T(8,128)S(1)} %collective-permute-done.1.beside.beside_place, ...), custom_call_target="tpu_custom_call" | custom-call | flops 4000000 | bytes 1000000 | tf_op jit(solution)/shard_map/pallas_call | solution.py:556
  (21 shorter events, 0.0 us)
Async XLA Ops:
  2.8 12.6 %collective-permute-start.1 = (f32[144,128]{1,0:T(8,128)}, f32[144,128]{1,0:T(8,128)S(1)}, u32[]{:S(2)}, u32[]{:S(2)}) collective-permute-start(f32[144,128]{1,0:T(8,128)} %get-tuple-element.48), channel_id=1, source_target_pairs={{0,1},{1,2},{2,3},{3,4},{4,5},{5,6},{6,7},{7,8},{8,9},{9,10},{10,1... | collective-permute-start | bytes 221192 | tf_op jit(solution)/shard_map/ppermute | solution.py:571
  6.0 7.4 %collective-permute-start = (f32[136,128]{1,0:T(8,128)}, f32[136,128]{1,0:T(8,128)S(1)}, u32[]{:S(2)}, u32[]{:S(2)}) collective-permute-start(f32[136,128]{1,0:T(8,128)} %get-tuple-element.47), channel_id=1, source_target_pairs={{0,64},{64,128},{128,192},{192,0},{1,65},{65,129},{129,193},{193,1... | collective-permute-start | bytes 208904 | tf_op jit(solution)/shard_map/ppermute | solution.py:571
  7.2 6.2 %copy-start = (bf16[1,1,3,64,64,128]{5,4,3,2,1,0:T(8,128)(2,1)S(1)}, bf16[1,1,3,64,64,128]{5,4,3,2,1,0:T(8,128)(2,1)}, u32[]{:S(2)}) copy-start(bf16[1,1,3,64,64,128]{5,4,3,2,1,0:T(8,128)(2,1)} %param.21) | copy-start | bytes 9437188
  7.2 6.2 %copy-start.1 = (s32[40,128]{1,0:T(8,128)S(1)}, s32[40,128]{1,0:T(8,128)}, u32[]{:S(2)}) copy-start(s32[40,128]{1,0:T(8,128)} %get-tuple-element.45.table_hbm.table) | copy-start | bytes 61444
  13.4 2.1 %copy-start.2 = (bf16[3,32,64,128]{3,2,1,0:T(8,128)(2,1)S(1)}, bf16[3,32,64,128]{3,2,1,0:T(8,128)(2,1)}, u32[]{:S(2)}) copy-start(bf16[3,32,64,128]{3,2,1,0:T(8,128)(2,1)} %get-tuple-element.49.first) | copy-start | bytes 4718596
  13.4 1.0 %copy-start.11 = (f32[4,64,128]{2,1,0:T(8,128)S(1)}, f32[4,64,128]{2,1,0:T(8,128)}, u32[]{:S(2)}) copy-start(f32[4,64,128]{2,1,0:T(8,128)} %get-tuple-element.46.known) | copy-start | bytes 393220
  14.5 5.3 %copy-start.8 = (bf16[1,1,2,64,64,32]{4,5,3,2,1,0:T(8,128)(2,1)S(1)}, bf16[1,1,2,64,64,32]{4,5,3,2,1,0:T(8,128)(2,1)}, u32[]{:S(2)}) copy-start(bf16[1,1,2,64,64,32]{4,5,3,2,1,0:T(8,128)(2,1)} %param.32) | copy-start | bytes 1572868
  15.5 4.3 %copy-start.5 = (bf16[1,1,3,64,64,64]{5,4,3,2,1,0:T(8,128)(2,1)S(1)}, bf16[1,1,3,64,64,64]{5,4,3,2,1,0:T(8,128)(2,1)}, u32[]{:S(2)}) copy-start(bf16[1,1,3,64,64,64]{5,4,3,2,1,0:T(8,128)(2,1)} %param.28) | copy-start | bytes 4718596
  15.5 4.2 %copy-start.7 = (bf16[1,1,64,64,64]{4,3,2,1,0:T(8,128)(2,1)S(1)}, bf16[1,1,64,64,64]{4,3,2,1,0:T(8,128)(2,1)}, u32[]{:S(2)}) copy-start(bf16[1,1,64,64,64]{4,3,2,1,0:T(8,128)(2,1)} %param.26) | copy-start | bytes 1572868
  15.5 4.2 %copy-start.9 = (bf16[1,1,64,64,32]{3,4,2,1,0:T(8,128)(2,1)S(1)}, bf16[1,1,64,64,32]{3,4,2,1,0:T(8,128)(2,1)}, u32[]{:S(2)}) copy-start(bf16[1,1,64,64,32]{3,4,2,1,0:T(8,128)(2,1)} %param.33) | copy-start | bytes 786436
  18.1 6.3 %collective-permute-start.3 = (f32[80,128]{1,0:T(8,128)S(1)}, f32[80,128]{1,0:T(8,128)S(1)}, u32[]{:S(2)}, u32[]{:S(2)}) collective-permute-start(f32[80,128]{1,0:T(8,128)S(1)} %get-tuple-element.56), channel_id=1, source_target_pairs={{0,1},{1,2},{2,3},{3,4},{4,5},{5,6},{6,7},{7,8},{8,9},{9,10},{10,1... | collective-permute-start | bytes 122888 | tf_op jit(solution)/shard_map/ppermute | solution.py:571
  18.5 5.2 %collective-permute-start.2 = (f32[72,128]{1,0:T(8,128)S(1)}, f32[72,128]{1,0:T(8,128)S(1)}, u32[]{:S(2)}, u32[]{:S(2)}) collective-permute-start(f32[72,128]{1,0:T(8,128)S(1)} %get-tuple-element.54), channel_id=1, source_target_pairs={{0,64},{64,128},{128,192},{192,0},{1,65},{65,129},{129,193},{193,1... | collective-permute-start | bytes 110600 | tf_op jit(solution)/shard_map/ppermute | solution.py:571
  23.7 4.7 %copy-start.6 = (bf16[1,1,3,64,64,32]{4,5,3,2,1,0:T(8,128)(2,1)S(1)}, bf16[1,1,3,64,64,32]{4,5,3,2,1,0:T(8,128)(2,1)}, u32[]{:S(2)}) copy-start(bf16[1,1,3,64,64,32]{4,5,3,2,1,0:T(8,128)(2,1)} %param.34) | copy-start | bytes 2359300
  25.9 6.0 %collective-permute-start.5 = (f32[72,128]{1,0:T(8,128)S(1)}, f32[72,128]{1,0:T(8,128)S(1)}, u32[]{:S(2)}, u32[]{:S(2)}) collective-permute-start(f32[72,128]{1,0:T(8,128)S(1)} %get-tuple-element.63), channel_id=1, source_target_pairs={{0,1},{1,2},{2,3},{3,4},{4,5},{5,6},{6,7},{7,8},{8,9},{9,10},{10,1... | collective-permute-start | bytes 110600 | tf_op jit(solution)/shard_map/ppermute | solution.py:571
  27.5 4.0 %collective-permute-start.4 = (f32[4,16,128]{2,1,0:T(8,128)S(1)}, f32[4,16,128]{2,1,0:T(8,128)S(1)}, u32[]{:S(2)}, u32[]{:S(2)}) collective-permute-start(f32[4,16,128]{2,1,0:T(8,128)S(1)} %get-tuple-element.60.own), channel_id=1, source_target_pairs={{0,64},{64,128},{128,192},{192,0},{1,65},{65,129},{129,193},{193,1... | collective-permute-start | bytes 98312 | tf_op jit(solution)/shard_map/ppermute | solution.py:571
  28.5 7.4 %copy-start.4 = (bf16[1,1,64,64,128]{4,3,2,1,0:T(8,128)(2,1)S(1)}, bf16[1,1,64,64,128]{4,3,2,1,0:T(8,128)(2,1)}, u32[]{:S(2)}) copy-start(bf16[1,1,64,64,128]{4,3,2,1,0:T(8,128)(2,1)} %param.20) | copy-start | bytes 3145732
  32.5 6.8 %collective-permute-start.7 = (f32[72,128]{1,0:T(8,128)S(1)}, f32[72,128]{1,0:T(8,128)S(1)}, u32[]{:S(2)}, u32[]{:S(2)}) collective-permute-start(f32[72,128]{1,0:T(8,128)S(1)} %get-tuple-element.66), channel_id=1, source_target_pairs={{0,1},{1,2},{2,3},{3,4},{4,5},{5,6},{6,7},{7,8},{8,9},{9,10},{10,1... | collective-permute-start | bytes 110600 | tf_op jit(solution)/shard_map/ppermute | solution.py:571
  35.0 4.0 %collective-permute-start.6 = (f32[4,16,128]{2,1,0:T(8,128)S(1)}, f32[4,16,128]{2,1,0:T(8,128)S(1)}, u32[]{:S(2)}, u32[]{:S(2)}) collective-permute-start(f32[4,16,128]{2,1,0:T(8,128)S(1)} %get-tuple-element.64.own), channel_id=1, source_target_pairs={{0,64},{64,128},{128,192},{192,0},{1,65},{65,129},{129,193},{193,1... | collective-permute-start | bytes 98312 | tf_op jit(solution)/shard_map/ppermute | solution.py:571
  40.0 6.8 %collective-permute-start.9 = (f32[72,128]{1,0:T(8,128)S(1)}, f32[72,128]{1,0:T(8,128)S(1)}, u32[]{:S(2)}, u32[]{:S(2)}) collective-permute-start(f32[72,128]{1,0:T(8,128)S(1)} %get-tuple-element.69), channel_id=1, source_target_pairs={{0,1},{1,2},{2,3},{3,4},{4,5},{5,6},{6,7},{7,8},{8,9},{9,10},{10,1... | collective-permute-start | bytes 110600 | tf_op jit(solution)/shard_map/ppermute | solution.py:571
  42.4 4.0 %collective-permute-start.8 = (f32[4,16,128]{2,1,0:T(8,128)S(1)}, f32[4,16,128]{2,1,0:T(8,128)S(1)}, u32[]{:S(2)}, u32[]{:S(2)}) collective-permute-start(f32[4,16,128]{2,1,0:T(8,128)S(1)} %get-tuple-element.67.own), channel_id=1, source_target_pairs={{0,64},{64,128},{128,192},{192,0},{1,65},{65,129},{129,193},{193,1... | collective-permute-start | bytes 98312 | tf_op jit(solution)/shard_map/ppermute | solution.py:571
  47.4 6.8 %collective-permute-start.11 = (f32[72,128]{1,0:T(8,128)S(1)}, f32[72,128]{1,0:T(8,128)S(1)}, u32[]{:S(2)}, u32[]{:S(2)}) collective-permute-start(f32[72,128]{1,0:T(8,128)S(1)} %get-tuple-element.71), channel_id=1, source_target_pairs={{0,1},{1,2},{2,3},{3,4},{4,5},{5,6},{6,7},{7,8},{8,9},{9,10},{10,1... | collective-permute-start | bytes 110600 | tf_op jit(solution)/shard_map/ppermute | solution.py:571
  49.9 4.0 %collective-permute-start.10 = (f32[4,16,128]{2,1,0:T(8,128)S(1)}, f32[4,16,128]{2,1,0:T(8,128)S(1)}, u32[]{:S(2)}, u32[]{:S(2)}) collective-permute-start(f32[4,16,128]{2,1,0:T(8,128)S(1)} %get-tuple-element.70.own), channel_id=1, source_target_pairs={{0,64},{64,128},{128,192},{192,0},{1,65},{65,129},{129,193},{193,1... | collective-permute-start | bytes 98312 | tf_op jit(solution)/shard_map/ppermute | solution.py:571
  54.8 6.8 %collective-permute-start.13 = (f32[72,128]{1,0:T(8,128)S(1)}, f32[72,128]{1,0:T(8,128)S(1)}, u32[]{:S(2)}, u32[]{:S(2)}) collective-permute-start(f32[72,128]{1,0:T(8,128)S(1)} %get-tuple-element.73), channel_id=1, source_target_pairs={{0,1},{1,2},{2,3},{3,4},{4,5},{5,6},{6,7},{7,8},{8,9},{9,10},{10,1... | collective-permute-start | bytes 110600 | tf_op jit(solution)/shard_map/ppermute | solution.py:571
  57.3 4.0 %collective-permute-start.12 = (f32[4,16,128]{2,1,0:T(8,128)S(1)}, f32[4,16,128]{2,1,0:T(8,128)S(1)}, u32[]{:S(2)}, u32[]{:S(2)}) collective-permute-start(f32[4,16,128]{2,1,0:T(8,128)S(1)} %get-tuple-element.72.own), channel_id=1, source_target_pairs={{0,64},{64,128},{128,192},{192,0},{1,65},{65,129},{129,193},{193,1... | collective-permute-start | bytes 98312 | tf_op jit(solution)/shard_map/ppermute | solution.py:571
  62.9 11.0 %copy-start.3 = (bf16[1,1,64,64,128]{4,3,2,1,0:T(8,128)(2,1)S(1)}, bf16[1,1,64,64,128]{4,3,2,1,0:T(8,128)(2,1)}, u32[]{:S(2)}) copy-start(bf16[1,1,64,64,128]{4,3,2,1,0:T(8,128)(2,1)} %param.19) | copy-start | bytes 3145732
  62.9 11.0 %copy-start.10 = (f32[4,64,128]{2,1,0:T(8,128)S(1)}, f32[4,64,128]{2,1,0:T(8,128)}, u32[]{:S(2)}) copy-start(f32[4,64,128]{2,1,0:T(8,128)} %get-tuple-element.44.f0_hbm.f0) | copy-start | bytes 393220
  62.9 3.9 %collective-permute-start.14 = (f32[4,16,128]{2,1,0:T(8,128)S(1)}, f32[4,16,128]{2,1,0:T(8,128)S(1)}, u32[]{:S(2)}, u32[]{:S(2)}) collective-permute-start(f32[4,16,128]{2,1,0:T(8,128)S(1)} %get-tuple-element.74.fix), channel_id=1, source_target_pairs={{0,1},{1,2},{2,3},{3,4},{4,5},{5,6},{6,7},{7,8},{8,9},{9,10},{10,1... | collective-permute-start | bytes 98312 | tf_op jit(solution)/shard_map/ppermute | solution.py:571
  67.8 10.2 %collective-permute-start.16 = (f32[136,128]{1,0:T(8,128)S(1)}, f32[136,128]{1,0:T(8,128)S(1)}, u32[]{:S(2)}, u32[]{:S(2)}) collective-permute-start(f32[136,128]{1,0:T(8,128)S(1)} %get-tuple-element.82), channel_id=1, source_target_pairs={{0,1},{1,2},{2,3},{3,4},{4,5},{5,6},{6,7},{7,8},{8,9},{9,10},{10,1... | collective-permute-start | bytes 208904 | tf_op jit(solution)/shard_map/ppermute | solution.py:571
  73.0 4.3 %collective-permute-start.15 = (f32[4,32,128]{2,1,0:T(8,128)S(1)}, f32[4,32,128]{2,1,0:T(8,128)S(1)}, u32[]{:S(2)}, u32[]{:S(2)}) collective-permute-start(f32[4,32,128]{2,1,0:T(8,128)S(1)} %get-tuple-element.78.fix), channel_id=1, source_target_pairs={{0,64},{64,128},{128,192},{192,0},{1,65},{65,129},{129,193},{193,1... | collective-permute-start | bytes 196616 | tf_op jit(solution)/shard_map/ppermute | solution.py:571

commit v3 on v2

--- a/solution.py
+++ b/solution.py
@@ -143,8 +143,8 @@
 
 
 def start_kernel(*refs):
-    sources, (f0, sent, longer, table) = refs[:9], refs[9:13]
-    held, semaphores = refs[13:22], refs[22]
+    sources, (f0, linked, sent, longer, table) = refs[:9], refs[9:14]
+    held, semaphores = refs[14:23], refs[23]
     b, inverse = held[:2]
     rows = B // CHUNKS
     copies = [pltpu.make_async_copy(sources[k], held[k], semaphores.at[k]) for k in (2, 3, 4, 5, 6, 7, 8, 0)]
@@ -170,6 +170,7 @@
     sent[0:128, :] = pack(wide, 2).reshape(128, LANES)
     sent[128:136, :] = table[F_POS:TABLE, :].astype(jnp.float32)
     copy_out(sent, longer)
+    linked[...] = take_lanes(f0[...], row(table, F_LINK))
 
 
 def place_lanes(n, offset):
@@ -260,24 +261,23 @@
 
 
 def fine_local_kernel(
-    b_hbm, f0_hbm, diag_hbm, faces_hbm, table_hbm, m_inverse_hbm, f_weights_hbm, out, first,
-    b, f0, diag, face, table, m_inverse, f_weights, semaphores, own, linked,
+    f0_hbm, linked_hbm, diag_hbm, faces_hbm, m_inverse_hbm, f_weights_hbm, out, first,
+    f0, linked, diag, face, m_inverse, f_weights, semaphores, own,
 ):
-    sources = [f0_hbm, table_hbm, diag_hbm, faces_hbm.at[0], b_hbm, m_inverse_hbm, f_weights_hbm]
-    targets = [f0, table, diag, face, b, m_inverse, f_weights]
+    sources = [f0_hbm, linked_hbm, diag_hbm, faces_hbm.at[0], m_inverse_hbm, f_weights_hbm]
+    targets = [f0, linked, diag, face, m_inverse, f_weights]
     copies = [pltpu.make_async_copy(x, y, semaphores.at[k]) for k, (x, y) in enumerate(zip(sources, targets))]
     for copy in copies:
         copy.start()
-    for copy in copies[:5]:
+    for copy in copies[:4]:
         copy.wait()
     own[...] = -f0[...]
-    linked[...] = take_lanes(f0[...], row(table, F_LINK))
-
-    def emit(s, rows, tile):
-        out[s, rows, :] = b[s, rows, :] + tile
+
+    def emit(s, rows, tile):
+        out[s, rows, :] = tile
 
     products([diag, face], [own, linked], B, emit)
-    for copy in copies[5:]:
+    for copy in copies[4:]:
         copy.wait()
     pack_halves([m_inverse, f_weights.at[0], f_weights.at[1]], first)
 
@@ -292,12 +292,12 @@
     return (flow[0] > 0).astype(jnp.float32)
 
 
-def fine_flow_kernel(known, up, faces, table, flow, out, v):
+def fine_flow_kernel(b, known, up, faces, table, flow, out, v):
     index, inside = chosen(up[128:136, :].astype(jnp.int32)[0:1], row(table, F_LINK + 1), 64, 128)
     expand(up[0:128, :].reshape(S, 32, LANES), index, v, inside * gate_of(flow))
 
     def emit(s, rows, tile):
-        out[s, rows, :] = known[s, rows, :] + tile
+        out[s, rows, :] = b[s, rows, :] + known[s, rows, :] + tile
 
     products([faces.at[1]], [v], B, emit)
 
@@ -426,7 +426,8 @@
 
 
 def coarse_step_kernel(step, known, own, beside, coarse, faces, table, flow, out, longer, v1, v2, total):
-    expand(beside[0:64, :].reshape(S, 16, LANES), row(table, C_LINK + 2), v2)
+    gate = (step > flow[0]).astype(jnp.float32)
+    expand(beside[0:64, :].reshape(S, 16, LANES), row(table, C_LINK + 2), v2, gate)
 
     def emit_total(s, rows, tile):
         total[s, rows, :] = known[s, rows, :] + tile
@@ -571,6 +572,16 @@
     return lax.ppermute(block, axis, [(i, (i + 1) % size) for i in range(size)])
 
 
+def iterate_from_behind(block, step):
+    flow_size, tiles = lax.axis_size("flow"), lax.axis_size("tile")
+    route = []
+    for g in range(flow_size):
+        sends = 0 <= step - 1 - g < SWEEPS - 1
+        for t in range(tiles):
+            route.append((g * tiles + t, g * tiles + ((t + 1) % tiles if sends else t ^ 1)))
+    return lax.ppermute(block, ("flow", "tile"), route)
+
+
 def own_part(array):
     return array[0, 0]
 
@@ -588,11 +599,11 @@
     f_links, m_links, c_links = (x.reshape(3, 1, -1) for x in (f_links, m_links, c_links))
     c_inverse, c_faces, m_weights = (jnp.swapaxes(x, -1, -2) for x in (c_inverse, c_faces, m_weights))
 
-    f0, f_sent, f_longer, table = call(
+    f0, f_linked, f_sent, f_longer, table = call(
         start_kernel,
         (b, f_inverse, f_links, f_order, f_picks, m_links, m_order, m_picks, c_links),
         (
-            f32(S, B, LANES), f32(136, LANES), f32(136 + SPARE, LANES),
+            f32(S, B, LANES), f32(S, B, LANES), f32(136, LANES), f32(136 + SPARE, LANES),
             jax.ShapeDtypeStruct((TABLE, LANES), jnp.int32),
         ),
         (
@@ -607,25 +618,23 @@
     f_beside, f_up = from_behind(f_longer, "tile"), from_behind(f_sent, "flow")
     known, first = call(
         fine_local_kernel,
-        (b, f0, f_diag, f_faces, table, m_inverse, f_weights),
+        (f0, f_linked, f_diag, f_faces, m_inverse, f_weights),
         (f32(S, B, LANES), bf16(3, 32, B, LANES)),
         (
             WIDE,
             WIDE,
             pltpu.VMEM((B, B, LANES), jnp.bfloat16),
             pltpu.VMEM((B, B, LANES), jnp.bfloat16),
-            pltpu.VMEM((TABLE, LANES), jnp.int32),
             pltpu.VMEM(m_inverse.shape, jnp.bfloat16),
             pltpu.VMEM(f_weights.shape, jnp.bfloat16),
-            pltpu.SemaphoreType.DMA((7,)),
-            WIDE,
+            pltpu.SemaphoreType.DMA((6,)),
             WIDE,
         ),
         3.0,
         space=pltpu.HBM,
-        limit=56000,
-    )
-    known = call(fine_flow_kernel, (known, f_up, f_faces, table), f32(S, B, LANES), (WIDE,), 0.0, flow)
+        limit=55000,
+    )
+    known = call(fine_flow_kernel, (b, known, f_up, f_faces, table), f32(S, B, LANES), (WIDE,), 0.0, flow)
     f_r0, right, m_f0, m_sent, m_longer = call(
         fine_down_kernel,
         (known, f_beside, f_faces, table, first),
@@ -653,7 +662,7 @@
     packed16 = pltpu.VMEM((S, 16, LANES), jnp.float32)
     packed32 = pltpu.VMEM((S, 32, LANES), jnp.float32)
     for step in range(1, SWEEPS + flow_size - 1):
-        beside, up = from_behind(longer, "tile"), from_behind(value, "flow")
+        beside, up = iterate_from_behind(longer, step), from_behind(value, "flow")
         if step == 1:
             known, faces = call(
                 coarse_first_kernel,

time: 80.8 us -> 76.1 us (0.942)
  starting transfers between devices: 30.7 us -> 22.6 us
  waiting for transfers between devices: 11.8 us -> 16.5 us
    ppermute x17 -> x12, starting transfers between devices: 30.7 us -> 15.6 us  [from_behind(): return lax.ppermute(block, axis, [(i, (i + 1) % size) for i in range(size)])]
    ppermute x0 -> x5, starting transfers between devices: none -> 6.99 us  [iterate_from_behind(): return lax.ppermute(block, ('flow', 'tile'), route)]
    ppermute x17 -> x12, waiting for transfers between devices: 11.8 us -> 16.5 us  [from_behind(): return lax.ppermute(block, axis, [(i, (i + 1) % size) for i in range(size)])]
  transfers between devices with their start and end apart: 17 -> 17, of which waited for: 6 -> 6; matrix products, arithmetic and copies ran while one was open for 0% -> 0% of each run, Pallas kernels for 28% -> 29%
where the time goes in v3:
time: 76.1 us; the launch traced here: 76 us
  Pallas kernels  36.2 us (48%)
  starting transfers between devices  22.6 us (30%)
  waiting for transfers between devices  16.5 us (22%)
    pallas_call x27, Pallas kernels, call(): pl.pallas_call(kernel, out_shape=outs, in_specs=specs, out_specs=jax.tree...  36.2 us
    ppermute x12, waiting for transfers between devices, from_behind(): return lax.ppermute(block, axis, [(i, (i + 1) % size) for i in range(size)])  16.5 us
    ppermute x12, starting transfers between devices, from_behind(): return lax.ppermute(block, axis, [(i, (i + 1) % size) for i in range(size)])  15.6 us
    ppermute x5, starting transfers between devices, iterate_from_behind(): return lax.ppermute(block, ('flow', 'tile'), route)  6.99 us
  transfers between devices with their start and end apart: 17, of which 6 were waited for; matrix products, arithmetic and copies ran while one was open for 0% of the time, Pallas kernels for 29%

profile of v3, /device:TPU:121, one launch (start us, length us, event | category | flops | bytes accessed | tf_op | source)
XLA Modules:
  0.0 76.0 jit_solution(18329902780555361776)
XLA Ops:
  0.0 2.9 %shard_map.172 = (f32[4,64,128]{2,1,0:T(8,128)}, f32[4,64,128]{2,1,0:T(8,128)}, f32[136,128]{1,0:T(8,128)}, f32[144,128]{1,0:T(8,128)}, s32[40,128]{1,0:T(8,128)}) custom-call(f32[4,64,128]{2,1,0:T(8,128)} %bitcast.40, bf16[64,64,128]{2,1,0:T(8,128)(2,1)} %bitcast.31, s32[3,1,128]{2,1,0:T(1,128)} %bitcast.44, s32[1,128]{1,0:T(1,128)} %bitcast.49, ...), custom_call_target="tpu_custom_call" | custom-call | flops 4000000 | bytes 1000000 | tf_op jit(solution)/shard_map/pallas_call | solution.py:557
  2.9 3.1 %collective-permute-start.1 = (f32[144,128]{1,0:T(8,128)}, f32[144,128]{1,0:T(8,128)S(1)}, u32[]{:S(2)}, u32[]{:S(2)}) collective-permute-start(f32[144,128]{1,0:T(8,128)} %get-tuple-element.50), channel_id=1, source_target_pairs={{0,1},{1,2},{2,3},{3,4},{4,5},{5,6},{6,7},{7,8},{8,9},{9,10},{10,1... | collective-permute-start | bytes 221192 | tf_op jit(solution)/shard_map/ppermute | solution.py:572
  6.0 1.2 %collective-permute-start = (f32[136,128]{1,0:T(8,128)}, f32[136,128]{1,0:T(8,128)S(1)}, u32[]{:S(2)}, u32[]{:S(2)}) collective-permute-start(f32[136,128]{1,0:T(8,128)} %get-tuple-element.48), channel_id=1, source_target_pairs={{0,64},{64,128},{128,192},{192,0},{1,65},{65,129},{129,193},{193,1... | collective-permute-start | bytes 208904 | tf_op jit(solution)/shard_map/ppermute | solution.py:572
  7.2 6.1 %shard_map.173 = (f32[4,64,128]{2,1,0:T(8,128)S(1)}, bf16[3,32,64,128]{3,2,1,0:T(8,128)(2,1)}) custom-call(f32[4,64,128]{2,1,0:T(8,128)} %get-tuple-element.45.f0_hbm.f0, f32[4,64,128]{2,1,0:T(8,128)} %get-tuple-element.46.linked_hbm, bf16[64,64,128]{2,1,0:T(8,128)(2,1)} %bitcast.33, bf16[3,64,64,128]{3,2,1,0:T(8,128)(2,1)} %bitcast.26, ...), custom_call_target="tpu_custom_call" | custom-call | flops 12000000 | bytes 3000000 | tf_op jit(solution)/shard_map/pallas_call | solution.py:557
  13.3 0.0 collective-permute-done.up.up_place
  13.4 0.0 copy-start.8
  13.4 1.0 %shard_map.174.known = f32[4,64,128]{2,1,0:T(8,128)S(1)} custom-call(f32[4,64,128]{2,1,0:T(8,128)S(1)} %bitcast.41, f32[4,64,128]{2,1,0:T(8,128)S(1)} %get-tuple-element.47.known, f32[136,128]{1,0:T(8,128)S(1)} %collective-permute-done.up.up_place, bf16[3,64,64,128]{3,2,1,0:T(8,128)(2,1)S(1)} %bitcast.27, s32[40,128]{1,0:T(8,128)S(1)} %copy-done.1, ...), custom_call_target="tpu_custom_call" | custom-call | tf_op jit(solution)/shard_map/pallas_call | solution.py:557
  14.4 0.0 collective-permute-done.1.beside.beside_place
  14.4 0.3 copy-done.2
  14.7 2.5 %shard_map.175 = (f32[4,64,128]{2,1,0:T(8,128)S(1)}, f32[4,32,128]{2,1,0:T(8,128)S(1)}, f32[4,32,128]{2,1,0:T(8,128)S(1)}, f32[72,128]{1,0:T(8,128)S(1)}, f32[80,128]{1,0:T(8,128)S(1)}) custom-call(f32[4,64,128]{2,1,0:T(8,128)S(1)} %shard_map.174.known, f32[144,128]{1,0:T(8,128)S(1)} %collective-permute-done.1.beside.beside_place, ...), custom_call_target="tpu_custom_call" | custom-call | flops 10000000 | bytes 2500000 | tf_op jit(solution)/shard_map/pallas_call | solution.py:557
  17.3 0.4 collective-permute-start.3
  17.7 1.2 %collective-permute-start.2 = (f32[72,128]{1,0:T(8,128)S(1)}, f32[72,128]{1,0:T(8,128)S(1)}, u32[]{:S(2)}, u32[]{:S(2)}) collective-permute-start(f32[72,128]{1,0:T(8,128)S(1)} %get-tuple-element.56), channel_id=1, source_target_pairs={{0,64},{64,128},{128,192},{192,0},{1,65},{65,129},{129,193},{193,1... | collective-permute-start | bytes 110600 | tf_op jit(solution)/shard_map/ppermute | solution.py:572
  18.9 4.0 %shard_map.176 = (f32[4,32,128]{2,1,0:T(8,128)S(1)}, bf16[4,32,64,128]{3,2,1,0:T(8,128)(2,1)S(1)}, bf16[3,16,64,128]{3,2,1,0:T(8,128)(2,1)S(1)}) custom-call(f32[4,32,128]{2,1,0:T(8,128)S(1)} %get-tuple-element.53.b, f32[4,32,128]{2,1,0:T(8,128)S(1)} %get-tuple-element.54.f0, s32[40,128]{1,0:T(8,128)S(1)} %copy-done.1, bf16[64,64,64]{2,1,0:T(8,128)(2,1)S(1)} %bitcast.37, ...), custom_call_target="tpu_custom_call" | custom-call | flops 8000000 | bytes 2000000 | tf_op jit(solution)/shard_map/pallas_call | solution.py:557
  22.9 0.0 collective-permute-done.2.up.up_place
  22.9 0.0 copy-start.6
  23.0 0.6 shard_map.177.known
  23.6 0.0 collective-permute-done.3.beside.beside_place
  23.6 1.5 %shard_map.178 = (f32[4,32,128]{2,1,0:T(8,128)S(1)}, f32[4,16,128]{2,1,0:T(8,128)S(1)}, f32[4,16,128]{2,1,0:T(8,128)S(1)}, f32[72,128]{1,0:T(8,128)S(1)}) custom-call(f32[4,32,128]{2,1,0:T(8,128)S(1)} %shard_map.177.known, f32[80,128]{1,0:T(8,128)S(1)} %collective-permute-done.3.beside.beside_place, bf16[4,32,64,128]{3,2,1,0:T(8,128)(2,1)S(1)} %get-tuple-element.57.middle, ...), custom_call_target="tpu_custom_call" | custom-call | flops 6000000 | bytes 1500000 | tf_op jit(solution)/shard_map/pallas_call | solution.py:557
  25.1 1.7 %collective-permute-start.5 = (f32[72,128]{1,0:T(8,128)S(1)}, f32[72,128]{1,0:T(8,128)S(1)}, u32[]{:S(2)}, u32[]{:S(2)}) collective-permute-start(f32[72,128]{1,0:T(8,128)S(1)} %get-tuple-element.65), channel_id=1, source_target_pairs={{0,1},{1,2},{2,3},{3,4},{4,5},{5,6},{6,7},{7,8},{8,9},{9,10},{10,1... | collective-permute-start | bytes 110600 | tf_op jit(solution)/shard_map/ppermute | solution.py:582
  26.8 0.0 collective-permute-start.4
  26.8 1.7 %shard_map.179 = (f32[4,16,128]{2,1,0:T(8,128)S(1)}, bf16[3,16,64,128]{3,2,1,0:T(8,128)(2,1)S(1)}) custom-call(f32[4,16,128]{2,1,0:T(8,128)S(1)} %get-tuple-element.61.right, f32[4,16,128]{2,1,0:T(8,128)S(1)} %get-tuple-element.62.own, bf16[3,64,32,64]{3,2,1,0:T(8,128)(2,1)S(1)} %bitcast.36, s32[40,128]{1,0:T(8,128)S(1)} %copy-done.1), custom_call_target="tpu_custom_call" | custom-call | flops 4000000 | bytes 1000000 | tf_op jit(solution)/shard_map/pallas_call | solution.py:557
  28.5 2.2 %collective-permute-done.4.up = f32[4,16,128]{2,1,0:T(8,128)S(1)} collective-permute-done((f32[4,16,128]{2,1,0:T(8,128)S(1)}, f32[4,16,128]{2,1,0:T(8,128)S(1)}, u32[]{:S(2)}, u32[]{:S(2)}) %collective-permute-start.4) | collective-permute-done | bytes 32800 | tf_op jit(solution)/shard_map/ppermute | solution.py:572
  30.7 0.3 shard_map.180.known
  31.1 0.0 collective-permute-done.5.beside
  31.1 0.7 shard_map.181
  31.7 2.5 %collective-permute-start.7 = (f32[72,128]{1,0:T(8,128)S(1)}, f32[72,128]{1,0:T(8,128)S(1)}, u32[]{:S(2)}, u32[]{:S(2)}) collective-permute-start(f32[72,128]{1,0:T(8,128)S(1)} %get-tuple-element.68), channel_id=1, source_target_pairs={{0,1},{1,2},{2,3},{3,4},{4,5},{5,6},{6,7},{7,8},{8,9},{9,10},{10,1... | collective-permute-start | bytes 110600 | tf_op jit(solution)/shard_map/ppermute | solution.py:582
  34.2 0.0 collective-permute-start.6
  34.2 1.7 %shard_map.182 = (f32[4,16,128]{2,1,0:T(8,128)S(1)}, bf16[3,32,64,128]{3,2,1,0:T(8,128)(2,1)S(1)}) custom-call(f32[4,16,128]{2,1,0:T(8,128)S(1)} %get-tuple-element.61.right, f32[4,16,128]{2,1,0:T(8,128)S(1)} %get-tuple-element.66.own, bf16[3,16,64,128]{3,2,1,0:T(8,128)(2,1)S(1)} %get-tuple-element.64.faces, s32[40,128]{1,0:T(8,128)S(1)} %copy-done.1, ...), custom_call_target="tpu_custom_call" | custom-call | flops 4000000 | bytes 1000000 | tf_op jit(solution)/shard_map/pallas_call | solution.py:557
  35.9 2.2 %collective-permute-done.6.up = f32[4,16,128]{2,1,0:T(8,128)S(1)} collective-permute-done((f32[4,16,128]{2,1,0:T(8,128)S(1)}, f32[4,16,128]{2,1,0:T(8,128)S(1)}, u32[]{:S(2)}, u32[]{:S(2)}) %collective-permute-start.6) | collective-permute-done | bytes 32800 | tf_op jit(solution)/shard_map/ppermute | solution.py:572
  38.2 0.3 shard_map.183.known
  38.5 0.0 collective-permute-done.7.beside
  38.5 0.7 shard_map.184
  39.2 0.1 collective-permute-start.9
  39.3 1.0 %collective-permute-start.8 = (f32[4,16,128]{2,1,0:T(8,128)S(1)}, f32[4,16,128]{2,1,0:T(8,128)S(1)}, u32[]{:S(2)}, u32[]{:S(2)}) collective-permute-start(f32[4,16,128]{2,1,0:T(8,128)S(1)} %get-tuple-element.69.own), channel_id=1, source_target_pairs={{0,64},{64,128},{128,192},{192,0},{1,65},{65,129},{129,193},{193,1... | collective-permute-start | bytes 98312 | tf_op jit(solution)/shard_map/ppermute | solution.py:572
  40.2 1.0 %shard_map.185 = (f32[4,16,128]{2,1,0:T(8,128)S(1)}, bf16[3,16,64,128]{3,2,1,0:T(8,128)(2,1)S(1)}) custom-call(f32[4,16,128]{2,1,0:T(8,128)S(1)} %get-tuple-element.61.right, f32[4,16,128]{2,1,0:T(8,128)S(1)} %get-tuple-element.69.own, bf16[3,16,64,128]{3,2,1,0:T(8,128)(2,1)S(1)} %get-tuple-element.64.faces, s32[40,128]{1,0:T(8,128)S(1)} %copy-done.1, ...), custom_call_target="tpu_custom_call" | custom-call | flops 4000000 | bytes 1000000 | tf_op jit(solution)/shard_map/pallas_call | solution.py:557
  41.3 2.2 %collective-permute-done.8.up = f32[4,16,128]{2,1,0:T(8,128)S(1)} collective-permute-done((f32[4,16,128]{2,1,0:T(8,128)S(1)}, f32[4,16,128]{2,1,0:T(8,128)S(1)}, u32[]{:S(2)}, u32[]{:S(2)}) %collective-permute-start.8) | collective-permute-done | bytes 32800 | tf_op jit(solution)/shard_map/ppermute | solution.py:572
  43.5 0.3 shard_map.186.known
  43.8 0.0 collective-permute-done.9.beside
  43.8 0.7 shard_map.187
  44.5 1.5 %collective-permute-start.11 = (f32[72,128]{1,0:T(8,128)S(1)}, f32[72,128]{1,0:T(8,128)S(1)}, u32[]{:S(2)}, u32[]{:S(2)}) collective-permute-start(f32[72,128]{1,0:T(8,128)S(1)} %get-tuple-element.73), channel_id=1, source_target_pairs={{0,1},{1,0},{2,3},{3,2},{4,5},{5,4},{6,7},{7,6},{8,9},{9,8},{10,11... | collective-permute-start | bytes 110600 | tf_op jit(solution)/shard_map/ppermute | solution.py:582
  46.0 0.0 collective-permute-start.10
  46.0 0.3 shard_map.188.known
  46.3 3.7 %collective-permute-done.10.up = f32[4,16,128]{2,1,0:T(8,128)S(1)} collective-permute-done((f32[4,16,128]{2,1,0:T(8,128)S(1)}, f32[4,16,128]{2,1,0:T(8,128)S(1)}, u32[]{:S(2)}, u32[]{:S(2)}) %collective-permute-start.10) | collective-permute-done | bytes 32800 | tf_op jit(solution)/shard_map/ppermute | solution.py:572
  49.9 0.3 shard_map.189.known
  50.3 0.0 collective-permute-done.11.beside
  50.3 0.7 shard_map.190
  50.9 1.3 %collective-permute-start.13 = (f32[72,128]{1,0:T(8,128)S(1)}, f32[72,128]{1,0:T(8,128)S(1)}, u32[]{:S(2)}, u32[]{:S(2)}) collective-permute-start(f32[72,128]{1,0:T(8,128)S(1)} %get-tuple-element.75), channel_id=1, source_target_pairs={{0,1},{1,0},{2,3},{3,2},{4,5},{5,4},{6,7},{7,6},{8,9},{9,8},{10,11... | collective-permute-start | bytes 110600 | tf_op jit(solution)/shard_map/ppermute | solution.py:582
  52.2 0.0 collective-permute-start.12
  52.2 0.3 shard_map.191.known
  52.6 3.7 %collective-permute-done.12.up = f32[4,16,128]{2,1,0:T(8,128)S(1)} collective-permute-done((f32[4,16,128]{2,1,0:T(8,128)S(1)}, f32[4,16,128]{2,1,0:T(8,128)S(1)}, u32[]{:S(2)}, u32[]{:S(2)}) %collective-permute-start.12) | collective-permute-done | bytes 32800 | tf_op jit(solution)/shard_map/ppermute | solution.py:572
  56.3 0.3 shard_map.192.known
  56.6 0.0 collective-permute-done.13.beside
  56.6 1.3 %shard_map.193 = (f32[4,16,128]{2,1,0:T(8,128)S(1)}, f32[72,128]{1,0:T(8,128)}) custom-call(f32[4,16,128]{2,1,0:T(8,128)S(1)} %shard_map.192.known, f32[4,16,128]{2,1,0:T(8,128)S(1)} %get-tuple-element.74.own, f32[72,128]{1,0:T(8,128)S(1)} %collective-permute-done.13.beside, bf16[3,16,64,128]{3,2,1,0:T(8,128)(2,1)S(1)} %get-tuple-element.59.coarse, ...), custom_call_target="tpu_custom_call" | custom-call | flops 2000000 | bytes 500000 | tf_op jit(solution)/shard_map/pallas_call | solution.py:557
  57.9 3.3 %collective-permute-start.14 = (f32[4,16,128]{2,1,0:T(8,128)S(1)}, f32[4,16,128]{2,1,0:T(8,128)S(1)}, u32[]{:S(2)}, u32[]{:S(2)}) collective-permute-start(f32[4,16,128]{2,1,0:T(8,128)S(1)} %get-tuple-element.76.fix), channel_id=1, source_target_pairs={{0,1},{1,2},{2,3},{3,4},{4,5},{5,6},{6,7},{7,8},{8,9},{9,10},{10,1... | collective-permute-start | bytes 98312 | tf_op jit(solution)/shard_map/ppermute | solution.py:572
  61.2 1.5 %shard_map.194 = (f32[4,16,128]{2,1,0:T(8,128)S(1)}, f32[4,32,128]{2,1,0:T(8,128)S(1)}) custom-call(f32[4,32,128]{2,1,0:T(8,128)S(1)} %get-tuple-element.60.r0, f32[4,32,128]{2,1,0:T(8,128)S(1)} %get-tuple-element.54.f0, f32[4,16,128]{2,1,0:T(8,128)S(1)} %get-tuple-element.76.fix, f32[4,16,128]{2,1,0:T(8,128)S(1)} %collective-permute-done.12.up, ...), custom_call_target="tpu_custom_call" | custom-call | flops 5000000 | bytes 1250000 | tf_op jit(solution)/shard_map/pallas_call | solution.py:557
  62.7 0.0 collective-permute-done.14.beside
  62.7 1.0 %shard_map.195 = (f32[4,32,128]{2,1,0:T(8,128)S(1)}, f32[136,128]{1,0:T(8,128)S(1)}) custom-call(f32[4,16,128]{2,1,0:T(8,128)S(1)} %get-tuple-element.78.known, f32[4,32,128]{2,1,0:T(8,128)S(1)} %get-tuple-element.79.base, f32[4,16,128]{2,1,0:T(8,128)S(1)} %collective-permute-done.14.beside, f32[80,128]{1,0:T(8,128)S(1)} %collective-permute-done.3.beside.beside_place, ...), custom_call_target="tpu_custom_call" | custom-call | flops 2000000 | bytes 500000 | tf_op jit(solution)/shard_map/pallas_call | solution.py:557
  63.7 5.2 %collective-permute-start.16 = (f32[136,128]{1,0:T(8,128)S(1)}, f32[136,128]{1,0:T(8,128)S(1)}, u32[]{:S(2)}, u32[]{:S(2)}) collective-permute-start(f32[136,128]{1,0:T(8,128)S(1)} %get-tuple-element.84), channel_id=1, source_target_pairs={{0,1},{1,2},{2,3},{3,4},{4,5},{5,6},{6,7},{7,8},{8,9},{9,10},{10,1... | collective-permute-start | bytes 208904 | tf_op jit(solution)/shard_map/ppermute | solution.py:572
  68.9 0.0 collective-permute-start.15
  68.9 1.9 %shard_map.196 = (f32[4,32,128]{2,1,0:T(8,128)S(1)}, f32[4,64,128]{2,1,0:T(8,128)S(1)}) custom-call(f32[4,64,128]{2,1,0:T(8,128)S(1)} %get-tuple-element.52.r0, f32[4,64,128]{2,1,0:T(8,128)S(1)} %copy-done.11, f32[4,32,128]{2,1,0:T(8,128)S(1)} %get-tuple-element.80.fix, bf16[64,64,128]{2,1,0:T(8,128)(2,1)S(1)} %bitcast.34, ...), custom_call_target="tpu_custom_call" | custom-call | flops 8000000 | bytes 2000000 | tf_op jit(solution)/shard_map/pallas_call | solution.py:557
  70.9 2.4 %collective-permute-done.15.up = f32[4,32,128]{2,1,0:T(8,128)S(1)} collective-permute-done((f32[4,32,128]{2,1,0:T(8,128)S(1)}, f32[4,32,128]{2,1,0:T(8,128)S(1)}, u32[]{:S(2)}, u32[]{:S(2)}) %collective-permute-start.15) | collective-permute-done | bytes 65568 | tf_op jit(solution)/shard_map/ppermute | solution.py:572
  73.3 0.7 shard_map.197.known
  73.9 0.0 collective-permute-done.16.beside
  73.9 2.0 %shard_map.198 = f32[4,64,128]{2,1,0:T(8,128)} custom-call(f32[4,32,128]{2,1,0:T(8,128)S(1)} %shard_map.197.known, f32[4,64,128]{2,1,0:T(8,128)S(1)} %get-tuple-element.83.base, f32[136,128]{1,0:T(8,128)S(1)} %collective-permute-done.16.beside, f32[144,128]{1,0:T(8,128)S(1)} %collective-permute-done.1.beside.beside_place, ...), custom_call_target="tpu_custom_call" | custom-call | flops 4000000 | bytes 1000000 | tf_op jit(solution)/shard_map/pallas_call | solution.py:557
  (21 shorter events, 0.0 us)
Async XLA Ops:
  2.9 11.5 %collective-permute-start.1 = (f32[144,128]{1,0:T(8,128)}, f32[144,128]{1,0:T(8,128)S(1)}, u32[]{:S(2)}, u32[]{:S(2)}) collective-permute-start(f32[144,128]{1,0:T(8,128)} %get-tuple-element.50), channel_id=1, source_target_pairs={{0,1},{1,2},{2,3},{3,4},{4,5},{5,6},{6,7},{7,8},{8,9},{9,10},{10,1... | collective-permute-start | bytes 221192 | tf_op jit(solution)/shard_map/ppermute | solution.py:572
  6.0 7.3 %collective-permute-start = (f32[136,128]{1,0:T(8,128)}, f32[136,128]{1,0:T(8,128)S(1)}, u32[]{:S(2)}, u32[]{:S(2)}) collective-permute-start(f32[136,128]{1,0:T(8,128)} %get-tuple-element.48), channel_id=1, source_target_pairs={{0,64},{64,128},{128,192},{192,0},{1,65},{65,129},{129,193},{193,1... | collective-permute-start | bytes 208904 | tf_op jit(solution)/shard_map/ppermute | solution.py:572
  7.2 6.1 %copy-start = (bf16[1,1,3,64,64,128]{5,4,3,2,1,0:T(8,128)(2,1)S(1)}, bf16[1,1,3,64,64,128]{5,4,3,2,1,0:T(8,128)(2,1)}, u32[]{:S(2)}) copy-start(bf16[1,1,3,64,64,128]{5,4,3,2,1,0:T(8,128)(2,1)} %param.21) | copy-start | bytes 9437188
  7.2 6.1 %copy-start.1 = (s32[40,128]{1,0:T(8,128)S(1)}, s32[40,128]{1,0:T(8,128)}, u32[]{:S(2)}) copy-start(s32[40,128]{1,0:T(8,128)} %get-tuple-element.49.table) | copy-start | bytes 61444
  7.2 6.1 %copy-start.10 = (f32[1,1,4,64,128]{4,3,2,1,0:T(8,128)S(1)}, f32[1,1,4,64,128]{4,3,2,1,0:T(8,128)}, u32[]{:S(2)}) copy-start(f32[1,1,4,64,128]{4,3,2,1,0:T(8,128)} %param.18) | copy-start | bytes 393220
  13.3 1.4 %copy-start.2 = (bf16[3,32,64,128]{3,2,1,0:T(8,128)(2,1)S(1)}, bf16[3,32,64,128]{3,2,1,0:T(8,128)(2,1)}, u32[]{:S(2)}) copy-start(bf16[3,32,64,128]{3,2,1,0:T(8,128)(2,1)} %get-tuple-element.51.first) | copy-start | bytes 4718596
  13.4 5.6 %copy-start.8 = (bf16[1,1,2,64,64,32]{4,5,3,2,1,0:T(8,128)(2,1)S(1)}, bf16[1,1,2,64,64,32]{4,5,3,2,1,0:T(8,128)(2,1)}, u32[]{:S(2)}) copy-start(bf16[1,1,2,64,64,32]{4,5,3,2,1,0:T(8,128)(2,1)} %param.32) | copy-start | bytes 1572868
  14.7 4.2 %copy-start.5 = (bf16[1,1,3,64,64,64]{5,4,3,2,1,0:T(8,128)(2,1)S(1)}, bf16[1,1,3,64,64,64]{5,4,3,2,1,0:T(8,128)(2,1)}, u32[]{:S(2)}) copy-start(bf16[1,1,3,64,64,64]{5,4,3,2,1,0:T(8,128)(2,1)} %param.28) | copy-start | bytes 4718596
  14.7 4.2 %copy-start.7 = (bf16[1,1,64,64,64]{4,3,2,1,0:T(8,128)(2,1)S(1)}, bf16[1,1,64,64,64]{4,3,2,1,0:T(8,128)(2,1)}, u32[]{:S(2)}) copy-start(bf16[1,1,64,64,64]{4,3,2,1,0:T(8,128)(2,1)} %param.26) | copy-start | bytes 1572868
  14.7 4.2 %copy-start.9 = (bf16[1,1,64,64,32]{3,4,2,1,0:T(8,128)(2,1)S(1)}, bf16[1,1,64,64,32]{3,4,2,1,0:T(8,128)(2,1)}, u32[]{:S(2)}) copy-start(bf16[1,1,64,64,32]{3,4,2,1,0:T(8,128)(2,1)} %param.33) | copy-start | bytes 786436
  17.3 6.3 %collective-permute-start.3 = (f32[80,128]{1,0:T(8,128)S(1)}, f32[80,128]{1,0:T(8,128)S(1)}, u32[]{:S(2)}, u32[]{:S(2)}) collective-permute-start(f32[80,128]{1,0:T(8,128)S(1)} %get-tuple-element.58), channel_id=1, source_target_pairs={{0,1},{1,2},{2,3},{3,4},{4,5},{5,6},{6,7},{7,8},{8,9},{9,10},{10,1... | collective-permute-start | bytes 122888 | tf_op jit(solution)/shard_map/ppermute | solution.py:572
  17.7 5.2 %collective-permute-start.2 = (f32[72,128]{1,0:T(8,128)S(1)}, f32[72,128]{1,0:T(8,128)S(1)}, u32[]{:S(2)}, u32[]{:S(2)}) collective-permute-start(f32[72,128]{1,0:T(8,128)S(1)} %get-tuple-element.56), channel_id=1, source_target_pairs={{0,64},{64,128},{128,192},{192,0},{1,65},{65,129},{129,193},{193,1... | collective-permute-start | bytes 110600 | tf_op jit(solution)/shard_map/ppermute | solution.py:572
  22.9 3.8 %copy-start.6 = (bf16[1,1,3,64,64,32]{4,5,3,2,1,0:T(8,128)(2,1)S(1)}, bf16[1,1,3,64,64,32]{4,5,3,2,1,0:T(8,128)(2,1)}, u32[]{:S(2)}) copy-start(bf16[1,1,3,64,64,32]{4,5,3,2,1,0:T(8,128)(2,1)} %param.34) | copy-start | bytes 2359300
  25.1 6.0 %collective-permute-start.5 = (f32[72,128]{1,0:T(8,128)S(1)}, f32[72,128]{1,0:T(8,128)S(1)}, u32[]{:S(2)}, u32[]{:S(2)}) collective-permute-start(f32[72,128]{1,0:T(8,128)S(1)} %get-tuple-element.65), channel_id=1, source_target_pairs={{0,1},{1,2},{2,3},{3,4},{4,5},{5,6},{6,7},{7,8},{8,9},{9,10},{10,1... | collective-permute-start | bytes 110600 | tf_op jit(solution)/shard_map/ppermute | solution.py:582
  26.8 4.0 %collective-permute-start.4 = (f32[4,16,128]{2,1,0:T(8,128)S(1)}, f32[4,16,128]{2,1,0:T(8,128)S(1)}, u32[]{:S(2)}, u32[]{:S(2)}) collective-permute-start(f32[4,16,128]{2,1,0:T(8,128)S(1)} %get-tuple-element.62.own), channel_id=1, source_target_pairs={{0,64},{64,128},{128,192},{192,0},{1,65},{65,129},{129,193},{193,1... | collective-permute-start | bytes 98312 | tf_op jit(solution)/shard_map/ppermute | solution.py:572
  26.8 7.4 %copy-start.3 = (bf16[1,1,64,64,128]{4,3,2,1,0:T(8,128)(2,1)S(1)}, bf16[1,1,64,64,128]{4,3,2,1,0:T(8,128)(2,1)}, u32[]{:S(2)}) copy-start(bf16[1,1,64,64,128]{4,3,2,1,0:T(8,128)(2,1)} %param.20) | copy-start | bytes 3145732
  31.7 6.8 %collective-permute-start.7 = (f32[72,128]{1,0:T(8,128)S(1)}, f32[72,128]{1,0:T(8,128)S(1)}, u32[]{:S(2)}, u32[]{:S(2)}) collective-permute-start(f32[72,128]{1,0:T(8,128)S(1)} %get-tuple-element.68), channel_id=1, source_target_pairs={{0,1},{1,2},{2,3},{3,4},{4,5},{5,6},{6,7},{7,8},{8,9},{9,10},{10,1... | collective-permute-start | bytes 110600 | tf_op jit(solution)/shard_map/ppermute | solution.py:582
  34.2 4.0 %collective-permute-start.6 = (f32[4,16,128]{2,1,0:T(8,128)S(1)}, f32[4,16,128]{2,1,0:T(8,128)S(1)}, u32[]{:S(2)}, u32[]{:S(2)}) collective-permute-start(f32[4,16,128]{2,1,0:T(8,128)S(1)} %get-tuple-element.66.own), channel_id=1, source_target_pairs={{0,64},{64,128},{128,192},{192,0},{1,65},{65,129},{129,193},{193,1... | collective-permute-start | bytes 98312 | tf_op jit(solution)/shard_map/ppermute | solution.py:572
  39.2 4.6 %collective-permute-start.9 = (f32[72,128]{1,0:T(8,128)S(1)}, f32[72,128]{1,0:T(8,128)S(1)}, u32[]{:S(2)}, u32[]{:S(2)}) collective-permute-start(f32[72,128]{1,0:T(8,128)S(1)} %get-tuple-element.71), channel_id=1, source_target_pairs={{0,1},{1,0},{2,3},{3,2},{4,5},{5,4},{6,7},{7,6},{8,9},{9,8},{10,11... | collective-permute-start | bytes 110600 | tf_op jit(solution)/shard_map/ppermute | solution.py:582
  39.3 4.2 %collective-permute-start.8 = (f32[4,16,128]{2,1,0:T(8,128)S(1)}, f32[4,16,128]{2,1,0:T(8,128)S(1)}, u32[]{:S(2)}, u32[]{:S(2)}) collective-permute-start(f32[4,16,128]{2,1,0:T(8,128)S(1)} %get-tuple-element.69.own), channel_id=1, source_target_pairs={{0,64},{64,128},{128,192},{192,0},{1,65},{65,129},{129,193},{193,1... | collective-permute-start | bytes 98312 | tf_op jit(solution)/shard_map/ppermute | solution.py:572
  44.5 5.8 %collective-permute-start.11 = (f32[72,128]{1,0:T(8,128)S(1)}, f32[72,128]{1,0:T(8,128)S(1)}, u32[]{:S(2)}, u32[]{:S(2)}) collective-permute-start(f32[72,128]{1,0:T(8,128)S(1)} %get-tuple-element.73), channel_id=1, source_target_pairs={{0,1},{1,0},{2,3},{3,2},{4,5},{5,4},{6,7},{7,6},{8,9},{9,8},{10,11... | collective-permute-start | bytes 110600 | tf_op jit(solution)/shard_map/ppermute | solution.py:582
  46.0 4.0 %collective-permute-start.10 = (f32[4,16,128]{2,1,0:T(8,128)S(1)}, f32[4,16,128]{2,1,0:T(8,128)S(1)}, u32[]{:S(2)}, u32[]{:S(2)}) collective-permute-start(f32[4,16,128]{2,1,0:T(8,128)S(1)} %get-tuple-element.72.own), channel_id=1, source_target_pairs={{0,64},{64,128},{128,192},{192,0},{1,65},{65,129},{129,193},{193,1... | collective-permute-start | bytes 98312 | tf_op jit(solution)/shard_map/ppermute | solution.py:572
  50.9 5.7 %collective-permute-start.13 = (f32[72,128]{1,0:T(8,128)S(1)}, f32[72,128]{1,0:T(8,128)S(1)}, u32[]{:S(2)}, u32[]{:S(2)}) collective-permute-start(f32[72,128]{1,0:T(8,128)S(1)} %get-tuple-element.75), channel_id=1, source_target_pairs={{0,1},{1,0},{2,3},{3,2},{4,5},{5,4},{6,7},{7,6},{8,9},{9,8},{10,11... | collective-permute-start | bytes 110600 | tf_op jit(solution)/shard_map/ppermute | solution.py:582
  52.2 4.0 %collective-permute-start.12 = (f32[4,16,128]{2,1,0:T(8,128)S(1)}, f32[4,16,128]{2,1,0:T(8,128)S(1)}, u32[]{:S(2)}, u32[]{:S(2)}) collective-permute-start(f32[4,16,128]{2,1,0:T(8,128)S(1)} %get-tuple-element.74.own), channel_id=1, source_target_pairs={{0,64},{64,128},{128,192},{192,0},{1,65},{65,129},{129,193},{193,1... | collective-permute-start | bytes 98312 | tf_op jit(solution)/shard_map/ppermute | solution.py:572
  57.9 11.1 %copy-start.4 = (bf16[1,1,64,64,128]{4,3,2,1,0:T(8,128)(2,1)S(1)}, bf16[1,1,64,64,128]{4,3,2,1,0:T(8,128)(2,1)}, u32[]{:S(2)}) copy-start(bf16[1,1,64,64,128]{4,3,2,1,0:T(8,128)(2,1)} %param.19) | copy-start | bytes 3145732
  57.9 11.1 %copy-start.11 = (f32[4,64,128]{2,1,0:T(8,128)S(1)}, f32[4,64,128]{2,1,0:T(8,128)}, u32[]{:S(2)}) copy-start(f32[4,64,128]{2,1,0:T(8,128)} %get-tuple-element.45.f0_hbm.f0) | copy-start | bytes 393220
  57.9 4.8 %collective-permute-start.14 = (f32[4,16,128]{2,1,0:T(8,128)S(1)}, f32[4,16,128]{2,1,0:T(8,128)S(1)}, u32[]{:S(2)}, u32[]{:S(2)}) collective-permute-start(f32[4,16,128]{2,1,0:T(8,128)S(1)} %get-tuple-element.76.fix), channel_id=1, source_target_pairs={{0,1},{1,2},{2,3},{3,4},{4,5},{5,6},{6,7},{7,8},{8,9},{9,10},{10,1... | collective-permute-start | bytes 98312 | tf_op jit(solution)/shard_map/ppermute | solution.py:572
  63.7 10.2 %collective-permute-start.16 = (f32[136,128]{1,0:T(8,128)S(1)}, f32[136,128]{1,0:T(8,128)S(1)}, u32[]{:S(2)}, u32[]{:S(2)}) collective-permute-start(f32[136,128]{1,0:T(8,128)S(1)} %get-tuple-element.84), channel_id=1, source_target_pairs={{0,1},{1,2},{2,3},{3,4},{4,5},{5,6},{6,7},{7,8},{8,9},{9,10},{10,1... | collective-permute-start | bytes 208904 | tf_op jit(solution)/shard_map/ppermute | solution.py:572
  68.9 4.3 %collective-permute-start.15 = (f32[4,32,128]{2,1,0:T(8,128)S(1)}, f32[4,32,128]{2,1,0:T(8,128)S(1)}, u32[]{:S(2)}, u32[]{:S(2)}) collective-permute-start(f32[4,32,128]{2,1,0:T(8,128)S(1)} %get-tuple-element.80.fix), channel_id=1, source_target_pairs={{0,64},{64,128},{128,192},{192,0},{1,65},{65,129},{129,193},{193,1... | collective-permute-start | bytes 196616 | tf_op jit(solution)/shard_map/ppermute | solution.py:572

commit v4 on v3

--- a/solution.py
+++ b/solution.py
@@ -261,15 +261,20 @@
 
 
 def fine_local_kernel(
-    f0_hbm, linked_hbm, diag_hbm, faces_hbm, m_inverse_hbm, f_weights_hbm, out, first,
-    f0, linked, diag, face, m_inverse, f_weights, semaphores, own,
+    f0_hbm, linked_hbm, diag_hbm, faces_hbm, m_inverse_hbm, f_weights_hbm, out, first_hbm,
+    f0, linked, diag, face, m_inverse, f_weights, first, semaphores, own,
 ):
-    sources = [f0_hbm, linked_hbm, diag_hbm, faces_hbm.at[0], m_inverse_hbm, f_weights_hbm]
-    targets = [f0, linked, diag, face, m_inverse, f_weights]
+    sources = [m_inverse_hbm, f_weights_hbm, f0_hbm, linked_hbm, diag_hbm, faces_hbm.at[0]]
+    targets = [m_inverse, f_weights, f0, linked, diag, face]
     copies = [pltpu.make_async_copy(x, y, semaphores.at[k]) for k, (x, y) in enumerate(zip(sources, targets))]
     for copy in copies:
         copy.start()
-    for copy in copies[:4]:
+    for copy in copies[:2]:
+        copy.wait()
+    pack_halves([m_inverse, f_weights.at[0], f_weights.at[1]], first)
+    packed = pltpu.make_async_copy(first, first_hbm, semaphores.at[6])
+    packed.start()
+    for copy in copies[2:]:
         copy.wait()
     own[...] = -f0[...]
 
@@ -277,9 +282,7 @@
         out[s, rows, :] = tile
 
     products([diag, face], [own, linked], B, emit)
-    for copy in copies[4:]:
-        copy.wait()
-    pack_halves([m_inverse, f_weights.at[0], f_weights.at[1]], first)
+    packed.wait()
 
 
 def chosen(place, index, low, high):
@@ -472,7 +475,7 @@
 def middle_up_kernel(known, base, beside, beside_place, chosen_middle, table, out, longer, v1, v2, total, result):
     link = pick(row(table, M_LINK + 2), row(table, M_FINE))
     index, inside = chosen(beside_place[64:72, :].astype(jnp.int32)[0:1], link, 0, 32)
-    expand(beside[...], index, v1, inside)
+    expand(beside[0:64, :].reshape(S, 16, LANES), index, v1, inside)
 
     def emit_total(s, rows, tile):
         total[s, rows, :] = known[s, rows, :] + tile
@@ -549,7 +552,7 @@
     return jax.ShapeDtypeStruct(shape, jnp.bfloat16)
 
 
-def call(kernel, operands, outs, scratch=(), work=1.0, flow=None, space=pltpu.VMEM, limit=40 * 1024):
+def call(kernel, operands, outs, scratch=(), work=1.0, flow=None, space=pltpu.VMEM, limit=40 * 1024, out_spaces=None):
     specs = [pl.BlockSpec(memory_space=space)] * len(operands)
     if flow is not None:
         specs.append(pl.BlockSpec(memory_space=pltpu.SMEM))
@@ -558,7 +561,9 @@
         kernel,
         out_shape=outs,
         in_specs=specs,
-        out_specs=jax.tree.map(lambda _: pl.BlockSpec(memory_space=pltpu.VMEM), outs),
+        out_specs=jax.tree.map(lambda _: pl.BlockSpec(memory_space=pltpu.VMEM), outs)
+        if out_spaces is None
+        else tuple(pl.BlockSpec(memory_space=x) for x in out_spaces),
         scratch_shapes=list(scratch),
         compiler_params=pltpu.CompilerParams(vmem_limit_bytes=limit * 1024),
         cost_estimate=pl.CostEstimate(
@@ -627,12 +632,14 @@
             pltpu.VMEM((B, B, LANES), jnp.bfloat16),
             pltpu.VMEM(m_inverse.shape, jnp.bfloat16),
             pltpu.VMEM(f_weights.shape, jnp.bfloat16),
-            pltpu.SemaphoreType.DMA((6,)),
+            pltpu.VMEM((3, 32, B, LANES), jnp.bfloat16),
+            pltpu.SemaphoreType.DMA((7,)),
             WIDE,
         ),
         3.0,
         space=pltpu.HBM,
         limit=55000,
+        out_spaces=(pltpu.VMEM, pltpu.HBM),
     )
     known = call(fine_flow_kernel, (b, known, f_up, f_faces, table), f32(S, B, LANES), (WIDE,), 0.0, flow)
     f_r0, right, m_f0, m_sent, m_longer = call(
@@ -695,7 +702,7 @@
             0.5,
             flow,
         )
-    beside = from_behind(value, "tile")
+    beside = from_behind(longer, "tile")
     known, base = call(
         middle_up_local_kernel,
         (m_r0, m_f0, value, up, m_up, middle, chosen_middle, table),

time: 76.1 us -> 74.5 us (0.979)
  Pallas kernels: 36.2 us -> 34.5 us
    pallas_call x27, Pallas kernels: 36.2 us -> 34.5 us  [call(): pl.pallas_call(kernel, out_shape=outs, in_specs=specs, out_specs=jax.tree...]
where the time goes in v4:
time: 74.5 us; the launch traced here: 74.4 us
  Pallas kernels  34.5 us (46%)
  starting transfers between devices  22.7 us (30%)
  waiting for transfers between devices  16.4 us (22%)
    pallas_call x27, Pallas kernels, call(): pl.pallas_call(kernel, out_shape=outs, in_specs=specs, out_specs=jax.tree...  34.5 us
    ppermute x12, waiting for transfers between devices, from_behind(): return lax.ppermute(block, axis, [(i, (i + 1) % size) for i in range(size)])  16.4 us
    ppermute x12, starting transfers between devices, from_behind(): return lax.ppermute(block, axis, [(i, (i + 1) % size) for i in range(size)])  15.7 us
    ppermute x5, starting transfers between devices, iterate_from_behind(): return lax.ppermute(block, ('flow', 'tile'), route)  6.99 us
  transfers between devices with their start and end apart: 17, of which 6 were waited for; matrix products, arithmetic and copies ran while one was open for 0% of the time, Pallas kernels for 29%

profile of v4, /device:TPU:121, one launch (start us, length us, event | category | flops | bytes accessed | tf_op | source)
XLA Modules:
  0.0 74.4 jit_solution(16054508522511957920)
XLA Ops:
  0.0 2.9 %shard_map.172 = (f32[4,64,128]{2,1,0:T(8,128)}, f32[4,64,128]{2,1,0:T(8,128)}, f32[136,128]{1,0:T(8,128)}, f32[144,128]{1,0:T(8,128)}, s32[40,128]{1,0:T(8,128)}) custom-call(f32[4,64,128]{2,1,0:T(8,128)} %bitcast.40, bf16[64,64,128]{2,1,0:T(8,128)(2,1)} %bitcast.31, s32[3,1,128]{2,1,0:T(1,128)} %bitcast.44, s32[1,128]{1,0:T(1,128)} %bitcast.49, ...), custom_call_target="tpu_custom_call" | custom-call | flops 4000000 | bytes 1000000 | tf_op jit(solution)/shard_map/pallas_call | solution.py:560
  2.9 3.1 %collective-permute-start.1 = (f32[144,128]{1,0:T(8,128)}, f32[144,128]{1,0:T(8,128)S(1)}, u32[]{:S(2)}, u32[]{:S(2)}) collective-permute-start(f32[144,128]{1,0:T(8,128)} %get-tuple-element.51), channel_id=1, source_target_pairs={{0,1},{1,2},{2,3},{3,4},{4,5},{5,6},{6,7},{7,8},{8,9},{9,10},{10,1... | collective-permute-start | bytes 221192 | tf_op jit(solution)/shard_map/ppermute | solution.py:577
  6.0 1.2 %collective-permute-start = (f32[136,128]{1,0:T(8,128)}, f32[136,128]{1,0:T(8,128)S(1)}, u32[]{:S(2)}, u32[]{:S(2)}) collective-permute-start(f32[136,128]{1,0:T(8,128)} %get-tuple-element.49), channel_id=1, source_target_pairs={{0,64},{64,128},{128,192},{192,0},{1,65},{65,129},{129,193},{193,1... | collective-permute-start | bytes 208904 | tf_op jit(solution)/shard_map/ppermute | solution.py:577
  7.2 5.0 %shard_map.173 = (f32[4,64,128]{2,1,0:T(8,128)S(1)}, bf16[3,32,64,128]{3,2,1,0:T(8,128)(2,1)}) custom-call(f32[4,64,128]{2,1,0:T(8,128)} %get-tuple-element.46.f0_hbm.f0, f32[4,64,128]{2,1,0:T(8,128)} %get-tuple-element.47.linked_hbm, bf16[64,64,128]{2,1,0:T(8,128)(2,1)} %bitcast.33, bf16[3,64,64,128]{3,2,1,0:T(8,128)(2,1)} %bitcast.26, ...), custom_call_target="tpu_custom_call" | custom-call | flops 12000000 | bytes 3000000 | tf_op jit(solution)/shard_map/pallas_call | solution.py:560
  12.2 0.0 collective-permute-done.up.up_place
  12.3 0.0 copy-start.8
  12.3 1.0 %shard_map.174.known = f32[4,64,128]{2,1,0:T(8,128)S(1)} custom-call(f32[4,64,128]{2,1,0:T(8,128)S(1)} %bitcast.41, f32[4,64,128]{2,1,0:T(8,128)S(1)} %get-tuple-element.48.known, f32[136,128]{1,0:T(8,128)S(1)} %collective-permute-done.up.up_place, bf16[3,64,64,128]{3,2,1,0:T(8,128)(2,1)S(1)} %bitcast.27, s32[40,128]{1,0:T(8,128)S(1)} %copy-done.1, ...), custom_call_target="tpu_custom_call" | custom-call | tf_op jit(solution)/shard_map/pallas_call | solution.py:560
  13.3 0.0 collective-permute-done.1.beside.beside_place
  13.3 0.3 copy-done.2
  13.6 2.5 %shard_map.175 = (f32[4,64,128]{2,1,0:T(8,128)S(1)}, f32[4,32,128]{2,1,0:T(8,128)S(1)}, f32[4,32,128]{2,1,0:T(8,128)S(1)}, f32[72,128]{1,0:T(8,128)S(1)}, f32[80,128]{1,0:T(8,128)S(1)}) custom-call(f32[4,64,128]{2,1,0:T(8,128)S(1)} %shard_map.174.known, f32[144,128]{1,0:T(8,128)S(1)} %collective-permute-done.1.beside.beside_place, ...), custom_call_target="tpu_custom_call" | custom-call | flops 10000000 | bytes 2500000 | tf_op jit(solution)/shard_map/pallas_call | solution.py:560
  16.2 0.4 collective-permute-start.3
  16.6 1.2 %collective-permute-start.2 = (f32[72,128]{1,0:T(8,128)S(1)}, f32[72,128]{1,0:T(8,128)S(1)}, u32[]{:S(2)}, u32[]{:S(2)}) collective-permute-start(f32[72,128]{1,0:T(8,128)S(1)} %get-tuple-element.57), channel_id=1, source_target_pairs={{0,64},{64,128},{128,192},{192,0},{1,65},{65,129},{129,193},{193,1... | collective-permute-start | bytes 110600 | tf_op jit(solution)/shard_map/ppermute | solution.py:577
  17.9 4.0 %shard_map.176 = (f32[4,32,128]{2,1,0:T(8,128)S(1)}, bf16[4,32,64,128]{3,2,1,0:T(8,128)(2,1)S(1)}, bf16[3,16,64,128]{3,2,1,0:T(8,128)(2,1)S(1)}) custom-call(f32[4,32,128]{2,1,0:T(8,128)S(1)} %get-tuple-element.54.b, f32[4,32,128]{2,1,0:T(8,128)S(1)} %get-tuple-element.55.f0, s32[40,128]{1,0:T(8,128)S(1)} %copy-done.1, bf16[64,64,64]{2,1,0:T(8,128)(2,1)S(1)} %bitcast.37, ...), custom_call_target="tpu_custom_call" | custom-call | flops 8000000 | bytes 2000000 | tf_op jit(solution)/shard_map/pallas_call | solution.py:560
  21.8 0.0 collective-permute-done.2.up.up_place
  21.9 0.0 copy-start.6
  21.9 0.6 shard_map.177.known
  22.5 0.0 collective-permute-done.3.beside.beside_place
  22.5 1.5 %shard_map.178 = (f32[4,32,128]{2,1,0:T(8,128)S(1)}, f32[4,16,128]{2,1,0:T(8,128)S(1)}, f32[4,16,128]{2,1,0:T(8,128)S(1)}, f32[72,128]{1,0:T(8,128)S(1)}) custom-call(f32[4,32,128]{2,1,0:T(8,128)S(1)} %shard_map.177.known, f32[80,128]{1,0:T(8,128)S(1)} %collective-permute-done.3.beside.beside_place, bf16[4,32,64,128]{3,2,1,0:T(8,128)(2,1)S(1)} %get-tuple-element.58.middle, ...), custom_call_target="tpu_custom_call" | custom-call | flops 6000000 | bytes 1500000 | tf_op jit(solution)/shard_map/pallas_call | solution.py:560
  24.0 1.7 %collective-permute-start.5 = (f32[72,128]{1,0:T(8,128)S(1)}, f32[72,128]{1,0:T(8,128)S(1)}, u32[]{:S(2)}, u32[]{:S(2)}) collective-permute-start(f32[72,128]{1,0:T(8,128)S(1)} %get-tuple-element.66), channel_id=1, source_target_pairs={{0,1},{1,2},{2,3},{3,4},{4,5},{5,6},{6,7},{7,8},{8,9},{9,10},{10,1... | collective-permute-start | bytes 110600 | tf_op jit(solution)/shard_map/ppermute | solution.py:587
  25.7 0.0 collective-permute-start.4
  25.7 1.7 %shard_map.179 = (f32[4,16,128]{2,1,0:T(8,128)S(1)}, bf16[3,16,64,128]{3,2,1,0:T(8,128)(2,1)S(1)}) custom-call(f32[4,16,128]{2,1,0:T(8,128)S(1)} %get-tuple-element.62.right, f32[4,16,128]{2,1,0:T(8,128)S(1)} %get-tuple-element.63.own, bf16[3,64,32,64]{3,2,1,0:T(8,128)(2,1)S(1)} %bitcast.36, s32[40,128]{1,0:T(8,128)S(1)} %copy-done.1), custom_call_target="tpu_custom_call" | custom-call | flops 4000000 | bytes 1000000 | tf_op jit(solution)/shard_map/pallas_call | solution.py:560
  27.4 2.2 %collective-permute-done.4.up = f32[4,16,128]{2,1,0:T(8,128)S(1)} collective-permute-done((f32[4,16,128]{2,1,0:T(8,128)S(1)}, f32[4,16,128]{2,1,0:T(8,128)S(1)}, u32[]{:S(2)}, u32[]{:S(2)}) %collective-permute-start.4) | collective-permute-done | bytes 32800 | tf_op jit(solution)/shard_map/ppermute | solution.py:577
  29.6 0.3 shard_map.180.known
  30.0 0.0 collective-permute-done.5.beside
  30.0 0.7 shard_map.181
  30.6 2.5 %collective-permute-start.7 = (f32[72,128]{1,0:T(8,128)S(1)}, f32[72,128]{1,0:T(8,128)S(1)}, u32[]{:S(2)}, u32[]{:S(2)}) collective-permute-start(f32[72,128]{1,0:T(8,128)S(1)} %get-tuple-element.69), channel_id=1, source_target_pairs={{0,1},{1,2},{2,3},{3,4},{4,5},{5,6},{6,7},{7,8},{8,9},{9,10},{10,1... | collective-permute-start | bytes 110600 | tf_op jit(solution)/shard_map/ppermute | solution.py:587
  33.1 0.0 collective-permute-start.6
  33.1 1.7 %shard_map.182 = (f32[4,16,128]{2,1,0:T(8,128)S(1)}, bf16[3,32,64,128]{3,2,1,0:T(8,128)(2,1)S(1)}) custom-call(f32[4,16,128]{2,1,0:T(8,128)S(1)} %get-tuple-element.62.right, f32[4,16,128]{2,1,0:T(8,128)S(1)} %get-tuple-element.67.own, bf16[3,16,64,128]{3,2,1,0:T(8,128)(2,1)S(1)} %get-tuple-element.65.faces, s32[40,128]{1,0:T(8,128)S(1)} %copy-done.1, ...), custom_call_target="tpu_custom_call" | custom-call | flops 4000000 | bytes 1000000 | tf_op jit(solution)/shard_map/pallas_call | solution.py:560
  34.8 2.2 %collective-permute-done.6.up = f32[4,16,128]{2,1,0:T(8,128)S(1)} collective-permute-done((f32[4,16,128]{2,1,0:T(8,128)S(1)}, f32[4,16,128]{2,1,0:T(8,128)S(1)}, u32[]{:S(2)}, u32[]{:S(2)}) %collective-permute-start.6) | collective-permute-done | bytes 32800 | tf_op jit(solution)/shard_map/ppermute | solution.py:577
  37.1 0.3 shard_map.183.known
  37.4 0.0 collective-permute-done.7.beside
  37.4 0.7 shard_map.184
  38.1 0.1 collective-permute-start.9
  38.2 1.0 %collective-permute-start.8 = (f32[4,16,128]{2,1,0:T(8,128)S(1)}, f32[4,16,128]{2,1,0:T(8,128)S(1)}, u32[]{:S(2)}, u32[]{:S(2)}) collective-permute-start(f32[4,16,128]{2,1,0:T(8,128)S(1)} %get-tuple-element.70.own), channel_id=1, source_target_pairs={{0,64},{64,128},{128,192},{192,0},{1,65},{65,129},{129,193},{193,1... | collective-permute-start | bytes 98312 | tf_op jit(solution)/shard_map/ppermute | solution.py:577
  39.2 1.0 %shard_map.185 = (f32[4,16,128]{2,1,0:T(8,128)S(1)}, bf16[3,16,64,128]{3,2,1,0:T(8,128)(2,1)S(1)}) custom-call(f32[4,16,128]{2,1,0:T(8,128)S(1)} %get-tuple-element.62.right, f32[4,16,128]{2,1,0:T(8,128)S(1)} %get-tuple-element.70.own, bf16[3,16,64,128]{3,2,1,0:T(8,128)(2,1)S(1)} %get-tuple-element.65.faces, s32[40,128]{1,0:T(8,128)S(1)} %copy-done.1, ...), custom_call_target="tpu_custom_call" | custom-call | flops 4000000 | bytes 1000000 | tf_op jit(solution)/shard_map/pallas_call | solution.py:560
  40.2 2.2 %collective-permute-done.8.up = f32[4,16,128]{2,1,0:T(8,128)S(1)} collective-permute-done((f32[4,16,128]{2,1,0:T(8,128)S(1)}, f32[4,16,128]{2,1,0:T(8,128)S(1)}, u32[]{:S(2)}, u32[]{:S(2)}) %collective-permute-start.8) | collective-permute-done | bytes 32800 | tf_op jit(solution)/shard_map/ppermute | solution.py:577
  42.4 0.3 shard_map.186.known
  42.7 0.0 collective-permute-done.9.beside
  42.7 0.7 shard_map.187
  43.4 1.5 %collective-permute-start.11 = (f32[72,128]{1,0:T(8,128)S(1)}, f32[72,128]{1,0:T(8,128)S(1)}, u32[]{:S(2)}, u32[]{:S(2)}) collective-permute-start(f32[72,128]{1,0:T(8,128)S(1)} %get-tuple-element.74), channel_id=1, source_target_pairs={{0,1},{1,0},{2,3},{3,2},{4,5},{5,4},{6,7},{7,6},{8,9},{9,8},{10,11... | collective-permute-start | bytes 110600 | tf_op jit(solution)/shard_map/ppermute | solution.py:587
  44.9 0.0 collective-permute-start.10
  44.9 0.3 shard_map.188.known
  45.2 3.7 %collective-permute-done.10.up = f32[4,16,128]{2,1,0:T(8,128)S(1)} collective-permute-done((f32[4,16,128]{2,1,0:T(8,128)S(1)}, f32[4,16,128]{2,1,0:T(8,128)S(1)}, u32[]{:S(2)}, u32[]{:S(2)}) %collective-permute-start.10) | collective-permute-done | bytes 32800 | tf_op jit(solution)/shard_map/ppermute | solution.py:577
  48.8 0.3 shard_map.189.known
  49.2 0.0 collective-permute-done.11.beside
  49.2 0.7 shard_map.190
  49.8 1.3 %collective-permute-start.13 = (f32[72,128]{1,0:T(8,128)S(1)}, f32[72,128]{1,0:T(8,128)S(1)}, u32[]{:S(2)}, u32[]{:S(2)}) collective-permute-start(f32[72,128]{1,0:T(8,128)S(1)} %get-tuple-element.76), channel_id=1, source_target_pairs={{0,1},{1,0},{2,3},{3,2},{4,5},{5,4},{6,7},{7,6},{8,9},{9,8},{10,11... | collective-permute-start | bytes 110600 | tf_op jit(solution)/shard_map/ppermute | solution.py:587
  51.1 0.3 shard_map.191.known
  51.5 3.7 %collective-permute-done.12.up = f32[4,16,128]{2,1,0:T(8,128)S(1)} collective-permute-done((f32[4,16,128]{2,1,0:T(8,128)S(1)}, f32[4,16,128]{2,1,0:T(8,128)S(1)}, u32[]{:S(2)}, u32[]{:S(2)}) %collective-permute-start.12) | collective-permute-done | bytes 32800 | tf_op jit(solution)/shard_map/ppermute | solution.py:577
  55.2 0.3 shard_map.192.known
  55.5 0.7 shard_map.193
  56.2 0.0 copy-start.4
  56.2 0.0 copy-start.11
  56.2 3.4 %collective-permute-start.14 = (f32[72,128]{1,0:T(8,128)S(1)}, f32[72,128]{1,0:T(8,128)S(1)}, u32[]{:S(2)}, u32[]{:S(2)}) collective-permute-start(f32[72,128]{1,0:T(8,128)S(1)} %get-tuple-element.81), channel_id=1, source_target_pairs={{0,1},{1,2},{2,3},{3,4},{4,5},{5,6},{6,7},{7,8},{8,9},{9,10},{10,1... | collective-permute-start | bytes 110600 | tf_op jit(solution)/shard_map/ppermute | solution.py:577
  59.6 1.5 %shard_map.194 = (f32[4,16,128]{2,1,0:T(8,128)S(1)}, f32[4,32,128]{2,1,0:T(8,128)S(1)}) custom-call(f32[4,32,128]{2,1,0:T(8,128)S(1)} %get-tuple-element.61.r0, f32[4,32,128]{2,1,0:T(8,128)S(1)} %get-tuple-element.55.f0, f32[4,16,128]{2,1,0:T(8,128)S(1)} %get-tuple-element.77.fix, f32[4,16,128]{2,1,0:T(8,128)S(1)} %collective-permute-done.12.up, ...), custom_call_target="tpu_custom_call" | custom-call | flops 5000000 | bytes 1250000 | tf_op jit(solution)/shard_map/pallas_call | solution.py:560
  61.1 0.0 collective-permute-done.14.beside
  61.1 1.0 %shard_map.195 = (f32[4,32,128]{2,1,0:T(8,128)S(1)}, f32[136,128]{1,0:T(8,128)S(1)}) custom-call(f32[4,16,128]{2,1,0:T(8,128)S(1)} %get-tuple-element.79.known, f32[4,32,128]{2,1,0:T(8,128)S(1)} %get-tuple-element.80.base, f32[72,128]{1,0:T(8,128)S(1)} %collective-permute-done.14.beside, f32[80,128]{1,0:T(8,128)S(1)} %collective-permute-done.3.beside.beside_place, ...), custom_call_target="tpu_custom_call" | custom-call | flops 2000000 | bytes 500000 | tf_op jit(solution)/shard_map/pallas_call | solution.py:560
  62.1 5.3 %collective-permute-start.16 = (f32[136,128]{1,0:T(8,128)S(1)}, f32[136,128]{1,0:T(8,128)S(1)}, u32[]{:S(2)}, u32[]{:S(2)}) collective-permute-start(f32[136,128]{1,0:T(8,128)S(1)} %get-tuple-element.86), channel_id=1, source_target_pairs={{0,1},{1,2},{2,3},{3,4},{4,5},{5,6},{6,7},{7,8},{8,9},{9,10},{10,1... | collective-permute-start | bytes 208904 | tf_op jit(solution)/shard_map/ppermute | solution.py:577
  67.4 0.0 collective-permute-start.15
  67.4 1.9 %shard_map.196 = (f32[4,32,128]{2,1,0:T(8,128)S(1)}, f32[4,64,128]{2,1,0:T(8,128)S(1)}) custom-call(f32[4,64,128]{2,1,0:T(8,128)S(1)} %get-tuple-element.53.r0, f32[4,64,128]{2,1,0:T(8,128)S(1)} %copy-done.11, f32[4,32,128]{2,1,0:T(8,128)S(1)} %get-tuple-element.82.fix, bf16[64,64,128]{2,1,0:T(8,128)(2,1)S(1)} %bitcast.34, ...), custom_call_target="tpu_custom_call" | custom-call | flops 8000000 | bytes 2000000 | tf_op jit(solution)/shard_map/pallas_call | solution.py:560
  69.3 2.4 %collective-permute-done.15.up = f32[4,32,128]{2,1,0:T(8,128)S(1)} collective-permute-done((f32[4,32,128]{2,1,0:T(8,128)S(1)}, f32[4,32,128]{2,1,0:T(8,128)S(1)}, u32[]{:S(2)}, u32[]{:S(2)}) %collective-permute-start.15) | collective-permute-done | bytes 65568 | tf_op jit(solution)/shard_map/ppermute | solution.py:577
  71.7 0.7 shard_map.197.known
  72.4 0.0 collective-permute-done.16.beside
  72.4 2.0 %shard_map.198 = f32[4,64,128]{2,1,0:T(8,128)} custom-call(f32[4,32,128]{2,1,0:T(8,128)S(1)} %shard_map.197.known, f32[4,64,128]{2,1,0:T(8,128)S(1)} %get-tuple-element.85.base, f32[136,128]{1,0:T(8,128)S(1)} %collective-permute-done.16.beside, f32[144,128]{1,0:T(8,128)S(1)} %collective-permute-done.1.beside.beside_place, ...), custom_call_target="tpu_custom_call" | custom-call | flops 4000000 | bytes 1000000 | tf_op jit(solution)/shard_map/pallas_call | solution.py:560
  (21 shorter events, 0.0 us)
Async XLA Ops:
  2.9 10.4 %collective-permute-start.1 = (f32[144,128]{1,0:T(8,128)}, f32[144,128]{1,0:T(8,128)S(1)}, u32[]{:S(2)}, u32[]{:S(2)}) collective-permute-start(f32[144,128]{1,0:T(8,128)} %get-tuple-element.51), channel_id=1, source_target_pairs={{0,1},{1,2},{2,3},{3,4},{4,5},{5,6},{6,7},{7,8},{8,9},{9,10},{10,1... | collective-permute-start | bytes 221192 | tf_op jit(solution)/shard_map/ppermute | solution.py:577
  6.0 6.2 %collective-permute-start = (f32[136,128]{1,0:T(8,128)}, f32[136,128]{1,0:T(8,128)S(1)}, u32[]{:S(2)}, u32[]{:S(2)}) collective-permute-start(f32[136,128]{1,0:T(8,128)} %get-tuple-element.49), channel_id=1, source_target_pairs={{0,64},{64,128},{128,192},{192,0},{1,65},{65,129},{129,193},{193,1... | collective-permute-start | bytes 208904 | tf_op jit(solution)/shard_map/ppermute | solution.py:577
  7.2 5.0 %copy-start = (bf16[1,1,3,64,64,128]{5,4,3,2,1,0:T(8,128)(2,1)S(1)}, bf16[1,1,3,64,64,128]{5,4,3,2,1,0:T(8,128)(2,1)}, u32[]{:S(2)}) copy-start(bf16[1,1,3,64,64,128]{5,4,3,2,1,0:T(8,128)(2,1)} %param.21) | copy-start | bytes 9437188
  7.2 5.0 %copy-start.1 = (s32[40,128]{1,0:T(8,128)S(1)}, s32[40,128]{1,0:T(8,128)}, u32[]{:S(2)}) copy-start(s32[40,128]{1,0:T(8,128)} %get-tuple-element.50.table) | copy-start | bytes 61444
  7.2 5.0 %copy-start.10 = (f32[1,1,4,64,128]{4,3,2,1,0:T(8,128)S(1)}, f32[1,1,4,64,128]{4,3,2,1,0:T(8,128)}, u32[]{:S(2)}) copy-start(f32[1,1,4,64,128]{4,3,2,1,0:T(8,128)} %param.18) | copy-start | bytes 393220
  12.2 1.4 %copy-start.2 = (bf16[3,32,64,128]{3,2,1,0:T(8,128)(2,1)S(1)}, bf16[3,32,64,128]{3,2,1,0:T(8,128)(2,1)}, u32[]{:S(2)}) copy-start(bf16[3,32,64,128]{3,2,1,0:T(8,128)(2,1)} %get-tuple-element.52.first) | copy-start | bytes 4718596
  12.3 5.6 %copy-start.8 = (bf16[1,1,2,64,64,32]{4,5,3,2,1,0:T(8,128)(2,1)S(1)}, bf16[1,1,2,64,64,32]{4,5,3,2,1,0:T(8,128)(2,1)}, u32[]{:S(2)}) copy-start(bf16[1,1,2,64,64,32]{4,5,3,2,1,0:T(8,128)(2,1)} %param.32) | copy-start | bytes 1572868
  13.6 4.2 %copy-start.5 = (bf16[1,1,3,64,64,64]{5,4,3,2,1,0:T(8,128)(2,1)S(1)}, bf16[1,1,3,64,64,64]{5,4,3,2,1,0:T(8,128)(2,1)}, u32[]{:S(2)}) copy-start(bf16[1,1,3,64,64,64]{5,4,3,2,1,0:T(8,128)(2,1)} %param.28) | copy-start | bytes 4718596
  13.6 4.2 %copy-start.7 = (bf16[1,1,64,64,64]{4,3,2,1,0:T(8,128)(2,1)S(1)}, bf16[1,1,64,64,64]{4,3,2,1,0:T(8,128)(2,1)}, u32[]{:S(2)}) copy-start(bf16[1,1,64,64,64]{4,3,2,1,0:T(8,128)(2,1)} %param.26) | copy-start | bytes 1572868
  13.6 4.2 %copy-start.9 = (bf16[1,1,64,64,32]{3,4,2,1,0:T(8,128)(2,1)S(1)}, bf16[1,1,64,64,32]{3,4,2,1,0:T(8,128)(2,1)}, u32[]{:S(2)}) copy-start(bf16[1,1,64,64,32]{3,4,2,1,0:T(8,128)(2,1)} %param.33) | copy-start | bytes 786436
  16.2 6.3 %collective-permute-start.3 = (f32[80,128]{1,0:T(8,128)S(1)}, f32[80,128]{1,0:T(8,128)S(1)}, u32[]{:S(2)}, u32[]{:S(2)}) collective-permute-start(f32[80,128]{1,0:T(8,128)S(1)} %get-tuple-element.59), channel_id=1, source_target_pairs={{0,1},{1,2},{2,3},{3,4},{4,5},{5,6},{6,7},{7,8},{8,9},{9,10},{10,1... | collective-permute-start | bytes 122888 | tf_op jit(solution)/shard_map/ppermute | solution.py:577
  16.6 5.2 %collective-permute-start.2 = (f32[72,128]{1,0:T(8,128)S(1)}, f32[72,128]{1,0:T(8,128)S(1)}, u32[]{:S(2)}, u32[]{:S(2)}) collective-permute-start(f32[72,128]{1,0:T(8,128)S(1)} %get-tuple-element.57), channel_id=1, source_target_pairs={{0,64},{64,128},{128,192},{192,0},{1,65},{65,129},{129,193},{193,1... | collective-permute-start | bytes 110600 | tf_op jit(solution)/shard_map/ppermute | solution.py:577
  21.9 3.8 %copy-start.6 = (bf16[1,1,3,64,64,32]{4,5,3,2,1,0:T(8,128)(2,1)S(1)}, bf16[1,1,3,64,64,32]{4,5,3,2,1,0:T(8,128)(2,1)}, u32[]{:S(2)}) copy-start(bf16[1,1,3,64,64,32]{4,5,3,2,1,0:T(8,128)(2,1)} %param.34) | copy-start | bytes 2359300
  24.0 6.0 %collective-permute-start.5 = (f32[72,128]{1,0:T(8,128)S(1)}, f32[72,128]{1,0:T(8,128)S(1)}, u32[]{:S(2)}, u32[]{:S(2)}) collective-permute-start(f32[72,128]{1,0:T(8,128)S(1)} %get-tuple-element.66), channel_id=1, source_target_pairs={{0,1},{1,2},{2,3},{3,4},{4,5},{5,6},{6,7},{7,8},{8,9},{9,10},{10,1... | collective-permute-start | bytes 110600 | tf_op jit(solution)/shard_map/ppermute | solution.py:587
  25.7 4.0 %collective-permute-start.4 = (f32[4,16,128]{2,1,0:T(8,128)S(1)}, f32[4,16,128]{2,1,0:T(8,128)S(1)}, u32[]{:S(2)}, u32[]{:S(2)}) collective-permute-start(f32[4,16,128]{2,1,0:T(8,128)S(1)} %get-tuple-element.63.own), channel_id=1, source_target_pairs={{0,64},{64,128},{128,192},{192,0},{1,65},{65,129},{129,193},{193,1... | collective-permute-start | bytes 98312 | tf_op jit(solution)/shard_map/ppermute | solution.py:577
  25.7 7.4 %copy-start.3 = (bf16[1,1,64,64,128]{4,3,2,1,0:T(8,128)(2,1)S(1)}, bf16[1,1,64,64,128]{4,3,2,1,0:T(8,128)(2,1)}, u32[]{:S(2)}) copy-start(bf16[1,1,64,64,128]{4,3,2,1,0:T(8,128)(2,1)} %param.20) | copy-start | bytes 3145732
  30.6 6.8 %collective-permute-start.7 = (f32[72,128]{1,0:T(8,128)S(1)}, f32[72,128]{1,0:T(8,128)S(1)}, u32[]{:S(2)}, u32[]{:S(2)}) collective-permute-start(f32[72,128]{1,0:T(8,128)S(1)} %get-tuple-element.69), channel_id=1, source_target_pairs={{0,1},{1,2},{2,3},{3,4},{4,5},{5,6},{6,7},{7,8},{8,9},{9,10},{10,1... | collective-permute-start | bytes 110600 | tf_op jit(solution)/shard_map/ppermute | solution.py:587
  33.1 4.0 %collective-permute-start.6 = (f32[4,16,128]{2,1,0:T(8,128)S(1)}, f32[4,16,128]{2,1,0:T(8,128)S(1)}, u32[]{:S(2)}, u32[]{:S(2)}) collective-permute-start(f32[4,16,128]{2,1,0:T(8,128)S(1)} %get-tuple-element.67.own), channel_id=1, source_target_pairs={{0,64},{64,128},{128,192},{192,0},{1,65},{65,129},{129,193},{193,1... | collective-permute-start | bytes 98312 | tf_op jit(solution)/shard_map/ppermute | solution.py:577
  38.1 4.6 %collective-permute-start.9 = (f32[72,128]{1,0:T(8,128)S(1)}, f32[72,128]{1,0:T(8,128)S(1)}, u32[]{:S(2)}, u32[]{:S(2)}) collective-permute-start(f32[72,128]{1,0:T(8,128)S(1)} %get-tuple-element.72), channel_id=1, source_target_pairs={{0,1},{1,0},{2,3},{3,2},{4,5},{5,4},{6,7},{7,6},{8,9},{9,8},{10,11... | collective-permute-start | bytes 110600 | tf_op jit(solution)/shard_map/ppermute | solution.py:587
  38.2 4.2 %collective-permute-start.8 = (f32[4,16,128]{2,1,0:T(8,128)S(1)}, f32[4,16,128]{2,1,0:T(8,128)S(1)}, u32[]{:S(2)}, u32[]{:S(2)}) collective-permute-start(f32[4,16,128]{2,1,0:T(8,128)S(1)} %get-tuple-element.70.own), channel_id=1, source_target_pairs={{0,64},{64,128},{128,192},{192,0},{1,65},{65,129},{129,193},{193,1... | collective-permute-start | bytes 98312 | tf_op jit(solution)/shard_map/ppermute | solution.py:577
  43.4 5.8 %collective-permute-start.11 = (f32[72,128]{1,0:T(8,128)S(1)}, f32[72,128]{1,0:T(8,128)S(1)}, u32[]{:S(2)}, u32[]{:S(2)}) collective-permute-start(f32[72,128]{1,0:T(8,128)S(1)} %get-tuple-element.74), channel_id=1, source_target_pairs={{0,1},{1,0},{2,3},{3,2},{4,5},{5,4},{6,7},{7,6},{8,9},{9,8},{10,11... | collective-permute-start | bytes 110600 | tf_op jit(solution)/shard_map/ppermute | solution.py:587
  44.9 4.0 %collective-permute-start.10 = (f32[4,16,128]{2,1,0:T(8,128)S(1)}, f32[4,16,128]{2,1,0:T(8,128)S(1)}, u32[]{:S(2)}, u32[]{:S(2)}) collective-permute-start(f32[4,16,128]{2,1,0:T(8,128)S(1)} %get-tuple-element.73.own), channel_id=1, source_target_pairs={{0,64},{64,128},{128,192},{192,0},{1,65},{65,129},{129,193},{193,1... | collective-permute-start | bytes 98312 | tf_op jit(solution)/shard_map/ppermute | solution.py:577
  49.8 5.7 %collective-permute-start.13 = (f32[72,128]{1,0:T(8,128)S(1)}, f32[72,128]{1,0:T(8,128)S(1)}, u32[]{:S(2)}, u32[]{:S(2)}) collective-permute-start(f32[72,128]{1,0:T(8,128)S(1)} %get-tuple-element.76), channel_id=1, source_target_pairs={{0,1},{1,0},{2,3},{3,2},{4,5},{5,4},{6,7},{7,6},{8,9},{9,8},{10,11... | collective-permute-start | bytes 110600 | tf_op jit(solution)/shard_map/ppermute | solution.py:587
  51.1 4.0 %collective-permute-start.12 = (f32[4,16,128]{2,1,0:T(8,128)S(1)}, f32[4,16,128]{2,1,0:T(8,128)S(1)}, u32[]{:S(2)}, u32[]{:S(2)}) collective-permute-start(f32[4,16,128]{2,1,0:T(8,128)S(1)} %get-tuple-element.75.own), channel_id=1, source_target_pairs={{0,64},{64,128},{128,192},{192,0},{1,65},{65,129},{129,193},{193,1... | collective-permute-start | bytes 98312 | tf_op jit(solution)/shard_map/ppermute | solution.py:577
  56.2 11.2 %copy-start.4 = (bf16[1,1,64,64,128]{4,3,2,1,0:T(8,128)(2,1)S(1)}, bf16[1,1,64,64,128]{4,3,2,1,0:T(8,128)(2,1)}, u32[]{:S(2)}) copy-start(bf16[1,1,64,64,128]{4,3,2,1,0:T(8,128)(2,1)} %param.19) | copy-start | bytes 3145732
  56.2 11.2 %copy-start.11 = (f32[4,64,128]{2,1,0:T(8,128)S(1)}, f32[4,64,128]{2,1,0:T(8,128)}, u32[]{:S(2)}) copy-start(f32[4,64,128]{2,1,0:T(8,128)} %get-tuple-element.46.f0_hbm.f0) | copy-start | bytes 393220
  56.2 4.9 %collective-permute-start.14 = (f32[72,128]{1,0:T(8,128)S(1)}, f32[72,128]{1,0:T(8,128)S(1)}, u32[]{:S(2)}, u32[]{:S(2)}) collective-permute-start(f32[72,128]{1,0:T(8,128)S(1)} %get-tuple-element.81), channel_id=1, source_target_pairs={{0,1},{1,2},{2,3},{3,4},{4,5},{5,6},{6,7},{7,8},{8,9},{9,10},{10,1... | collective-permute-start | bytes 110600 | tf_op jit(solution)/shard_map/ppermute | solution.py:577
  62.1 10.3 %collective-permute-start.16 = (f32[136,128]{1,0:T(8,128)S(1)}, f32[136,128]{1,0:T(8,128)S(1)}, u32[]{:S(2)}, u32[]{:S(2)}) collective-permute-start(f32[136,128]{1,0:T(8,128)S(1)} %get-tuple-element.86), channel_id=1, source_target_pairs={{0,1},{1,2},{2,3},{3,4},{4,5},{5,6},{6,7},{7,8},{8,9},{9,10},{10,1... | collective-permute-start | bytes 208904 | tf_op jit(solution)/shard_map/ppermute | solution.py:577
  67.4 4.3 %collective-permute-start.15 = (f32[4,32,128]{2,1,0:T(8,128)S(1)}, f32[4,32,128]{2,1,0:T(8,128)S(1)}, u32[]{:S(2)}, u32[]{:S(2)}) collective-permute-start(f32[4,32,128]{2,1,0:T(8,128)S(1)} %get-tuple-element.82.fix), channel_id=1, source_target_pairs={{0,64},{64,128},{128,192},{192,0},{1,65},{65,129},{129,193},{193,1... | collective-permute-start | bytes 196616 | tf_op jit(solution)/shard_map/ppermute | solution.py:577

commit v5 on v4

--- a/solution.py
+++ b/solution.py
@@ -251,7 +251,7 @@
     lax.fori_loop(0, 2, body, 0)
 
 
-M_INVERSE, F_WEIGHT = 0, 1
+M_INVERSE, F_WEIGHT, M_NEXT = 0, 1, 3
 M_DIAG, M_FACE = 0, 1
 C_INVERSE, M_WEIGHT = 0, 1
 
@@ -261,20 +261,20 @@
 
 
 def fine_local_kernel(
-    f0_hbm, linked_hbm, diag_hbm, faces_hbm, m_inverse_hbm, f_weights_hbm, out, first_hbm,
-    f0, linked, diag, face, m_inverse, f_weights, first, semaphores, own,
+    f0_hbm, linked_hbm, diag_hbm, faces_hbm, m_inverse_hbm, f_weights_hbm, m_faces_hbm, out, first_hbm,
+    f0, linked, diag, face, m_inverse, f_weights, m_faces, first, semaphores, own,
 ):
-    sources = [m_inverse_hbm, f_weights_hbm, f0_hbm, linked_hbm, diag_hbm, faces_hbm.at[0]]
-    targets = [m_inverse, f_weights, f0, linked, diag, face]
+    sources = [m_inverse_hbm, f_weights_hbm, m_faces_hbm.at[pl.ds(1, 2)], f0_hbm, linked_hbm, diag_hbm, faces_hbm.at[0]]
+    targets = [m_inverse, f_weights, m_faces, f0, linked, diag, face]
     copies = [pltpu.make_async_copy(x, y, semaphores.at[k]) for k, (x, y) in enumerate(zip(sources, targets))]
     for copy in copies:
         copy.start()
-    for copy in copies[:2]:
+    for copy in copies[:3]:
         copy.wait()
-    pack_halves([m_inverse, f_weights.at[0], f_weights.at[1]], first)
-    packed = pltpu.make_async_copy(first, first_hbm, semaphores.at[6])
+    pack_halves([m_inverse, f_weights.at[0], f_weights.at[1], m_faces.at[0], m_faces.at[1]], first)
+    packed = pltpu.make_async_copy(first, first_hbm, semaphores.at[7])
     packed.start()
-    for copy in copies[2:]:
+    for copy in copies[3:]:
         copy.wait()
     own[...] = -f0[...]
 
@@ -342,7 +342,7 @@
 def middle_local_kernel(
     b, f0, table, m_diag, m_faces, c_inverse, m_weights, out, middle, coarse, own, linked
 ):
-    pack_halves([m_diag, m_faces.at[0], m_faces.at[1], m_faces.at[2]], middle)
+    pack_halves([m_diag, m_faces.at[0]], middle)
     pack_quarters([c_inverse, m_weights.at[0], m_weights.at[1]], coarse)
     expand(-f0[...], lane_index() % 64, own)
     expand(f0[...], row(table, M_LINK), linked)
@@ -353,18 +353,18 @@
     products([middle.at[M_DIAG], middle.at[M_FACE]], [own, linked], 32, emit)
 
 
-def middle_flow_kernel(known, up, middle, table, flow, out, v):
+def middle_flow_kernel(known, up, first, table, flow, out, v):
     index, inside = chosen(up[64:72, :].astype(jnp.int32)[0:1], row(table, M_LINK + 1), 32, 64)
     expand(up[0:64, :].reshape(S, 16, LANES), index, v, inside * gate_of(flow))
 
     def emit(s, rows, tile):
         out[s, rows, :] = known[s, rows, :] + tile
 
-    products([middle.at[M_FACE + 1]], [v], 32, emit)
+    products([first.at[M_NEXT]], [v], 32, emit)
 
 
 def middle_down_kernel(
-    known, beside, middle, coarse, table, flow,
+    known, beside, blocks, coarse, table, flow,
     r0, right, first, longer, v1, v2, wide,
 ):
     index, inside = chosen(beside[64:72, :].astype(jnp.int32)[0:1], row(table, M_LINK + 2), 32, 64)
@@ -373,7 +373,7 @@
     def emit_residual(s, rows, tile):
         r0[s, rows, :] = known[s, rows, :] + tile
 
-    products([middle.at[M_FACE + 2]], [v2], 32, emit_residual)
+    products([blocks.at[M_NEXT + 1]], [v2], 32, emit_residual)
     residual = r0[...]
     expand(residual, row(table, M_PICK), v1)
     expand(residual, row(table, M_PICK + 1), v2)
@@ -404,8 +404,8 @@
     coarse_local_kernel(right, own, faces, table, out, wide)
 
 
-def coarse_middle_kernel(right, own, faces, table, first, middle, out, chosen_middle, wide):
-    sources = [first.at[M_INVERSE], middle.at[M_FACE + 1], middle.at[M_FACE + 2]]
+def coarse_middle_kernel(right, own, faces, table, first, out, chosen_middle, wide):
+    sources = [first.at[M_INVERSE], first.at[M_NEXT], first.at[M_NEXT + 1]]
     select_middle(sources, table, chosen_middle)
     coarse_local_kernel(right, own, faces, table, out, wide)
 
@@ -623,8 +623,8 @@
     f_beside, f_up = from_behind(f_longer, "tile"), from_behind(f_sent, "flow")
     known, first = call(
         fine_local_kernel,
-        (f0, f_linked, f_diag, f_faces, m_inverse, f_weights),
-        (f32(S, B, LANES), bf16(3, 32, B, LANES)),
+        (f0, f_linked, f_diag, f_faces, m_inverse, f_weights, m_faces),
+        (f32(S, B, LANES), bf16(5, 32, B, LANES)),
         (
             WIDE,
             WIDE,
@@ -632,8 +632,9 @@
             pltpu.VMEM((B, B, LANES), jnp.bfloat16),
             pltpu.VMEM(m_inverse.shape, jnp.bfloat16),
             pltpu.VMEM(f_weights.shape, jnp.bfloat16),
-            pltpu.VMEM((3, 32, B, LANES), jnp.bfloat16),
-            pltpu.SemaphoreType.DMA((7,)),
+            pltpu.VMEM((2, B, B, 64), jnp.bfloat16),
+            pltpu.VMEM((5, 32, B, LANES), jnp.bfloat16),
+            pltpu.SemaphoreType.DMA((8,)),
             WIDE,
         ),
         3.0,
@@ -653,14 +654,14 @@
     known, middle, coarse = call(
         middle_local_kernel,
         (right, m_f0, table, m_diag, m_faces, c_inverse, m_weights),
-        (f32(S, 32, LANES), bf16(4, 32, B, LANES), bf16(3, 16, B, LANES)),
+        (f32(S, 32, LANES), bf16(2, 32, B, LANES), bf16(3, 16, B, LANES)),
         (WIDE, WIDE),
         2.0,
     )
-    known = call(middle_flow_kernel, (known, m_up, middle, table), f32(S, 32, LANES), (WIDE,), 0.0, flow)
+    known = call(middle_flow_kernel, (known, m_up, first, table), f32(S, 32, LANES), (WIDE,), 0.0, flow)
     m_r0, right, value, longer = call(
         middle_down_kernel,
-        (known, m_beside, middle, coarse, table),
+        (known, m_beside, first, coarse, table),
         (f32(S, 32, LANES), f32(S, 16, LANES), f32(S, 16, LANES), f32(64 + SPARE, LANES)),
         (WIDE, WIDE, WIDE),
         1.5,
@@ -687,7 +688,7 @@
         elif step == 3:
             known, chosen_middle = call(
                 coarse_middle_kernel,
-                (right, value, faces, table, first, middle),
+                (right, value, faces, table, first),
                 (f32(S, 16, LANES), bf16(3, 16, B, LANES)),
                 (WIDE,),
             )

time: 74.5 us -> 75.9 us (1.019)
  no operation moved by 1% of the time
where the time goes in v5:
time: 75.9 us; the launch traced here: 75.6 us
  Pallas kernels  35.2 us (46%)
  starting transfers between devices  22.9 us (30%)
  waiting for transfers between devices  16.4 us (22%)
    pallas_call x27, Pallas kernels, call(): pl.pallas_call(kernel, out_shape=outs, in_specs=specs, out_specs=jax.tree...  35.2 us
    ppermute x12, waiting for transfers between devices, from_behind(): return lax.ppermute(block, axis, [(i, (i + 1) % size) for i in range(size)])  16.4 us
    ppermute x12, starting transfers between devices, from_behind(): return lax.ppermute(block, axis, [(i, (i + 1) % size) for i in range(size)])  15.7 us
    ppermute x5, starting transfers between devices, iterate_from_behind(): return lax.ppermute(block, ('flow', 'tile'), route)  7.2 us
  transfers between devices with their start and end apart: 17, of which 6 were waited for; matrix products, arithmetic and copies ran while one was open for 0% of the time, Pallas kernels for 29%

profile of v5, /device:TPU:121, one launch (start us, length us, event | category | flops | bytes accessed | tf_op | source)
XLA Modules:
  0.0 75.6 jit_solution(1023143436614214527)
XLA Ops:
  0.0 2.9 %shard_map.172 = (f32[4,64,128]{2,1,0:T(8,128)}, f32[4,64,128]{2,1,0:T(8,128)}, f32[136,128]{1,0:T(8,128)}, f32[144,128]{1,0:T(8,128)}, s32[40,128]{1,0:T(8,128)}) custom-call(f32[4,64,128]{2,1,0:T(8,128)} %bitcast.41, bf16[64,64,128]{2,1,0:T(8,128)(2,1)} %bitcast.33, s32[3,1,128]{2,1,0:T(1,128)} %bitcast.45, s32[1,128]{1,0:T(1,128)} %bitcast.50, ...), custom_call_target="tpu_custom_call" | custom-call | flops 4000000 | bytes 1000000 | tf_op jit(solution)/shard_map/pallas_call | solution.py:560
  2.9 3.1 %collective-permute-start.1 = (f32[144,128]{1,0:T(8,128)}, f32[144,128]{1,0:T(8,128)S(1)}, u32[]{:S(2)}, u32[]{:S(2)}) collective-permute-start(f32[144,128]{1,0:T(8,128)} %get-tuple-element.51), channel_id=1, source_target_pairs={{0,1},{1,2},{2,3},{3,4},{4,5},{5,6},{6,7},{7,8},{8,9},{9,10},{10,1... | collective-permute-start | bytes 221192 | tf_op jit(solution)/shard_map/ppermute | solution.py:577
  6.0 1.2 %collective-permute-start = (f32[136,128]{1,0:T(8,128)}, f32[136,128]{1,0:T(8,128)S(1)}, u32[]{:S(2)}, u32[]{:S(2)}) collective-permute-start(f32[136,128]{1,0:T(8,128)} %get-tuple-element.49), channel_id=1, source_target_pairs={{0,64},{64,128},{128,192},{192,0},{1,65},{65,129},{129,193},{193,1... | collective-permute-start | bytes 208904 | tf_op jit(solution)/shard_map/ppermute | solution.py:577
  7.2 6.2 %shard_map.173 = (f32[4,64,128]{2,1,0:T(8,128)S(1)}, bf16[5,32,64,128]{3,2,1,0:T(8,128)(2,1)}) custom-call(f32[4,64,128]{2,1,0:T(8,128)} %get-tuple-element.46.f0_hbm.f0, f32[4,64,128]{2,1,0:T(8,128)} %get-tuple-element.47.linked_hbm, bf16[64,64,128]{2,1,0:T(8,128)(2,1)} %bitcast.35, bf16[3,64,64,128]{3,2,1,0:T(8,128)(2,1)} %bitcast.26, ...), custom_call_target="tpu_custom_call" | custom-call | flops 12000000 | bytes 3000000 | tf_op jit(solution)/shard_map/pallas_call | solution.py:560
  13.4 0.0 collective-permute-done.up.up_place
  13.4 1.0 %shard_map.174.known = f32[4,64,128]{2,1,0:T(8,128)S(1)} custom-call(f32[4,64,128]{2,1,0:T(8,128)S(1)} %bitcast.42, f32[4,64,128]{2,1,0:T(8,128)S(1)} %get-tuple-element.48.known, f32[136,128]{1,0:T(8,128)S(1)} %collective-permute-done.up.up_place, bf16[3,64,64,128]{3,2,1,0:T(8,128)(2,1)S(1)} %bitcast.27, s32[40,128]{1,0:T(8,128)S(1)} %copy-done.2, ...), custom_call_target="tpu_custom_call" | custom-call | tf_op jit(solution)/shard_map/pallas_call | solution.py:560
  14.5 0.0 collective-permute-done.1.beside.beside_place
  14.5 0.7 copy-done.1
  15.1 2.5 %shard_map.175 = (f32[4,64,128]{2,1,0:T(8,128)S(1)}, f32[4,32,128]{2,1,0:T(8,128)S(1)}, f32[4,32,128]{2,1,0:T(8,128)S(1)}, f32[72,128]{1,0:T(8,128)S(1)}, f32[80,128]{1,0:T(8,128)S(1)}) custom-call(f32[4,64,128]{2,1,0:T(8,128)S(1)} %shard_map.174.known, f32[144,128]{1,0:T(8,128)S(1)} %collective-permute-done.1.beside.beside_place, ...), custom_call_target="tpu_custom_call" | custom-call | flops 10000000 | bytes 2500000 | tf_op jit(solution)/shard_map/pallas_call | solution.py:560
  17.7 0.5 collective-permute-start.3
  18.2 1.2 %collective-permute-start.2 = (f32[72,128]{1,0:T(8,128)S(1)}, f32[72,128]{1,0:T(8,128)S(1)}, u32[]{:S(2)}, u32[]{:S(2)}) collective-permute-start(f32[72,128]{1,0:T(8,128)S(1)} %get-tuple-element.57), channel_id=1, source_target_pairs={{0,64},{64,128},{128,192},{192,0},{1,65},{65,129},{129,193},{193,1... | collective-permute-start | bytes 110600 | tf_op jit(solution)/shard_map/ppermute | solution.py:577
  19.4 3.4 %shard_map.176 = (f32[4,32,128]{2,1,0:T(8,128)S(1)}, bf16[2,32,64,128]{3,2,1,0:T(8,128)(2,1)S(1)}, bf16[3,16,64,128]{3,2,1,0:T(8,128)(2,1)S(1)}) custom-call(f32[4,32,128]{2,1,0:T(8,128)S(1)} %get-tuple-element.54.b, f32[4,32,128]{2,1,0:T(8,128)S(1)} %get-tuple-element.55.f0, s32[40,128]{1,0:T(8,128)S(1)} %copy-done.2, bf16[64,64,64]{2,1,0:T(8,128)(2,1)S(1)} %bitcast.38, ...), custom_call_target="tpu_custom_call" | custom-call | flops 8000000 | bytes 2000000 | tf_op jit(solution)/shard_map/pallas_call | solution.py:560
  22.8 0.0 collective-permute-done.2.up.up_place
  22.8 0.0 copy-start.6
  22.8 0.6 shard_map.177.known
  23.4 0.0 collective-permute-done.3.beside.beside_place
  23.4 1.5 %shard_map.178 = (f32[4,32,128]{2,1,0:T(8,128)S(1)}, f32[4,16,128]{2,1,0:T(8,128)S(1)}, f32[4,16,128]{2,1,0:T(8,128)S(1)}, f32[72,128]{1,0:T(8,128)S(1)}) custom-call(f32[4,32,128]{2,1,0:T(8,128)S(1)} %shard_map.177.known, f32[80,128]{1,0:T(8,128)S(1)} %collective-permute-done.3.beside.beside_place, bf16[5,32,64,128]{3,2,1,0:T(8,128)(2,1)S(1)} %copy-done.1, ...), custom_call_target="tpu_custom_call" | custom-call | flops 6000000 | bytes 1500000 | tf_op jit(solution)/shard_map/pallas_call | solution.py:560
  24.9 0.0 copy-start.4
  25.0 1.9 %collective-permute-start.5 = (f32[72,128]{1,0:T(8,128)S(1)}, f32[72,128]{1,0:T(8,128)S(1)}, u32[]{:S(2)}, u32[]{:S(2)}) collective-permute-start(f32[72,128]{1,0:T(8,128)S(1)} %get-tuple-element.65), channel_id=1, source_target_pairs={{0,1},{1,2},{2,3},{3,4},{4,5},{5,6},{6,7},{7,8},{8,9},{9,10},{10,1... | collective-permute-start | bytes 110600 | tf_op jit(solution)/shard_map/ppermute | solution.py:587
  26.9 0.0 collective-permute-start.4
  26.9 1.7 %shard_map.179 = (f32[4,16,128]{2,1,0:T(8,128)S(1)}, bf16[3,16,64,128]{3,2,1,0:T(8,128)(2,1)S(1)}) custom-call(f32[4,16,128]{2,1,0:T(8,128)S(1)} %get-tuple-element.61.right, f32[4,16,128]{2,1,0:T(8,128)S(1)} %get-tuple-element.62.own, bf16[3,64,32,64]{3,2,1,0:T(8,128)(2,1)S(1)} %bitcast.37, s32[40,128]{1,0:T(8,128)S(1)} %copy-done.2), custom_call_target="tpu_custom_call" | custom-call | flops 4000000 | bytes 1000000 | tf_op jit(solution)/shard_map/pallas_call | solution.py:560
  28.6 2.2 %collective-permute-done.4.up = f32[4,16,128]{2,1,0:T(8,128)S(1)} collective-permute-done((f32[4,16,128]{2,1,0:T(8,128)S(1)}, f32[4,16,128]{2,1,0:T(8,128)S(1)}, u32[]{:S(2)}, u32[]{:S(2)}) %collective-permute-start.4) | collective-permute-done | bytes 32800 | tf_op jit(solution)/shard_map/ppermute | solution.py:577
  30.8 0.3 shard_map.180.known
  31.2 0.0 collective-permute-done.5.beside
  31.2 0.7 shard_map.181
  31.8 2.5 %collective-permute-start.7 = (f32[72,128]{1,0:T(8,128)S(1)}, f32[72,128]{1,0:T(8,128)S(1)}, u32[]{:S(2)}, u32[]{:S(2)}) collective-permute-start(f32[72,128]{1,0:T(8,128)S(1)} %get-tuple-element.68), channel_id=1, source_target_pairs={{0,1},{1,2},{2,3},{3,4},{4,5},{5,6},{6,7},{7,8},{8,9},{9,10},{10,1... | collective-permute-start | bytes 110600 | tf_op jit(solution)/shard_map/ppermute | solution.py:587
  34.3 0.0 collective-permute-start.6
  34.3 1.7 %shard_map.182 = (f32[4,16,128]{2,1,0:T(8,128)S(1)}, bf16[3,32,64,128]{3,2,1,0:T(8,128)(2,1)S(1)}) custom-call(f32[4,16,128]{2,1,0:T(8,128)S(1)} %get-tuple-element.61.right, f32[4,16,128]{2,1,0:T(8,128)S(1)} %get-tuple-element.66.own, bf16[3,16,64,128]{3,2,1,0:T(8,128)(2,1)S(1)} %get-tuple-element.64.faces, s32[40,128]{1,0:T(8,128)S(1)} %copy-done.2, ...), custom_call_target="tpu_custom_call" | custom-call | flops 4000000 | bytes 1000000 | tf_op jit(solution)/shard_map/pallas_call | solution.py:560
  36.0 2.2 %collective-permute-done.6.up = f32[4,16,128]{2,1,0:T(8,128)S(1)} collective-permute-done((f32[4,16,128]{2,1,0:T(8,128)S(1)}, f32[4,16,128]{2,1,0:T(8,128)S(1)}, u32[]{:S(2)}, u32[]{:S(2)}) %collective-permute-start.6) | collective-permute-done | bytes 32800 | tf_op jit(solution)/shard_map/ppermute | solution.py:577
  38.3 0.3 shard_map.183.known
  38.6 0.0 collective-permute-done.7.beside
  38.6 0.7 shard_map.184
  39.3 0.1 collective-permute-start.9
  39.4 1.0 %collective-permute-start.8 = (f32[4,16,128]{2,1,0:T(8,128)S(1)}, f32[4,16,128]{2,1,0:T(8,128)S(1)}, u32[]{:S(2)}, u32[]{:S(2)}) collective-permute-start(f32[4,16,128]{2,1,0:T(8,128)S(1)} %get-tuple-element.69.own), channel_id=1, source_target_pairs={{0,64},{64,128},{128,192},{192,0},{1,65},{65,129},{129,193},{193,1... | collective-permute-start | bytes 98312 | tf_op jit(solution)/shard_map/ppermute | solution.py:577
  40.4 1.0 %shard_map.185 = (f32[4,16,128]{2,1,0:T(8,128)S(1)}, bf16[3,16,64,128]{3,2,1,0:T(8,128)(2,1)S(1)}) custom-call(f32[4,16,128]{2,1,0:T(8,128)S(1)} %get-tuple-element.61.right, f32[4,16,128]{2,1,0:T(8,128)S(1)} %get-tuple-element.69.own, bf16[3,16,64,128]{3,2,1,0:T(8,128)(2,1)S(1)} %get-tuple-element.64.faces, s32[40,128]{1,0:T(8,128)S(1)} %copy-done.2, ...), custom_call_target="tpu_custom_call" | custom-call | flops 4000000 | bytes 1000000 | tf_op jit(solution)/shard_map/pallas_call | solution.py:560
  41.4 2.2 %collective-permute-done.8.up = f32[4,16,128]{2,1,0:T(8,128)S(1)} collective-permute-done((f32[4,16,128]{2,1,0:T(8,128)S(1)}, f32[4,16,128]{2,1,0:T(8,128)S(1)}, u32[]{:S(2)}, u32[]{:S(2)}) %collective-permute-start.8) | collective-permute-done | bytes 32800 | tf_op jit(solution)/shard_map/ppermute | solution.py:577
  43.6 0.3 shard_map.186.known
  43.9 0.0 collective-permute-done.9.beside
  43.9 0.7 shard_map.187
  44.6 1.5 %collective-permute-start.11 = (f32[72,128]{1,0:T(8,128)S(1)}, f32[72,128]{1,0:T(8,128)S(1)}, u32[]{:S(2)}, u32[]{:S(2)}) collective-permute-start(f32[72,128]{1,0:T(8,128)S(1)} %get-tuple-element.73), channel_id=1, source_target_pairs={{0,1},{1,0},{2,3},{3,2},{4,5},{5,4},{6,7},{7,6},{8,9},{9,8},{10,11... | collective-permute-start | bytes 110600 | tf_op jit(solution)/shard_map/ppermute | solution.py:587
  46.0 0.0 collective-permute-start.10
  46.0 0.3 shard_map.188.known
  46.4 3.7 %collective-permute-done.10.up = f32[4,16,128]{2,1,0:T(8,128)S(1)} collective-permute-done((f32[4,16,128]{2,1,0:T(8,128)S(1)}, f32[4,16,128]{2,1,0:T(8,128)S(1)}, u32[]{:S(2)}, u32[]{:S(2)}) %collective-permute-start.10) | collective-permute-done | bytes 32800 | tf_op jit(solution)/shard_map/ppermute | solution.py:577
  50.0 0.3 shard_map.189.known
  50.4 0.0 collective-permute-done.11.beside
  50.4 0.7 shard_map.190
  51.0 1.3 %collective-permute-start.13 = (f32[72,128]{1,0:T(8,128)S(1)}, f32[72,128]{1,0:T(8,128)S(1)}, u32[]{:S(2)}, u32[]{:S(2)}) collective-permute-start(f32[72,128]{1,0:T(8,128)S(1)} %get-tuple-element.75), channel_id=1, source_target_pairs={{0,1},{1,0},{2,3},{3,2},{4,5},{5,4},{6,7},{7,6},{8,9},{9,8},{10,11... | collective-permute-start | bytes 110600 | tf_op jit(solution)/shard_map/ppermute | solution.py:587
  52.3 0.0 collective-permute-start.12
  52.3 0.3 shard_map.191.known
  52.6 0.0 copy-start.5
  52.7 0.0 copy-start.11
  52.7 3.7 %collective-permute-done.12.up = f32[4,16,128]{2,1,0:T(8,128)S(1)} collective-permute-done((f32[4,16,128]{2,1,0:T(8,128)S(1)}, f32[4,16,128]{2,1,0:T(8,128)S(1)}, u32[]{:S(2)}, u32[]{:S(2)}) %collective-permute-start.12) | collective-permute-done | bytes 32800 | tf_op jit(solution)/shard_map/ppermute | solution.py:577
  56.4 0.3 shard_map.192.known
  56.7 0.7 shard_map.193
  57.4 3.4 %collective-permute-start.14 = (f32[72,128]{1,0:T(8,128)S(1)}, f32[72,128]{1,0:T(8,128)S(1)}, u32[]{:S(2)}, u32[]{:S(2)}) collective-permute-start(f32[72,128]{1,0:T(8,128)S(1)} %get-tuple-element.81), channel_id=1, source_target_pairs={{0,1},{1,2},{2,3},{3,4},{4,5},{5,6},{6,7},{7,8},{8,9},{9,10},{10,1... | collective-permute-start | bytes 110600 | tf_op jit(solution)/shard_map/ppermute | solution.py:577
  60.8 1.5 %shard_map.194 = (f32[4,16,128]{2,1,0:T(8,128)S(1)}, f32[4,32,128]{2,1,0:T(8,128)S(1)}) custom-call(f32[4,32,128]{2,1,0:T(8,128)S(1)} %get-tuple-element.60.r0, f32[4,32,128]{2,1,0:T(8,128)S(1)} %get-tuple-element.55.f0, f32[4,16,128]{2,1,0:T(8,128)S(1)} %get-tuple-element.76.fix, f32[4,16,128]{2,1,0:T(8,128)S(1)} %collective-permute-done.12.up, ...), custom_call_target="tpu_custom_call" | custom-call | flops 5000000 | bytes 1250000 | tf_op jit(solution)/shard_map/pallas_call | solution.py:560
  62.3 0.0 collective-permute-done.14.beside
  62.3 1.0 %shard_map.195 = (f32[4,32,128]{2,1,0:T(8,128)S(1)}, f32[136,128]{1,0:T(8,128)S(1)}) custom-call(f32[4,16,128]{2,1,0:T(8,128)S(1)} %get-tuple-element.79.known, f32[4,32,128]{2,1,0:T(8,128)S(1)} %get-tuple-element.80.base, f32[72,128]{1,0:T(8,128)S(1)} %collective-permute-done.14.beside, f32[80,128]{1,0:T(8,128)S(1)} %collective-permute-done.3.beside.beside_place, ...), custom_call_target="tpu_custom_call" | custom-call | flops 2000000 | bytes 500000 | tf_op jit(solution)/shard_map/pallas_call | solution.py:560
  63.3 5.3 %collective-permute-start.16 = (f32[136,128]{1,0:T(8,128)S(1)}, f32[136,128]{1,0:T(8,128)S(1)}, u32[]{:S(2)}, u32[]{:S(2)}) collective-permute-start(f32[136,128]{1,0:T(8,128)S(1)} %get-tuple-element.86), channel_id=1, source_target_pairs={{0,1},{1,2},{2,3},{3,4},{4,5},{5,6},{6,7},{7,8},{8,9},{9,10},{10,1... | collective-permute-start | bytes 208904 | tf_op jit(solution)/shard_map/ppermute | solution.py:577
  68.5 1.9 %shard_map.196 = (f32[4,32,128]{2,1,0:T(8,128)S(1)}, f32[4,64,128]{2,1,0:T(8,128)S(1)}) custom-call(f32[4,64,128]{2,1,0:T(8,128)S(1)} %get-tuple-element.53.r0, f32[4,64,128]{2,1,0:T(8,128)S(1)} %copy-done.11, f32[4,32,128]{2,1,0:T(8,128)S(1)} %get-tuple-element.82.fix, bf16[64,64,128]{2,1,0:T(8,128)(2,1)S(1)} %bitcast.36, ...), custom_call_target="tpu_custom_call" | custom-call | flops 8000000 | bytes 2000000 | tf_op jit(solution)/shard_map/pallas_call | solution.py:560
  70.5 2.4 %collective-permute-done.15.up = f32[4,32,128]{2,1,0:T(8,128)S(1)} collective-permute-done((f32[4,32,128]{2,1,0:T(8,128)S(1)}, f32[4,32,128]{2,1,0:T(8,128)S(1)}, u32[]{:S(2)}, u32[]{:S(2)}) %collective-permute-start.15) | collective-permute-done | bytes 65568 | tf_op jit(solution)/shard_map/ppermute | solution.py:577
  72.9 0.7 shard_map.197.known
  73.5 0.0 collective-permute-done.16.beside
  73.5 2.0 %shard_map.198 = f32[4,64,128]{2,1,0:T(8,128)} custom-call(f32[4,32,128]{2,1,0:T(8,128)S(1)} %shard_map.197.known, f32[4,64,128]{2,1,0:T(8,128)S(1)} %get-tuple-element.85.base, f32[136,128]{1,0:T(8,128)S(1)} %collective-permute-done.16.beside, f32[144,128]{1,0:T(8,128)S(1)} %collective-permute-done.1.beside.beside_place, ...), custom_call_target="tpu_custom_call" | custom-call | flops 4000000 | bytes 1000000 | tf_op jit(solution)/shard_map/pallas_call | solution.py:560
  (21 shorter events, 0.0 us)
Async XLA Ops:
  2.9 11.6 %collective-permute-start.1 = (f32[144,128]{1,0:T(8,128)}, f32[144,128]{1,0:T(8,128)S(1)}, u32[]{:S(2)}, u32[]{:S(2)}) collective-permute-start(f32[144,128]{1,0:T(8,128)} %get-tuple-element.51), channel_id=1, source_target_pairs={{0,1},{1,2},{2,3},{3,4},{4,5},{5,6},{6,7},{7,8},{8,9},{9,10},{10,1... | collective-permute-start | bytes 221192 | tf_op jit(solution)/shard_map/ppermute | solution.py:577
  6.0 7.4 %collective-permute-start = (f32[136,128]{1,0:T(8,128)}, f32[136,128]{1,0:T(8,128)S(1)}, u32[]{:S(2)}, u32[]{:S(2)}) collective-permute-start(f32[136,128]{1,0:T(8,128)} %get-tuple-element.49), channel_id=1, source_target_pairs={{0,64},{64,128},{128,192},{192,0},{1,65},{65,129},{129,193},{193,1... | collective-permute-start | bytes 208904 | tf_op jit(solution)/shard_map/ppermute | solution.py:577
  7.2 6.2 %copy-start = (bf16[1,1,3,64,64,128]{5,4,3,2,1,0:T(8,128)(2,1)S(1)}, bf16[1,1,3,64,64,128]{5,4,3,2,1,0:T(8,128)(2,1)}, u32[]{:S(2)}) copy-start(bf16[1,1,3,64,64,128]{5,4,3,2,1,0:T(8,128)(2,1)} %param.21) | copy-start | bytes 9437188
  7.2 6.2 %copy-start.2 = (s32[40,128]{1,0:T(8,128)S(1)}, s32[40,128]{1,0:T(8,128)}, u32[]{:S(2)}) copy-start(s32[40,128]{1,0:T(8,128)} %get-tuple-element.50.table) | copy-start | bytes 61444
  7.2 6.2 %copy-start.10 = (f32[1,1,4,64,128]{4,3,2,1,0:T(8,128)S(1)}, f32[1,1,4,64,128]{4,3,2,1,0:T(8,128)}, u32[]{:S(2)}) copy-start(f32[1,1,4,64,128]{4,3,2,1,0:T(8,128)} %param.18) | copy-start | bytes 393220
  13.4 1.7 %copy-start.1 = (bf16[5,32,64,128]{3,2,1,0:T(8,128)(2,1)S(1)}, bf16[5,32,64,128]{3,2,1,0:T(8,128)(2,1)}, u32[]{:S(2)}) copy-start(bf16[5,32,64,128]{3,2,1,0:T(8,128)(2,1)} %get-tuple-element.52.first.blocks) | copy-start | bytes 7864324
  15.1 4.2 %copy-start.3 = (bf16[1,1,3,64,64,64]{5,4,3,2,1,0:T(8,128)(2,1)S(1)}, bf16[1,1,3,64,64,64]{5,4,3,2,1,0:T(8,128)(2,1)}, u32[]{:S(2)}) copy-start(bf16[1,1,3,64,64,64]{5,4,3,2,1,0:T(8,128)(2,1)} %param.28) | copy-start | bytes 4718596
  15.1 4.2 %copy-start.7 = (bf16[1,1,64,64,64]{4,3,2,1,0:T(8,128)(2,1)S(1)}, bf16[1,1,64,64,64]{4,3,2,1,0:T(8,128)(2,1)}, u32[]{:S(2)}) copy-start(bf16[1,1,64,64,64]{4,3,2,1,0:T(8,128)(2,1)} %param.26) | copy-start | bytes 1572868
  15.1 4.2 %copy-start.8 = (bf16[1,1,2,64,64,32]{4,5,3,2,1,0:T(8,128)(2,1)S(1)}, bf16[1,1,2,64,64,32]{4,5,3,2,1,0:T(8,128)(2,1)}, u32[]{:S(2)}) copy-start(bf16[1,1,2,64,64,32]{4,5,3,2,1,0:T(8,128)(2,1)} %param.32) | copy-start | bytes 1572868
  15.1 4.2 %copy-start.9 = (bf16[1,1,64,64,32]{3,4,2,1,0:T(8,128)(2,1)S(1)}, bf16[1,1,64,64,32]{3,4,2,1,0:T(8,128)(2,1)}, u32[]{:S(2)}) copy-start(bf16[1,1,64,64,32]{3,4,2,1,0:T(8,128)(2,1)} %param.33) | copy-start | bytes 786436
  17.7 5.7 %collective-permute-start.3 = (f32[80,128]{1,0:T(8,128)S(1)}, f32[80,128]{1,0:T(8,128)S(1)}, u32[]{:S(2)}, u32[]{:S(2)}) collective-permute-start(f32[80,128]{1,0:T(8,128)S(1)} %get-tuple-element.58), channel_id=1, source_target_pairs={{0,1},{1,2},{2,3},{3,4},{4,5},{5,6},{6,7},{7,8},{8,9},{9,10},{10,1... | collective-permute-start | bytes 122888 | tf_op jit(solution)/shard_map/ppermute | solution.py:577
  18.2 4.7 %collective-permute-start.2 = (f32[72,128]{1,0:T(8,128)S(1)}, f32[72,128]{1,0:T(8,128)S(1)}, u32[]{:S(2)}, u32[]{:S(2)}) collective-permute-start(f32[72,128]{1,0:T(8,128)S(1)} %get-tuple-element.57), channel_id=1, source_target_pairs={{0,64},{64,128},{128,192},{192,0},{1,65},{65,129},{129,193},{193,1... | collective-permute-start | bytes 110600 | tf_op jit(solution)/shard_map/ppermute | solution.py:577
  22.8 4.0 %copy-start.6 = (bf16[1,1,3,64,64,32]{4,5,3,2,1,0:T(8,128)(2,1)S(1)}, bf16[1,1,3,64,64,32]{4,5,3,2,1,0:T(8,128)(2,1)}, u32[]{:S(2)}) copy-start(bf16[1,1,3,64,64,32]{4,5,3,2,1,0:T(8,128)(2,1)} %param.34) | copy-start | bytes 2359300
  24.9 9.4 %copy-start.4 = (bf16[1,1,64,64,128]{4,3,2,1,0:T(8,128)(2,1)S(1)}, bf16[1,1,64,64,128]{4,3,2,1,0:T(8,128)(2,1)}, u32[]{:S(2)}) copy-start(bf16[1,1,64,64,128]{4,3,2,1,0:T(8,128)(2,1)} %param.20) | copy-start | bytes 3145732
  25.0 6.2 %collective-permute-start.5 = (f32[72,128]{1,0:T(8,128)S(1)}, f32[72,128]{1,0:T(8,128)S(1)}, u32[]{:S(2)}, u32[]{:S(2)}) collective-permute-start(f32[72,128]{1,0:T(8,128)S(1)} %get-tuple-element.65), channel_id=1, source_target_pairs={{0,1},{1,2},{2,3},{3,4},{4,5},{5,6},{6,7},{7,8},{8,9},{9,10},{10,1... | collective-permute-start | bytes 110600 | tf_op jit(solution)/shard_map/ppermute | solution.py:587
  26.9 4.0 %collective-permute-start.4 = (f32[4,16,128]{2,1,0:T(8,128)S(1)}, f32[4,16,128]{2,1,0:T(8,128)S(1)}, u32[]{:S(2)}, u32[]{:S(2)}) collective-permute-start(f32[4,16,128]{2,1,0:T(8,128)S(1)} %get-tuple-element.62.own), channel_id=1, source_target_pairs={{0,64},{64,128},{128,192},{192,0},{1,65},{65,129},{129,193},{193,1... | collective-permute-start | bytes 98312 | tf_op jit(solution)/shard_map/ppermute | solution.py:577
  31.8 6.8 %collective-permute-start.7 = (f32[72,128]{1,0:T(8,128)S(1)}, f32[72,128]{1,0:T(8,128)S(1)}, u32[]{:S(2)}, u32[]{:S(2)}) collective-permute-start(f32[72,128]{1,0:T(8,128)S(1)} %get-tuple-element.68), channel_id=1, source_target_pairs={{0,1},{1,2},{2,3},{3,4},{4,5},{5,6},{6,7},{7,8},{8,9},{9,10},{10,1... | collective-permute-start | bytes 110600 | tf_op jit(solution)/shard_map/ppermute | solution.py:587
  34.3 4.0 %collective-permute-start.6 = (f32[4,16,128]{2,1,0:T(8,128)S(1)}, f32[4,16,128]{2,1,0:T(8,128)S(1)}, u32[]{:S(2)}, u32[]{:S(2)}) collective-permute-start(f32[4,16,128]{2,1,0:T(8,128)S(1)} %get-tuple-element.66.own), channel_id=1, source_target_pairs={{0,64},{64,128},{128,192},{192,0},{1,65},{65,129},{129,193},{193,1... | collective-permute-start | bytes 98312 | tf_op jit(solution)/shard_map/ppermute | solution.py:577
  39.3 4.6 %collective-permute-start.9 = (f32[72,128]{1,0:T(8,128)S(1)}, f32[72,128]{1,0:T(8,128)S(1)}, u32[]{:S(2)}, u32[]{:S(2)}) collective-permute-start(f32[72,128]{1,0:T(8,128)S(1)} %get-tuple-element.71), channel_id=1, source_target_pairs={{0,1},{1,0},{2,3},{3,2},{4,5},{5,4},{6,7},{7,6},{8,9},{9,8},{10,11... | collective-permute-start | bytes 110600 | tf_op jit(solution)/shard_map/ppermute | solution.py:587
  39.4 4.2 %collective-permute-start.8 = (f32[4,16,128]{2,1,0:T(8,128)S(1)}, f32[4,16,128]{2,1,0:T(8,128)S(1)}, u32[]{:S(2)}, u32[]{:S(2)}) collective-permute-start(f32[4,16,128]{2,1,0:T(8,128)S(1)} %get-tuple-element.69.own), channel_id=1, source_target_pairs={{0,64},{64,128},{128,192},{192,0},{1,65},{65,129},{129,193},{193,1... | collective-permute-start | bytes 98312 | tf_op jit(solution)/shard_map/ppermute | solution.py:577
  44.6 5.8 %collective-permute-start.11 = (f32[72,128]{1,0:T(8,128)S(1)}, f32[72,128]{1,0:T(8,128)S(1)}, u32[]{:S(2)}, u32[]{:S(2)}) collective-permute-start(f32[72,128]{1,0:T(8,128)S(1)} %get-tuple-element.73), channel_id=1, source_target_pairs={{0,1},{1,0},{2,3},{3,2},{4,5},{5,4},{6,7},{7,6},{8,9},{9,8},{10,11... | collective-permute-start | bytes 110600 | tf_op jit(solution)/shard_map/ppermute | solution.py:587
  46.0 4.0 %collective-permute-start.10 = (f32[4,16,128]{2,1,0:T(8,128)S(1)}, f32[4,16,128]{2,1,0:T(8,128)S(1)}, u32[]{:S(2)}, u32[]{:S(2)}) collective-permute-start(f32[4,16,128]{2,1,0:T(8,128)S(1)} %get-tuple-element.72.own), channel_id=1, source_target_pairs={{0,64},{64,128},{128,192},{192,0},{1,65},{65,129},{129,193},{193,1... | collective-permute-start | bytes 98312 | tf_op jit(solution)/shard_map/ppermute | solution.py:577
  51.0 5.7 %collective-permute-start.13 = (f32[72,128]{1,0:T(8,128)S(1)}, f32[72,128]{1,0:T(8,128)S(1)}, u32[]{:S(2)}, u32[]{:S(2)}) collective-permute-start(f32[72,128]{1,0:T(8,128)S(1)} %get-tuple-element.75), channel_id=1, source_target_pairs={{0,1},{1,0},{2,3},{3,2},{4,5},{5,4},{6,7},{7,6},{8,9},{9,8},{10,11... | collective-permute-start | bytes 110600 | tf_op jit(solution)/shard_map/ppermute | solution.py:587
  52.3 4.0 %collective-permute-start.12 = (f32[4,16,128]{2,1,0:T(8,128)S(1)}, f32[4,16,128]{2,1,0:T(8,128)S(1)}, u32[]{:S(2)}, u32[]{:S(2)}) collective-permute-start(f32[4,16,128]{2,1,0:T(8,128)S(1)} %get-tuple-element.74.own), channel_id=1, source_target_pairs={{0,64},{64,128},{128,192},{192,0},{1,65},{65,129},{129,193},{193,1... | collective-permute-start | bytes 98312 | tf_op jit(solution)/shard_map/ppermute | solution.py:577
  52.6 15.9 %copy-start.5 = (bf16[1,1,64,64,128]{4,3,2,1,0:T(8,128)(2,1)S(1)}, bf16[1,1,64,64,128]{4,3,2,1,0:T(8,128)(2,1)}, u32[]{:S(2)}) copy-start(bf16[1,1,64,64,128]{4,3,2,1,0:T(8,128)(2,1)} %param.19) | copy-start | bytes 3145732
  52.7 15.9 %copy-start.11 = (f32[4,64,128]{2,1,0:T(8,128)S(1)}, f32[4,64,128]{2,1,0:T(8,128)}, u32[]{:S(2)}) copy-start(f32[4,64,128]{2,1,0:T(8,128)} %get-tuple-element.46.f0_hbm.f0) | copy-start | bytes 393220
  57.4 4.9 %collective-permute-start.14 = (f32[72,128]{1,0:T(8,128)S(1)}, f32[72,128]{1,0:T(8,128)S(1)}, u32[]{:S(2)}, u32[]{:S(2)}) collective-permute-start(f32[72,128]{1,0:T(8,128)S(1)} %get-tuple-element.81), channel_id=1, source_target_pairs={{0,1},{1,2},{2,3},{3,4},{4,5},{5,6},{6,7},{7,8},{8,9},{9,10},{10,1... | collective-permute-start | bytes 110600 | tf_op jit(solution)/shard_map/ppermute | solution.py:577
  63.3 10.3 %collective-permute-start.16 = (f32[136,128]{1,0:T(8,128)S(1)}, f32[136,128]{1,0:T(8,128)S(1)}, u32[]{:S(2)}, u32[]{:S(2)}) collective-permute-start(f32[136,128]{1,0:T(8,128)S(1)} %get-tuple-element.86), channel_id=1, source_target_pairs={{0,1},{1,2},{2,3},{3,4},{4,5},{5,6},{6,7},{7,8},{8,9},{9,10},{10,1... | collective-permute-start | bytes 208904 | tf_op jit(solution)/shard_map/ppermute | solution.py:577
  68.5 4.3 %collective-permute-start.15 = (f32[4,32,128]{2,1,0:T(8,128)S(1)}, f32[4,32,128]{2,1,0:T(8,128)S(1)}, u32[]{:S(2)}, u32[]{:S(2)}) collective-permute-start(f32[4,32,128]{2,1,0:T(8,128)S(1)} %get-tuple-element.82.fix), channel_id=1, source_target_pairs={{0,64},{64,128},{128,192},{192,0},{1,65},{65,129},{129,193},{193,1... | collective-permute-start | bytes 196616 | tf_op jit(solution)/shard_map/ppermute | solution.py:577
